TPU v7x, 32 devices: a whole 2x2x4 slice. The times are simulated.
32 devices in a mesh: tensor: 4 (over y, core), fsdp: 4 (over z), dp: 2 (over x).
Axes of the slice: x: 2, y: 2, z: 4, core: 2. Of those that a mesh axis runs over, the one named last changes fastest.
Arguments:
- tokens: bfloat16 [256, 8192], P(('tensor', 'dp'), 'fsdp'), may hold values from -6 to 6
- gate_weight: bfloat16 [8192, 28672], P('fsdp', 'tensor'), may hold values from -0.0625 to 0.0625
- up_weight: bfloat16 [8192, 28672], P('fsdp', 'tensor'), may hold values from -0.0625 to 0.0625
- down_weight: bfloat16 [28672, 8192], P('tensor', 'fsdp'), may hold values from -0.03125 to 0.03125
- keep_bits: int32 [256, 512], P(('tensor', 'dp'), 'fsdp'), may hold values from 0 to 65535
Outputs:
- mixed: bfloat16 [256, 8192], P(('tensor', 'dp'), 'fsdp')
Inputs may be any that keep to these rules, and one draw needn't show every extreme that they name: `keep_bits`: bit j of word c of a row is the keep flag of column 16 c + j of that row; every 16-bit pattern can occur.
All inputs are finite; a program needn't handle non-finite values.
Results may differ from a plain program's by a relative error of at most 0.0049.
Values may be sent and summed in bfloat16 or wider, within the bound.
No kernel may reach another device: no remote copies, remote signals or barrier semaphores. Data moves between devices by JAX's collectives and lax.ppermute only.
A program may use at most 192 MiB of HBM per device.

v0:
```python
import jax
import jax.numpy as jnp
from jax import lax
from jax.sharding import PartitionSpec as P


def shards(tokens, gate_weight, up_weight, down_weight, keep_bits):
    gathered = lax.all_gather(tokens, "tensor", axis=0, tiled=True)
    width_dev = down_weight.shape[1]
    units_dev = gate_weight.shape[1]
    gate_part = jnp.dot(gathered, gate_weight, preferred_element_type=jnp.float32)
    up_part = jnp.dot(gathered, up_weight, preferred_element_type=jnp.float32)
    summed = lax.psum_scatter(
        jnp.concatenate([gate_part, up_part], axis=1), "fsdp", scatter_dimension=0, tiled=True
    )
    hidden = (jax.nn.silu(summed[:, :units_dev]) * summed[:, units_dev:]).astype(jnp.bfloat16)
    projected = jnp.dot(
        lax.all_gather(hidden, "fsdp", axis=0, tiled=True),
        down_weight,
        preferred_element_type=jnp.float32,
    )
    mine = lax.psum_scatter(projected, "tensor", scatter_dimension=0, tiled=True)
    shifts = jnp.arange(16, dtype=jnp.int32)
    keep = jnp.right_shift(keep_bits[:, :, None], shifts[None, None, :]) & 1
    keep = keep.reshape(mine.shape[0], width_dev).astype(jnp.float32)
    return (2.0 * keep * mine).astype(jnp.bfloat16)


def solution(mesh):
    return jax.shard_map(
        shards,
        mesh=mesh,
        in_specs=(
            P(("tensor", "dp"), "fsdp"),
            P("fsdp", "tensor"),
            P("fsdp", "tensor"),
            P("tensor", "fsdp"),
            P(("tensor", "dp"), "fsdp"),
        ),
        out_specs=P(("tensor", "dp"), "fsdp"),
        check_vma=False,
    )
```

profile of v0, /device:TPU:0, one launch (start us, length us, event | category | flops | bytes accessed | tf_op | source)
XLA Modules:
  0.0 262.2 jit_solution(10747325293449939366)
XLA Ops:
  6.5 0.0 reduce-scatter.3.cloned.1.call-start
  6.5 8.8 %all_gather.6 = bf16[128,2048]{1,0:T(8,128)(2,1)S(1)} all-gather(bf16[32,2048]{1,0:T(8,128)(2,1)} %param.5), channel_id=1, replica_groups=mesh['tensor'=4,'fsdp'=4,'dp'=2] {'tensor'}, dimensions={0}, use_global_device_ids=true | all-gather | bytes 655360 | tf_op jit(solution)/shard_map/all_gather | solution.py:8
  15.4 11.5 %fusion.1 = f32[128,7168]{1,0:T(8,128)S(1)} fusion(bf16[128,2048]{1,0:T(8,128)(2,1)S(1)} %all_gather.6, bf16[2048,7168]{1,0:T(8,128)(2,1)} %param.6), kind=kOutput, calls=%fused_computation.4 | convolution fusion | flops 3758096384 | bytes 33554432 | tf_op jit(solution)/shard_map/dot_general | solution.py:11
  26.8 11.5 %fusion.2 = f32[128,7168]{1,0:T(8,128)S(1)} fusion(bf16[128,2048]{1,0:T(8,128)(2,1)S(1)} %all_gather.6, bf16[2048,7168]{1,0:T(8,128)(2,1)} %param.7), kind=kOutput, calls=%fused_computation.5 | convolution fusion | flops 3758096384 | bytes 33554432 | tf_op jit(solution)/shard_map/dot_general | solution.py:12
  38.3 3.5 %pad_maximum_fusion = f32[128,14336]{1,0:T(8,128)} fusion(f32[128,7168]{1,0:T(8,128)S(1)} %fusion.2, f32[128,7168]{1,0:T(8,128)S(1)} %fusion.1), kind=kLoop, calls=%fused_computation | loop fusion | flops 1835008 | bytes 14680064 | tf_op jit(solution)/shard_map/concatenate | solution.py:14
  41.8 0.0 reduce-scatter.3.cloned.1.call-update
  41.9 0.0 all-gather.2.cloned.1.call-start
  41.9 128.7 %reduce-scatter.3.cloned.1.call-done = f32[32,14336]{1,0:T(8,128)} async-done(((f32[128,14336]{1,0:T(8,128)}), f32[32,14336]{1,0:T(8,128)}) %reduce-scatter.3.cloned.1.call-update) | async-done | bytes 1835024 | tf_op jit(solution)/shard_map/reduce_scatter | solution.py:13
  170.6 2.5 fusion
  173.1 0.0 all-gather.2.cloned.1.call-update
  173.1 0.0 copy-start
  173.2 0.0 reduce-scatter.5.cloned.1.call-start
  173.2 42.0 %all-gather.2.cloned.1.call-done = bf16[128,7168]{1,0:T(8,128)(2,1)} async-done(((bf16[32,7168]{1,0:T(8,128)(2,1)}), bf16[128,7168]{1,0:T(8,128)(2,1)}) %all-gather.2.cloned.1.call-update) | async-done | bytes 1835024 | tf_op jit(solution)/shard_map/all_gather | solution.py:18
  215.2 14.9 %fusion.3 = f32[128,2048]{1,0:T(8,128)} fusion(bf16[128,7168]{1,0:T(8,128)(2,1)} %all-gather.2.cloned.1.call-done, bf16[7168,2048]{1,0:T(8,128)(2,1)} %param.8), kind=kOutput, calls=%fused_computation.6 | convolution fusion | flops 3758096384 | bytes 32243712 | tf_op jit(solution)/shard_map/dot_general | solution.py:17
  230.1 0.0 reduce-scatter.5.cloned.1.call-update
  230.1 0.0 copy-done
  230.1 0.1 copy.6
  230.2 0.1 shift_right_arithmetic.20
  230.3 0.3 copy.7
  230.6 0.1 shift_right_arithmetic.23
  230.7 23.3 %reduce-scatter.5.cloned.1.call-done = f32[32,2048]{1,0:T(8,128)} async-done(((f32[128,2048]{1,0:T(8,128)}), f32[32,2048]{1,0:T(8,128)}) %reduce-scatter.5.cloned.1.call-update) | async-done | bytes 262160 | tf_op jit(solution)/shard_map/reduce_scatter | solution.py:22
  254.0 1.7 multiply_convert_fusion
  (1 shorter events, 0.0 us)
Async XLA Ops:
  6.5 164.1 %reduce-scatter.3.cloned.1.call-start = ((), (), s32[]{:S(2)}) async-start(), calls=%async_computation.2 | async-start | bytes 9175040 | tf_op jit(solution)/shard_map/reduce_scatter | solution.py:13
  41.9 173.4 %all-gather.2.cloned.1.call-start = ((), (), s32[]{:S(2)}) async-start(), calls=%async_computation.3 | async-start | bytes 2293760 | tf_op jit(solution)/shard_map/all_gather | solution.py:18
  173.1 57.0 %copy-start = (s32[32,128]{1,0:T(8,128)S(1)}, s32[32,128]{1,0:T(8,128)}, u32[]{:S(2)}) copy-start(s32[32,128]{1,0:T(8,128)} %param.9) | copy-start | bytes 49156
  173.2 80.9 %reduce-scatter.5.cloned.1.call-start = ((), (), s32[]{:S(2)}) async-start(), calls=%async_computation.4 | async-start | bytes 1310720 | tf_op jit(solution)/shard_map/reduce_scatter | solution.py:22
Sparse Core Ops, SparseCore 0:
  42.0 128.5 reduce-scatter.2
  173.3 41.9 all-gather.1
  230.2 23.7 reduce-scatter.4
where the time goes:
time: 262 us
  waiting for transfers between devices  194 us (74%)
  matrix products  37.8 us (14%)
  between operations  13.2 us (5%)
  blocking collectives  8.84 us (3%)
  other arithmetic  7.67 us (3%)
    reduce_scatter x1, waiting for transfers between devices, shards(): lax.psum_scatter(jnp.concatenate([gate_part, up_part], axis=1), 'fsdp', s...  129 us
    all_gather x1, waiting for transfers between devices, shards(): lax.all_gather(hidden, 'fsdp', axis=0, tiled=True)  42 us
    reduce_scatter x1, waiting for transfers between devices, shards(): lax.psum_scatter(projected, 'tensor', scatter_dimension=0, tiled=True)  23.3 us
    dot_general x1, matrix products, shards(): jnp.dot(lax.all_gather(hidden, 'fsdp', axis=0, tiled=True), down_weight,...  14.9 us
    dot_general x1, matrix products, shards(): up_part = jnp.dot(gathered, up_weight, preferred_element_type=jnp.float32)  11.5 us
    dot_general x1, matrix products, shards(): jnp.dot(gathered, gate_weight, preferred_element_type=jnp.float32)  11.5 us
    all_gather x1, blocking collectives, shards(): gathered = lax.all_gather(tokens, 'tensor', axis=0, tiled=True)  8.84 us
  transfers between devices with their start and end apart: 3, of which 3 were waited for; matrix products, arithmetic and copies ran while one was open for 0% of the time, Pallas kernels for 0%

commit v1 on v0

v1 whole, which is shorter than its diff:
```python
import jax
import jax.numpy as jnp
from jax import lax
from jax.experimental import pallas as pl
from jax.experimental.pallas import tpu as pltpu
from jax.sharding import PartitionSpec as P

F32, BF16 = jnp.float32, jnp.bfloat16
SHARES = (1, 3, 3, 3, 3, 1)
VMEM_LIMIT = 48 << 20


def swap(size, bit):
    return [(i, i ^ bit) for i in range(size)]


def unit_tile(units, shares):
    tile = units // sum(shares)
    return tile if tile * sum(shares) == units and tile % 128 == 0 else 0


def up_kernel(x, g, u, *rest):
    narrow, wide = rest[-2:]
    a = jnp.dot(x[...], g[...], preferred_element_type=F32)
    b = jnp.dot(x[...], u[...], preferred_element_type=F32)
    narrow[0], narrow[1] = a.astype(BF16), b.astype(BF16)
    wide[0], wide[1] = a, b


def partial_sums(x, gate, up, first, count, tile, after):
    rows, depth = x.shape
    units = count * tile
    weight = pl.BlockSpec((depth, tile), lambda i: (0, first + i))
    out = pl.BlockSpec((2, rows, tile), lambda i: (0, 0, i))
    return pl.pallas_call(
        up_kernel,
        grid=(count,),
        in_specs=[pl.BlockSpec((rows, depth), lambda i: (0, 0)), weight, weight] + [pl.BlockSpec(memory_space=pl.ANY)] * len(after),
        out_specs=[out, out],
        out_shape=[
            jax.ShapeDtypeStruct((2, rows, units), BF16),
            jax.ShapeDtypeStruct((2, rows, units), F32),
        ],
        compiler_params=pltpu.CompilerParams(vmem_limit_bytes=VMEM_LIMIT),
        cost_estimate=pl.CostEstimate(
            flops=4 * rows * depth * units, bytes_accessed=4 * depth * units, transcendentals=0
        ),
        name="gate_up",
    )(x, gate, up, *after)


def down_kernel(inner, own, other, w, base, total):
    h = jnp.where(inner[0] > 0, own[...], other[...])
    part = jnp.dot(h, w[...], preferred_element_type=F32)

    @pl.when(pl.program_id(0) == 0)
    def _():
        total[...] = base[...] + part

    @pl.when(pl.program_id(0) > 0)
    def _():
        total[...] += part


def add_down(inner, own, other, down, base, first, count, tile):
    rows, width = base.shape
    piece = pl.BlockSpec((rows, tile), lambda i, s: (0, i))
    whole = pl.BlockSpec((rows, width), lambda i, s: (0, 0))
    return pl.pallas_call(
        down_kernel,
        grid_spec=pltpu.PrefetchScalarGridSpec(
            num_scalar_prefetch=1,
            grid=(count,),
            in_specs=[piece, piece, pl.BlockSpec((tile, width), lambda i, s: (first + i, 0)), whole],
            out_specs=whole,
        ),
        out_shape=jax.ShapeDtypeStruct((rows, width), F32),
        compiler_params=pltpu.CompilerParams(vmem_limit_bytes=VMEM_LIMIT),
        cost_estimate=pl.CostEstimate(
            flops=2 * rows * width * count * tile,
            bytes_accessed=2 * width * count * tile,
            transcendentals=0,
        ),
        name="down",
    )(inner, own, other, down, base)


def keep_scale(keep_bits, width):
    shifts = jnp.arange(16, dtype=jnp.int32)
    keep = jnp.right_shift(keep_bits[:, :, None], shifts[None, None, :]) & 1
    return 2.0 * keep.reshape(keep_bits.shape[0], width).astype(F32)


def line_of_four(tensor):
    def shards(tokens, gate, up, down, keep_bits):
        rows = tokens.shape[0]
        units, width = down.shape
        tile = unit_tile(units, SHARES)
        inner = ((lax.axis_index("fsdp") + 1) // 2 == 1).astype(jnp.int32).reshape(1)
        scale = keep_scale(keep_bits, width)
        x = tokens
        bits = [1 << b for b in reversed(range((tensor - 1).bit_length()))]
        for bit in bits:
            x = jnp.concatenate([x, lax.ppermute(x, "tensor", swap(tensor, bit))], axis=0)
        total = jnp.zeros((x.shape[0], width), F32)
        count = len(SHARES)
        firsts = [sum(SHARES[:c]) for c in range(count)]
        wide, heard, side, crossed, hidden, given = ([None] * count for _ in range(6))

        def send_out(c):
            after = [side[c - 2][1]] if c >= 2 else []
            narrow, wide[c] = partial_sums(x, gate, up, firsts[c], SHARES[c], tile, after)
            heard[c] = lax.ppermute(narrow, "fsdp", [(0, 1), (3, 2)])

        def cross(c):
            added = wide[c] + heard[c].astype(F32)
            side[c] = (added, added.astype(BF16))
            crossed[c] = lax.ppermute(side[c][1], "fsdp", [(1, 2), (2, 1)])

        def give(c):
            both = side[c][0] + crossed[c].astype(F32)
            hidden[c] = (jax.nn.silu(both[0]) * both[1]).astype(BF16)
            given[c] = lax.ppermute(hidden[c], "fsdp", [(1, 0), (2, 3)])

        for c in range(count + 3):
            if c < count:
                send_out(c)
            if 0 <= c - 1 < count:
                cross(c - 1)
            if 0 <= c - 2 < count:
                give(c - 2)
            if 0 <= c - 3 < count:
                p = c - 3
                total = add_down(inner, hidden[p], given[p], down, total, firsts[p], SHARES[p], tile)
        for step, bit in enumerate(reversed(bits)):
            half = total.shape[0] // 2
            away = total[half:]
            away = away if step == 0 else away.astype(BF16)
            total = total[:half] + lax.ppermute(away, "tensor", swap(tensor, bit)).astype(F32)
        return (scale * total).astype(BF16)

    return shards


def any_line(tokens, gate, up, down, keep_bits):
    units, width = down.shape
    x = lax.all_gather(tokens, "tensor", axis=0, tiled=True)
    both = jnp.concatenate(
        [jnp.dot(x, gate, preferred_element_type=F32), jnp.dot(x, up, preferred_element_type=F32)], axis=1
    )
    both = lax.psum_scatter(both, "fsdp", scatter_dimension=0, tiled=True)
    hidden = (jax.nn.silu(both[:, :units]) * both[:, units:]).astype(BF16)
    hidden = lax.all_gather(hidden, "fsdp", axis=0, tiled=True)
    total = jnp.dot(hidden, down, preferred_element_type=F32)
    total = lax.psum_scatter(total, "tensor", scatter_dimension=0, tiled=True)
    return (keep_scale(keep_bits, width) * total).astype(BF16)


def solution(mesh):
    tensor, fsdp = mesh.shape["tensor"], mesh.shape["fsdp"]

    def shards(tokens, gate, up, down, keep_bits):
        cut = fsdp == 4 and tensor & (tensor - 1) == 0 and unit_tile(down.shape[0], SHARES)
        return (line_of_four(tensor) if cut else any_line)(tokens, gate, up, down, keep_bits)

    return jax.shard_map(
        shards,
        mesh=mesh,
        in_specs=(
            P(("tensor", "dp"), "fsdp"),
            P("fsdp", "tensor"),
            P("fsdp", "tensor"),
            P("tensor", "fsdp"),
            P(("tensor", "dp"), "fsdp"),
        ),
        out_specs=P(("tensor", "dp"), "fsdp"),
        check_vma=False,
    )
```

time: 262 us -> 157 us (0.60)
  waiting for transfers between devices: 194 us -> 39.6 us
  Pallas kernels: 0 us -> 54 us
  starting transfers between devices: 0.09 us -> 48.7 us
  matrix products: 37.8 us -> 0 us
  between operations: 13.2 us -> 0.53 us
  blocking collectives: 8.84 us -> 0 us
  other arithmetic: 7.67 us -> 11 us
    reduce_scatter x2 -> x0, waiting for transfers between devices: 152 us -> none  [the longest x1 129 us: shards(): lax.psum_scatter(jnp.concatenate([gate_part, up_part], axis=1), 'fsdp', s...]
    pallas_call x0 -> x12, Pallas kernels: none -> 54 us  [the longest x6 32.3 us: partial_sums(): pl.pallas_call(up_kernel, grid=(count,), in_specs=[pl.BlockSpec((rows, de...]
    ppermute x0 -> x22, starting transfers between devices: none -> 48.7 us  [the longest x6 29.1 us: send_out(): heard[c] = lax.ppermute(narrow, 'fsdp', [(0, 1), (3, 2)])]
    all_gather x1 -> x0, waiting for transfers between devices: 42 us -> none  [shards(): lax.all_gather(hidden, 'fsdp', axis=0, tiled=True)]
    ppermute x0 -> x22, waiting for transfers between devices: none -> 39.6 us  [the longest x6 20.1 us: give(): given[c] = lax.ppermute(hidden[c], 'fsdp', [(1, 0), (2, 3)])]
    dot_general x3 -> x0, matrix products: 37.8 us -> none  [the longest x1 14.9 us: shards(): jnp.dot(lax.all_gather(hidden, 'fsdp', axis=0, tiled=True), down_weight,...]
    all_gather x1 -> x0, blocking collectives: 8.84 us -> none  [shards(): gathered = lax.all_gather(tokens, 'tensor', axis=0, tiled=True)]
    add x0 -> x7, other arithmetic: none -> 5.19 us  [the longest x6 5.13 us: give(): both = side[c][0] + crossed[c].astype(F32)]
  transfers between devices with their start and end apart: 3 -> 22, of which waited for: 3 -> 10; matrix products, arithmetic and copies ran while one was open for 0% -> 7% of each run, Pallas kernels for 0% -> 31%
where the time goes in v1:
time: 157 us; the launch traced here: 156 us
  Pallas kernels  54 us (34%)
  starting transfers between devices  48.7 us (31%)
  waiting for transfers between devices  39.6 us (25%)
  other arithmetic  11 us (7%)
  local copies, waits for them, and re-layouts  2.58 us (2%)
    pallas_call x6, Pallas kernels, partial_sums(): pl.pallas_call(up_kernel, grid=(count,), in_specs=[pl.BlockSpec((rows, de...  32.3 us
    ppermute x6, starting transfers between devices, send_out(): heard[c] = lax.ppermute(narrow, 'fsdp', [(0, 1), (3, 2)])  29.1 us
    pallas_call x6, Pallas kernels, add_down(): pl.pallas_call(down_kernel, grid_spec=pltpu.PrefetchScalarGridSpec(num_sc...  21.8 us
    ppermute x6, waiting for transfers between devices, give(): given[c] = lax.ppermute(hidden[c], 'fsdp', [(1, 0), (2, 3)])  20.1 us
    ppermute x6, waiting for transfers between devices, send_out(): heard[c] = lax.ppermute(narrow, 'fsdp', [(0, 1), (3, 2)])  9.89 us
    ppermute x6, starting transfers between devices, give(): given[c] = lax.ppermute(hidden[c], 'fsdp', [(1, 0), (2, 3)])  7.93 us
    ppermute x6, starting transfers between devices, cross(): crossed[c] = lax.ppermute(side[c][1], 'fsdp', [(1, 2), (2, 1)])  6.89 us
    ppermute x2, waiting for transfers between devices, shards(): lax.ppermute(away, 'tensor', swap(tensor, bit)).astype(F32)  5.31 us
  transfers between devices with their start and end apart: 22, of which 10 were waited for; matrix products, arithmetic and copies ran while one was open for 7% of the time, Pallas kernels for 31%

profile of v1, /device:TPU:0, one launch (start us, length us, event | category | flops | bytes accessed | tf_op | source)
XLA Modules:
  0.0 156.4 jit_solution(5014830071488351670)
XLA Ops:
  0.0 3.0 %collective-permute-start = (bf16[32,2048]{1,0:T(8,128)(2,1)}, bf16[32,2048]{1,0:T(8,128)(2,1)S(1)}, u32[]{:S(2)}, u32[]{:S(2)}) collective-permute-start(bf16[32,2048]{1,0:T(8,128)(2,1)} %param.5), channel_id=1, source_target_pairs={{0,16},{8,24},{16,0},{24,8},{1,17},{9,25},{17,1},{25,9},{2,18},{10... | collective-permute-start | bytes 393224 | tf_op jit(solution)/shard_map/ppermute | solution.py:104
  3.0 3.7 %collective-permute-done = bf16[32,2048]{1,0:T(8,128)(2,1)S(1)} collective-permute-done((bf16[32,2048]{1,0:T(8,128)(2,1)}, bf16[32,2048]{1,0:T(8,128)(2,1)S(1)}, u32[]{:S(2)}, u32[]{:S(2)}) %collective-permute-start) | collective-permute-done | bytes 131104 | tf_op jit(solution)/shard_map/ppermute | solution.py:104
  9.2 3.0 %gate_up.9 = (bf16[2,128,512]{2,1,0:T(8,128)(2,1)S(1)}, f32[2,128,512]{2,1,0:T(8,128)S(1)}) custom-call(bf16[128,2048]{1,0:T(8,128)(2,1)S(1)} %constant_dynamic-update-slice_fusion.x, bf16[2048,7168]{1,0:T(8,128)(2,1)} %g.11, bf16[2048,7168]{1,0:T(8,128)(2,1)} %u.11), custom_call_target="tpu_custom_call" | custom-call | flops 536870912 | bytes 4194304 | tf_op jit(solution)/shard_map/gate_up/pallas_call | solution.py:35
  12.2 3.7 %collective-permute-start.7 = (bf16[2,128,512]{2,1,0:T(8,128)(2,1)S(1)}, bf16[2,128,512]{2,1,0:T(8,128)(2,1)S(1)}, u32[]{:S(2)}, u32[]{:S(2)}) collective-permute-start(bf16[2,128,512]{2,1,0:T(8,128)(2,1)S(1)} %get-tuple-element.24), channel_id=1, source_target_pairs={{0,2},{6,4},{1,3},{7,5},{8,10},{14,12},{9,11},{15,13},{16,18},{22,... | collective-permute-start | bytes 786440 | tf_op jit(solution)/shard_map/ppermute | solution.py:113
  15.9 6.2 %gate_up.6 = (bf16[2,128,1536]{2,1,0:T(8,128)(2,1)S(1)}, f32[2,128,1536]{2,1,0:T(8,128)S(1)}) custom-call(bf16[128,2048]{1,0:T(8,128)(2,1)S(1)} %constant_dynamic-update-slice_fusion.x, bf16[2048,7168]{1,0:T(8,128)(2,1)} %g.11, bf16[2048,7168]{1,0:T(8,128)(2,1)} %u.11), custom_call_target="tpu_custom_call" | custom-call | flops 1610612736 | bytes 12582912 | tf_op jit(solution)/shard_map/gate_up/pallas_call | solution.py:35
  24.2 7.0 %gate_up.10 = (bf16[2,128,1536]{2,1,0:T(8,128)(2,1)}, f32[2,128,1536]{2,1,0:T(8,128)S(1)}) custom-call(bf16[128,2048]{1,0:T(8,128)(2,1)S(1)} %constant_dynamic-update-slice_fusion.x, bf16[2048,7168]{1,0:T(8,128)(2,1)} %g.11, bf16[2048,7168]{1,0:T(8,128)(2,1)} %u.11, bf16[2,128,512]{2,1,0:T(8,128)(2,1)S(1)} %fusion.13.rest_0_), custom_call_target="tpu_custom_call" | custom-call | flops 1610612736 | bytes 12582912 | tf_op jit(solution)/shard_map/gate_up/pallas_call | solution.py:35
  31.2 6.3 %collective-permute-start.8 = (bf16[2,128,1536]{2,1,0:T(8,128)(2,1)}, bf16[2,128,1536]{2,1,0:T(8,128)(2,1)}, u32[]{:S(2)}, u32[]{:S(2)}) collective-permute-start(bf16[2,128,1536]{2,1,0:T(8,128)(2,1)} %get-tuple-element.26), channel_id=1, source_target_pairs={{0,2},{6,4},{1,3},{7,5},{8,10},{14,12},{9,11},{15,13},{16,18},{22,... | collective-permute-start | bytes 2359304 | tf_op jit(solution)/shard_map/ppermute | solution.py:113
  39.1 2.2 %collective-permute-done.2 = bf16[2,128,1536]{2,1,0:T(8,128)(2,1)S(1)} collective-permute-done((bf16[2,128,1536]{2,1,0:T(8,128)(2,1)S(1)}, bf16[2,128,1536]{2,1,0:T(8,128)(2,1)S(1)}, u32[]{:S(2)}, u32[]{:S(2)}) %collective-permute-start.2) | collective-permute-done | bytes 786464 | tf_op jit(solution)/shard_map/ppermute | solution.py:113
  42.4 7.0 %gate_up.7 = (bf16[2,128,1536]{2,1,0:T(8,128)(2,1)}, f32[2,128,1536]{2,1,0:T(8,128)S(1)}) custom-call(bf16[128,2048]{1,0:T(8,128)(2,1)S(1)} %constant_dynamic-update-slice_fusion.x, bf16[2048,7168]{1,0:T(8,128)(2,1)} %g.11, bf16[2048,7168]{1,0:T(8,128)(2,1)} %u.11, bf16[2,128,1536]{2,1,0:T(8,128)(2,1)S(1)} %fusion.rest_0_), custom_call_target="tpu_custom_call" | custom-call | flops 1610612736 | bytes 12582912 | tf_op jit(solution)/shard_map/gate_up/pallas_call | solution.py:35
  49.4 5.3 %collective-permute-start.3 = (bf16[2,128,1536]{2,1,0:T(8,128)(2,1)}, bf16[2,128,1536]{2,1,0:T(8,128)(2,1)}, u32[]{:S(2)}, u32[]{:S(2)}) collective-permute-start(bf16[2,128,1536]{2,1,0:T(8,128)(2,1)} %get-tuple-element.20), channel_id=1, source_target_pairs={{0,2},{6,4},{1,3},{7,5},{8,10},{14,12},{9,11},{15,13},{16,18},{22,... | collective-permute-start | bytes 2359304 | tf_op jit(solution)/shard_map/ppermute | solution.py:113
  54.8 2.2 %down.6.base = f32[128,2048]{1,0:T(8,128)S(1)} custom-call(s32[1]{0:T(128)} %bitcast.1.inner, bf16[128,512]{1,0:T(8,128)(2,1)S(1)} %fusion.17.own, bf16[128,512]{1,0:T(8,128)(2,1)S(1)} %collective-permute-done.19.other, bf16[7168,2048]{1,0:T(8,128)(2,1)} %w.11, f32[128,2048]{1,0:T(8,128)S(1)} %broadcast_in_dim.2.base), custom_call_target="tpu_custom_call" | custom-call | flops 268435456 | bytes 2097152 | tf_op jit(solution)/shard_map/down/pallas_call | solution.py:69
  57.0 1.6 %collective-permute-start.16 = (bf16[2,128,1536]{2,1,0:T(8,128)(2,1)S(1)}, bf16[2,128,1536]{2,1,0:T(8,128)(2,1)}, u32[]{:S(2)}, u32[]{:S(2)}) collective-permute-start(bf16[2,128,1536]{2,1,0:T(8,128)(2,1)S(1)} %fusion.rest_0_), channel_id=1, source_target_pairs={{2,4},{4,2},{3,5},{5,3},{10,12},{12,10},{11,13},{13,11},{18,20},{2... | collective-permute-start | bytes 2359304 | tf_op jit(solution)/shard_map/ppermute | solution.py:118
  59.9 1.5 collective-permute-start.14
  61.4 6.2 %gate_up.11 = (bf16[2,128,1536]{2,1,0:T(8,128)(2,1)S(1)}, f32[2,128,1536]{2,1,0:T(8,128)S(1)}) custom-call(bf16[128,2048]{1,0:T(8,128)(2,1)S(1)} %constant_dynamic-update-slice_fusion.x, bf16[2048,7168]{1,0:T(8,128)(2,1)} %g.11, bf16[2048,7168]{1,0:T(8,128)(2,1)} %u.11, bf16[2,128,1536]{2,1,0:T(8,128)(2,1)S(1)} %fusion.2.rest_0_), custom_call_target="tpu_custom_call" | custom-call | flops 1610612736 | bytes 12582912 | tf_op jit(solution)/shard_map/gate_up/pallas_call | solution.py:35
  67.6 6.1 %collective-permute-start.9 = (bf16[2,128,1536]{2,1,0:T(8,128)(2,1)S(1)}, bf16[2,128,1536]{2,1,0:T(8,128)(2,1)S(1)}, u32[]{:S(2)}, u32[]{:S(2)}) collective-permute-start(bf16[2,128,1536]{2,1,0:T(8,128)(2,1)S(1)} %get-tuple-element.28), channel_id=1, source_target_pairs={{0,2},{6,4},{1,3},{7,5},{8,10},{14,12},{9,11},{15,13},{16,18},{22,... | collective-permute-start | bytes 2359304 | tf_op jit(solution)/shard_map/ppermute | solution.py:113
  76.4 1.7 %collective-permute-start.12 = (bf16[2,128,1536]{2,1,0:T(8,128)(2,1)S(1)}, bf16[2,128,1536]{2,1,0:T(8,128)(2,1)}, u32[]{:S(2)}, u32[]{:S(2)}) collective-permute-start(bf16[2,128,1536]{2,1,0:T(8,128)(2,1)S(1)} %fusion.1.rest_0_), channel_id=1, source_target_pairs={{2,4},{4,2},{3,5},{5,3},{10,12},{12,10},{11,13},{13,11},{18,20},{2... | collective-permute-start | bytes 2359304 | tf_op jit(solution)/shard_map/ppermute | solution.py:118
  78.1 2.9 %gate_up.8 = (bf16[2,128,512]{2,1,0:T(8,128)(2,1)S(1)}, f32[2,128,512]{2,1,0:T(8,128)S(1)}) custom-call(bf16[128,2048]{1,0:T(8,128)(2,1)S(1)} %constant_dynamic-update-slice_fusion.x, bf16[2048,7168]{1,0:T(8,128)(2,1)} %g.11, bf16[2048,7168]{1,0:T(8,128)(2,1)} %u.11, bf16[2,128,1536]{2,1,0:T(8,128)(2,1)S(1)} %fusion.1.rest_0_), custom_call_target="tpu_custom_call" | custom-call | flops 536870912 | bytes 4194304 | tf_op jit(solution)/shard_map/gate_up/pallas_call | solution.py:35
  81.1 6.3 %collective-permute-start.4 = (bf16[2,128,512]{2,1,0:T(8,128)(2,1)S(1)}, bf16[2,128,512]{2,1,0:T(8,128)(2,1)S(1)}, u32[]{:S(2)}, u32[]{:S(2)}) collective-permute-start(bf16[2,128,512]{2,1,0:T(8,128)(2,1)S(1)} %get-tuple-element.22), channel_id=1, source_target_pairs={{0,2},{6,4},{1,3},{7,5},{8,10},{14,12},{9,11},{15,13},{16,18},{22,... | collective-permute-start | bytes 786440 | tf_op jit(solution)/shard_map/ppermute | solution.py:113
  90.4 6.3 %collective-permute-done.4 = bf16[2,128,512]{2,1,0:T(8,128)(2,1)S(1)} collective-permute-done((bf16[2,128,512]{2,1,0:T(8,128)(2,1)S(1)}, bf16[2,128,512]{2,1,0:T(8,128)(2,1)S(1)}, u32[]{:S(2)}, u32[]{:S(2)}) %collective-permute-start.4) | collective-permute-done | bytes 262176 | tf_op jit(solution)/shard_map/ppermute | solution.py:113
  97.4 1.6 %convert_add_fusion.1 = f32[2,128,1536]{2,1,0:T(8,128)S(1)} fusion(bf16[2,128,1536]{2,1,0:T(8,128)(2,1)} %collective-permute-done.14, f32[2,128,1536]{2,1,0:T(8,128)S(1)} %copy-done.1, bf16[2,128,1536]{2,1,0:T(8,128)(2,1)} %collective-permute-done.8), kind=kLoop, calls=%fused_computation.1 | loop fusion | flops 1572864 | bytes 4718592 | tf_op jit(solution)/shard_map/add | solution.py:121
  101.5 4.4 %down.7.base = f32[128,2048]{1,0:T(8,128)S(1)} custom-call(s32[1]{0:T(128)} %bitcast.1.inner, bf16[128,1536]{1,0:T(8,128)(2,1)S(1)} %fusion.5.own, bf16[128,1536]{1,0:T(8,128)(2,1)S(1)} %collective-permute-done.17.other, bf16[7168,2048]{1,0:T(8,128)(2,1)} %w.11, f32[128,2048]{1,0:T(8,128)S(1)} %down.6.base), custom_call_target="tpu_custom_call" | custom-call | flops 805306368 | bytes 6291456 | tf_op jit(solution)/shard_map/down/pallas_call | solution.py:69
  106.0 1.6 %convert_add_fusion.2 = f32[2,128,1536]{2,1,0:T(8,128)S(1)} fusion(bf16[2,128,1536]{2,1,0:T(8,128)(2,1)} %collective-permute-done.12, f32[2,128,1536]{2,1,0:T(8,128)S(1)} %get-tuple-element.19, bf16[2,128,1536]{2,1,0:T(8,128)(2,1)} %collective-permute-done.3), kind=kLoop, calls=%fused_computation.2 | loop fusion | flops 1572864 | bytes 4718592 | tf_op jit(solution)/shard_map/add | solution.py:121
  112.6 1.6 %collective-permute-done.15.other = bf16[128,1536]{1,0:T(8,128)(2,1)S(1)} collective-permute-done((bf16[128,1536]{1,0:T(8,128)(2,1)S(1)}, bf16[128,1536]{1,0:T(8,128)(2,1)S(1)}, u32[]{:S(2)}, u32[]{:S(2)}) %collective-permute-start.15) | collective-permute-done | bytes 393248 | tf_op jit(solution)/shard_map/ppermute | solution.py:123
  114.3 4.4 %down.8.base = f32[128,2048]{1,0:T(8,128)S(1)} custom-call(s32[1]{0:T(128)} %bitcast.1.inner, bf16[128,1536]{1,0:T(8,128)(2,1)S(1)} %fusion.7.own, bf16[128,1536]{1,0:T(8,128)(2,1)S(1)} %collective-permute-done.15.other, bf16[7168,2048]{1,0:T(8,128)(2,1)} %w.11, f32[128,2048]{1,0:T(8,128)S(1)} %down.7.base), custom_call_target="tpu_custom_call" | custom-call | flops 805306368 | bytes 6291456 | tf_op jit(solution)/shard_map/down/pallas_call | solution.py:69
  118.7 5.5 %collective-permute-done.13.other = bf16[128,1536]{1,0:T(8,128)(2,1)S(1)} collective-permute-done((bf16[128,1536]{1,0:T(8,128)(2,1)S(1)}, bf16[128,1536]{1,0:T(8,128)(2,1)S(1)}, u32[]{:S(2)}, u32[]{:S(2)}) %collective-permute-start.13) | collective-permute-done | bytes 393248 | tf_op jit(solution)/shard_map/ppermute | solution.py:123
  124.2 4.4 %down.9.base = f32[128,2048]{1,0:T(8,128)S(1)} custom-call(s32[1]{0:T(128)} %bitcast.1.inner, bf16[128,1536]{1,0:T(8,128)(2,1)S(1)} %fusion.9.own, bf16[128,1536]{1,0:T(8,128)(2,1)S(1)} %collective-permute-done.13.other, bf16[7168,2048]{1,0:T(8,128)(2,1)} %w.11, f32[128,2048]{1,0:T(8,128)S(1)} %down.8.base), custom_call_target="tpu_custom_call" | custom-call | flops 805306368 | bytes 6291456 | tf_op jit(solution)/shard_map/down/pallas_call | solution.py:69
  128.6 12.9 %collective-permute-done.11.other = bf16[128,1536]{1,0:T(8,128)(2,1)S(1)} collective-permute-done((bf16[128,1536]{1,0:T(8,128)(2,1)S(1)}, bf16[128,1536]{1,0:T(8,128)(2,1)S(1)}, u32[]{:S(2)}, u32[]{:S(2)}) %collective-permute-start.11) | collective-permute-done | bytes 393248 | tf_op jit(solution)/shard_map/ppermute | solution.py:123
  141.5 4.4 %down.10.base = f32[128,2048]{1,0:T(8,128)S(1)} custom-call(s32[1]{0:T(128)} %bitcast.1.inner, bf16[128,1536]{1,0:T(8,128)(2,1)S(1)} %fusion.11.own, bf16[128,1536]{1,0:T(8,128)(2,1)S(1)} %collective-permute-done.11.other, bf16[7168,2048]{1,0:T(8,128)(2,1)} %w.11, f32[128,2048]{1,0:T(8,128)S(1)} %down.9.base), custom_call_target="tpu_custom_call" | custom-call | flops 805306368 | bytes 6291456 | tf_op jit(solution)/shard_map/down/pallas_call | solution.py:69
  145.9 2.0 %down.11 = f32[128,2048]{1,0:T(8,128)S(1)} custom-call(s32[1]{0:T(128)} %bitcast.1.inner, bf16[128,512]{1,0:T(8,128)(2,1)S(1)} %fusion.19.own, bf16[128,512]{1,0:T(8,128)(2,1)S(1)} %collective-permute-done.6.other, bf16[7168,2048]{1,0:T(8,128)(2,1)} %w.11, f32[128,2048]{1,0:T(8,128)S(1)} %down.10.base), custom_call_target="tpu_custom_call" | custom-call | flops 268435456 | bytes 2097152 | tf_op jit(solution)/shard_map/down/pallas_call | solution.py:69
  148.1 1.9 %collective-permute-done.20 = f32[64,2048]{1,0:T(8,128)S(1)} collective-permute-done((f32[64,2048]{1,0:T(8,128)S(1)}, f32[64,2048]{1,0:T(8,128)S(1)}, u32[]{:S(2)}, u32[]{:S(2)}) %collective-permute-start.20) | collective-permute-done | bytes 524320 | tf_op jit(solution)/shard_map/ppermute | solution.py:139
  150.1 1.6 %collective-permute-start.21 = (bf16[32,2048]{1,0:T(8,128)(2,1)S(1)}, bf16[32,2048]{1,0:T(8,128)(2,1)S(1)}, u32[]{:S(2)}, u32[]{:S(2)}) collective-permute-start(bf16[32,2048]{1,0:T(8,128)(2,1)S(1)} %slice.136), channel_id=1, source_target_pairs={{0,16},{8,24},{16,0},{24,8},{1,17},{9,25},{17,1},{25,9},{2,18},{10... | collective-permute-start | bytes 393224 | tf_op jit(solution)/shard_map/ppermute | solution.py:139
  152.3 3.4 %collective-permute-done.21 = bf16[32,2048]{1,0:T(8,128)(2,1)S(1)} collective-permute-done((bf16[32,2048]{1,0:T(8,128)(2,1)S(1)}, bf16[32,2048]{1,0:T(8,128)(2,1)S(1)}, u32[]{:S(2)}, u32[]{:S(2)}) %collective-permute-start.21) | collective-permute-done | bytes 131104 | tf_op jit(solution)/shard_map/ppermute | solution.py:139
  (70 shorter events, 23.8 us)
Async XLA Ops:
  0.0 6.7 %collective-permute-start = (bf16[32,2048]{1,0:T(8,128)(2,1)}, bf16[32,2048]{1,0:T(8,128)(2,1)S(1)}, u32[]{:S(2)}, u32[]{:S(2)}) collective-permute-start(bf16[32,2048]{1,0:T(8,128)(2,1)} %param.5), channel_id=1, source_target_pairs={{0,16},{8,24},{16,0},{24,8},{1,17},{9,25},{17,1},{25,9},{2,18},{10... | collective-permute-start | bytes 393224 | tf_op jit(solution)/shard_map/ppermute | solution.py:104
  7.6 1.6 %collective-permute-start.1 = (bf16[64,2048]{1,0:T(8,128)(2,1)S(1)}, bf16[64,2048]{1,0:T(8,128)(2,1)S(1)}, u32[]{:S(2)}, u32[]{:S(2)}) collective-permute-start(bf16[64,2048]{1,0:T(8,128)(2,1)S(1)} %pad_maximum_fusion), channel_id=1, source_target_pairs={{0,8},{8,0},{16,24},{24,16},{1,9},{9,1},{17,25},{25,17},{2,10},{10... | collective-permute-start | bytes 786440 | tf_op jit(solution)/shard_map/ppermute | solution.py:104
  12.2 11.3 %collective-permute-start.7 = (bf16[2,128,512]{2,1,0:T(8,128)(2,1)S(1)}, bf16[2,128,512]{2,1,0:T(8,128)(2,1)S(1)}, u32[]{:S(2)}, u32[]{:S(2)}) collective-permute-start(bf16[2,128,512]{2,1,0:T(8,128)(2,1)S(1)} %get-tuple-element.24), channel_id=1, source_target_pairs={{0,2},{6,4},{1,3},{7,5},{8,10},{14,12},{9,11},{15,13},{16,18},{22,... | collective-permute-start | bytes 786440 | tf_op jit(solution)/shard_map/ppermute | solution.py:113
  22.1 19.2 %copy-start.2 = (f32[2,128,1536]{2,1,0:T(8,128)}, f32[2,128,1536]{2,1,0:T(8,128)S(1)}, u32[]{:S(2)}) copy-start(f32[2,128,1536]{2,1,0:T(8,128)S(1)} %get-tuple-element.17) | copy-start | bytes 4718596
  22.1 19.2 %collective-permute-start.2 = (bf16[2,128,1536]{2,1,0:T(8,128)(2,1)S(1)}, bf16[2,128,1536]{2,1,0:T(8,128)(2,1)S(1)}, u32[]{:S(2)}, u32[]{:S(2)}) collective-permute-start(bf16[2,128,1536]{2,1,0:T(8,128)(2,1)S(1)} %get-tuple-element.18), channel_id=1, source_target_pairs={{0,2},{6,4},{1,3},{7,5},{8,10},{14,12},{9,11},{15,13},{16,18},{22,... | collective-permute-start | bytes 2359304 | tf_op jit(solution)/shard_map/ppermute | solution.py:113
  23.5 14.0 %collective-permute-start.18 = (bf16[2,128,512]{2,1,0:T(8,128)(2,1)S(1)}, bf16[2,128,512]{2,1,0:T(8,128)(2,1)S(1)}, u32[]{:S(2)}, u32[]{:S(2)}) collective-permute-start(bf16[2,128,512]{2,1,0:T(8,128)(2,1)S(1)} %fusion.13.rest_0_), channel_id=1, source_target_pairs={{2,4},{4,2},{3,5},{5,3},{10,12},{12,10},{11,13},{13,11},{18,20},{2... | collective-permute-start | bytes 786440 | tf_op jit(solution)/shard_map/ppermute | solution.py:118
  31.2 10.1 %copy-start = (f32[2,128,1536]{2,1,0:T(8,128)}, f32[2,128,1536]{2,1,0:T(8,128)S(1)}, u32[]{:S(2)}) copy-start(f32[2,128,1536]{2,1,0:T(8,128)S(1)} %get-tuple-element.25) | copy-start | bytes 4718596
  31.2 27.3 %collective-permute-start.8 = (bf16[2,128,1536]{2,1,0:T(8,128)(2,1)}, bf16[2,128,1536]{2,1,0:T(8,128)(2,1)}, u32[]{:S(2)}, u32[]{:S(2)}) collective-permute-start(bf16[2,128,1536]{2,1,0:T(8,128)(2,1)} %get-tuple-element.26), channel_id=1, source_target_pairs={{0,2},{6,4},{1,3},{7,5},{8,10},{14,12},{9,11},{15,13},{16,18},{22,... | collective-permute-start | bytes 2359304 | tf_op jit(solution)/shard_map/ppermute | solution.py:113
  37.8 16.9 %collective-permute-start.19 = (bf16[128,512]{1,0:T(8,128)(2,1)S(1)}, bf16[128,512]{1,0:T(8,128)(2,1)S(1)}, u32[]{:S(2)}, u32[]{:S(2)}) collective-permute-start(bf16[128,512]{1,0:T(8,128)(2,1)S(1)} %fusion.17.own), channel_id=1, source_target_pairs={{2,0},{4,6},{3,1},{5,7},{10,8},{12,14},{11,9},{13,15},{18,16},{20,... | collective-permute-start | bytes 393224 | tf_op jit(solution)/shard_map/ppermute | solution.py:123
  41.3 0.9 copy-start.4
  49.4 25.7 %collective-permute-start.3 = (bf16[2,128,1536]{2,1,0:T(8,128)(2,1)}, bf16[2,128,1536]{2,1,0:T(8,128)(2,1)}, u32[]{:S(2)}, u32[]{:S(2)}) collective-permute-start(bf16[2,128,1536]{2,1,0:T(8,128)(2,1)} %get-tuple-element.20), channel_id=1, source_target_pairs={{0,2},{6,4},{1,3},{7,5},{8,10},{14,12},{9,11},{15,13},{16,18},{22,... | collective-permute-start | bytes 2359304 | tf_op jit(solution)/shard_map/ppermute | solution.py:113
  54.8 3.8 %copy-start.1 = (f32[2,128,1536]{2,1,0:T(8,128)S(1)}, f32[2,128,1536]{2,1,0:T(8,128)}, u32[]{:S(2)}) copy-start(f32[2,128,1536]{2,1,0:T(8,128)} %copy-done) | copy-start | bytes 4718596
  57.0 30.5 %collective-permute-start.16 = (bf16[2,128,1536]{2,1,0:T(8,128)(2,1)S(1)}, bf16[2,128,1536]{2,1,0:T(8,128)(2,1)}, u32[]{:S(2)}, u32[]{:S(2)}) collective-permute-start(bf16[2,128,1536]{2,1,0:T(8,128)(2,1)S(1)} %fusion.rest_0_), channel_id=1, source_target_pairs={{2,4},{4,2},{3,5},{5,3},{10,12},{12,10},{11,13},{13,11},{18,20},{2... | collective-permute-start | bytes 2359304 | tf_op jit(solution)/shard_map/ppermute | solution.py:118
  59.9 37.6 %collective-permute-start.14 = (bf16[2,128,1536]{2,1,0:T(8,128)(2,1)S(1)}, bf16[2,128,1536]{2,1,0:T(8,128)(2,1)}, u32[]{:S(2)}, u32[]{:S(2)}) collective-permute-start(bf16[2,128,1536]{2,1,0:T(8,128)(2,1)S(1)} %fusion.2.rest_0_), channel_id=1, source_target_pairs={{2,4},{4,2},{3,5},{5,3},{10,12},{12,10},{11,13},{13,11},{18,20},{2... | collective-permute-start | bytes 2359304 | tf_op jit(solution)/shard_map/ppermute | solution.py:118
  67.6 33.0 %collective-permute-start.9 = (bf16[2,128,1536]{2,1,0:T(8,128)(2,1)S(1)}, bf16[2,128,1536]{2,1,0:T(8,128)(2,1)S(1)}, u32[]{:S(2)}, u32[]{:S(2)}) collective-permute-start(bf16[2,128,1536]{2,1,0:T(8,128)(2,1)S(1)} %get-tuple-element.28), channel_id=1, source_target_pairs={{0,2},{6,4},{1,3},{7,5},{8,10},{14,12},{9,11},{15,13},{16,18},{22,... | collective-permute-start | bytes 2359304 | tf_op jit(solution)/shard_map/ppermute | solution.py:113
  76.4 11.0 %copy-start.3 = (f32[2,128,1536]{2,1,0:T(8,128)S(1)}, f32[2,128,1536]{2,1,0:T(8,128)}, u32[]{:S(2)}) copy-start(f32[2,128,1536]{2,1,0:T(8,128)} %copy-done.2) | copy-start | bytes 4718596
  76.4 11.0 %copy-start.5 = (bf16[2,128,1536]{2,1,0:T(8,128)(2,1)S(1)}, bf16[2,128,1536]{2,1,0:T(8,128)(2,1)}, u32[]{:S(2)}) copy-start(bf16[2,128,1536]{2,1,0:T(8,128)(2,1)} %copy-done.4) | copy-start | bytes 2359300
  76.4 29.5 %collective-permute-start.12 = (bf16[2,128,1536]{2,1,0:T(8,128)(2,1)S(1)}, bf16[2,128,1536]{2,1,0:T(8,128)(2,1)}, u32[]{:S(2)}, u32[]{:S(2)}) collective-permute-start(bf16[2,128,1536]{2,1,0:T(8,128)(2,1)S(1)} %fusion.1.rest_0_), channel_id=1, source_target_pairs={{2,4},{4,2},{3,5},{5,3},{10,12},{12,10},{11,13},{13,11},{18,20},{2... | collective-permute-start | bytes 2359304 | tf_op jit(solution)/shard_map/ppermute | solution.py:118
  81.1 15.6 %collective-permute-start.4 = (bf16[2,128,512]{2,1,0:T(8,128)(2,1)S(1)}, bf16[2,128,512]{2,1,0:T(8,128)(2,1)S(1)}, u32[]{:S(2)}, u32[]{:S(2)}) collective-permute-start(bf16[2,128,512]{2,1,0:T(8,128)(2,1)S(1)} %get-tuple-element.22), channel_id=1, source_target_pairs={{0,2},{6,4},{1,3},{7,5},{8,10},{14,12},{9,11},{15,13},{16,18},{22,... | collective-permute-start | bytes 786440 | tf_op jit(solution)/shard_map/ppermute | solution.py:113
  89.1 12.4 %collective-permute-start.17 = (bf16[128,1536]{1,0:T(8,128)(2,1)S(1)}, bf16[128,1536]{1,0:T(8,128)(2,1)S(1)}, u32[]{:S(2)}, u32[]{:S(2)}) collective-permute-start(bf16[128,1536]{1,0:T(8,128)(2,1)S(1)} %fusion.5.own), channel_id=1, source_target_pairs={{2,0},{4,6},{3,1},{5,7},{10,8},{12,14},{11,9},{13,15},{18,16},{20,... | collective-permute-start | bytes 1179656 | tf_op jit(solution)/shard_map/ppermute | solution.py:123
  96.7 14.2 %collective-permute-start.5 = (bf16[2,128,512]{2,1,0:T(8,128)(2,1)S(1)}, bf16[2,128,512]{2,1,0:T(8,128)(2,1)S(1)}, u32[]{:S(2)}, u32[]{:S(2)}) collective-permute-start(bf16[2,128,512]{2,1,0:T(8,128)(2,1)S(1)} %fusion.12), channel_id=1, source_target_pairs={{2,4},{4,2},{3,5},{5,3},{10,12},{12,10},{11,13},{13,11},{18,20},{2... | collective-permute-start | bytes 786440 | tf_op jit(solution)/shard_map/ppermute | solution.py:118
  99.3 15.0 %collective-permute-start.15 = (bf16[128,1536]{1,0:T(8,128)(2,1)S(1)}, bf16[128,1536]{1,0:T(8,128)(2,1)S(1)}, u32[]{:S(2)}, u32[]{:S(2)}) collective-permute-start(bf16[128,1536]{1,0:T(8,128)(2,1)S(1)} %fusion.7.own), channel_id=1, source_target_pairs={{2,0},{4,6},{3,1},{5,7},{10,8},{12,14},{11,9},{13,15},{18,16},{20,... | collective-permute-start | bytes 1179656 | tf_op jit(solution)/shard_map/ppermute | solution.py:123
  100.8 8.3 %collective-permute-start.10 = (bf16[2,128,1536]{2,1,0:T(8,128)(2,1)S(1)}, bf16[2,128,1536]{2,1,0:T(8,128)(2,1)S(1)}, u32[]{:S(2)}, u32[]{:S(2)}) collective-permute-start(bf16[2,128,1536]{2,1,0:T(8,128)(2,1)S(1)} %fusion.3), channel_id=1, source_target_pairs={{2,4},{4,2},{3,5},{5,3},{10,12},{12,10},{11,13},{13,11},{18,20},{2... | collective-permute-start | bytes 2359304 | tf_op jit(solution)/shard_map/ppermute | solution.py:118
  107.8 16.4 %collective-permute-start.13 = (bf16[128,1536]{1,0:T(8,128)(2,1)S(1)}, bf16[128,1536]{1,0:T(8,128)(2,1)S(1)}, u32[]{:S(2)}, u32[]{:S(2)}) collective-permute-start(bf16[128,1536]{1,0:T(8,128)(2,1)S(1)} %fusion.9.own), channel_id=1, source_target_pairs={{2,0},{4,6},{3,1},{5,7},{10,8},{12,14},{11,9},{13,15},{18,16},{20,... | collective-permute-start | bytes 1179656 | tf_op jit(solution)/shard_map/ppermute | solution.py:123
  109.7 31.9 %collective-permute-start.11 = (bf16[128,1536]{1,0:T(8,128)(2,1)S(1)}, bf16[128,1536]{1,0:T(8,128)(2,1)S(1)}, u32[]{:S(2)}, u32[]{:S(2)}) collective-permute-start(bf16[128,1536]{1,0:T(8,128)(2,1)S(1)} %fusion.11.own), channel_id=1, source_target_pairs={{2,0},{4,6},{3,1},{5,7},{10,8},{12,14},{11,9},{13,15},{18,16},{20,... | collective-permute-start | bytes 1179656 | tf_op jit(solution)/shard_map/ppermute | solution.py:123
  111.2 34.8 %collective-permute-start.6 = (bf16[128,512]{1,0:T(8,128)(2,1)S(1)}, bf16[128,512]{1,0:T(8,128)(2,1)S(1)}, u32[]{:S(2)}, u32[]{:S(2)}) collective-permute-start(bf16[128,512]{1,0:T(8,128)(2,1)S(1)} %fusion.19.own), channel_id=1, source_target_pairs={{2,0},{4,6},{3,1},{5,7},{10,8},{12,14},{11,9},{13,15},{18,16},{20,... | collective-permute-start | bytes 393224 | tf_op jit(solution)/shard_map/ppermute | solution.py:123
  148.0 3.7 %copy-start.6 = (s32[32,128]{1,0:T(8,128)S(1)}, s32[32,128]{1,0:T(8,128)}, u32[]{:S(2)}) copy-start(s32[32,128]{1,0:T(8,128)} %param.9) | copy-start | bytes 49156
  148.1 2.0 %collective-permute-start.20 = (f32[64,2048]{1,0:T(8,128)S(1)}, f32[64,2048]{1,0:T(8,128)S(1)}, u32[]{:S(2)}, u32[]{:S(2)}) collective-permute-start(f32[64,2048]{1,0:T(8,128)S(1)} %slice.78), channel_id=1, source_target_pairs={{0,8},{8,0},{16,24},{24,16},{1,9},{9,1},{17,25},{25,17},{2,10},{10... | collective-permute-start | bytes 1572872 | tf_op jit(solution)/shard_map/ppermute | solution.py:139
  150.1 5.6 %collective-permute-start.21 = (bf16[32,2048]{1,0:T(8,128)(2,1)S(1)}, bf16[32,2048]{1,0:T(8,128)(2,1)S(1)}, u32[]{:S(2)}, u32[]{:S(2)}) collective-permute-start(bf16[32,2048]{1,0:T(8,128)(2,1)S(1)} %slice.136), channel_id=1, source_target_pairs={{0,16},{8,24},{16,0},{24,8},{1,17},{9,25},{17,1},{25,9},{2,18},{10... | collective-permute-start | bytes 393224 | tf_op jit(solution)/shard_map/ppermute | solution.py:139

commit v2 on v1

--- a/solution.py
+++ b/solution.py
@@ -6,8 +6,9 @@
 from jax.sharding import PartitionSpec as P
 
 F32, BF16 = jnp.float32, jnp.bfloat16
-SHARES = (1, 3, 3, 3, 3, 1)
-VMEM_LIMIT = 48 << 20
+SHARES = (1, 5, 6, 6, 5, 4, 1)
+SLOTS = 4
+VMEM_LIMIT = 40 << 20
 
 
 def swap(size, bit):
@@ -19,68 +20,109 @@
     return tile if tile * sum(shares) == units and tile % 128 == 0 else 0
 
 
-def up_kernel(x, g, u, *rest):
-    narrow, wide = rest[-2:]
-    a = jnp.dot(x[...], g[...], preferred_element_type=F32)
-    b = jnp.dot(x[...], u[...], preferred_element_type=F32)
-    narrow[0], narrow[1] = a.astype(BF16), b.astype(BF16)
-    wide[0], wide[1] = a, b
-
-
-def partial_sums(x, gate, up, first, count, tile, after):
-    rows, depth = x.shape
+def stream(count, copies, work):
+    for i in range(min(SLOTS, count)):
+        for copy in copies(i, i):
+            copy.start()
+
+    def step(i, _):
+        slot = lax.rem(i, SLOTS)
+        for copy in copies(i, slot):
+            copy.wait()
+        work(i, slot)
+
+        @pl.when(i + SLOTS < count)
+        def _():
+            for copy in copies(i + SLOTS, slot):
+                copy.start()
+
+        return 0
+
+    lax.fori_loop(0, count, step, 0)
+
+
+def up_kernel(first, count, tile, pieces, *refs):
+    parts, (gate, up) = refs[:pieces], refs[pieces : pieces + 2]
+    outs, (x, held, sems) = refs[:-3], refs[-3:]
+    narrow, wide = outs[-2:] if pieces == 1 else outs[-3:-1]
+
+    def copies(i, slot):
+        columns = pl.ds(pl.multiple_of((first + i) * tile, tile), tile)
+        return [
+            pltpu.make_async_copy(w.at[:, columns], held.at[slot, j], sems.at[slot, j])
+            for j, w in enumerate((gate, up))
+        ]
+
+    row = 0
+    for part in parts:
+        x[row : row + part.shape[0]] = part[...]
+        row += part.shape[0]
+    if pieces > 1:
+        outs[-1][...] = x[...]
+
+    def work(i, slot):
+        columns = pl.ds(pl.multiple_of(i * tile, tile), tile)
+        for j in range(2):
+            part = jnp.dot(x[...], held[slot, j], preferred_element_type=F32)
+            narrow[j, :, columns] = part.astype(BF16)
+            wide[j, :, columns] = part
+
+    stream(count, copies, work)
+
+
+def partial_sums(parts, gate, up, first, count, tile, after):
+    depth = gate.shape[0]
+    rows = sum(part.shape[0] for part in parts)
     units = count * tile
-    weight = pl.BlockSpec((depth, tile), lambda i: (0, first + i))
-    out = pl.BlockSpec((2, rows, tile), lambda i: (0, 0, i))
+    in_vmem, anywhere = pl.BlockSpec(memory_space=pltpu.VMEM), pl.BlockSpec(memory_space=pl.ANY)
+    out_shape = [jax.ShapeDtypeStruct((2, rows, units), BF16), jax.ShapeDtypeStruct((2, rows, units), F32)]
+    if len(parts) > 1:
+        out_shape.append(jax.ShapeDtypeStruct((rows, depth), BF16))
     return pl.pallas_call(
-        up_kernel,
-        grid=(count,),
-        in_specs=[pl.BlockSpec((rows, depth), lambda i: (0, 0)), weight, weight] + [pl.BlockSpec(memory_space=pl.ANY)] * len(after),
-        out_specs=[out, out],
-        out_shape=[
-            jax.ShapeDtypeStruct((2, rows, units), BF16),
-            jax.ShapeDtypeStruct((2, rows, units), F32),
+        lambda *refs: up_kernel(first, count, tile, len(parts), *refs),
+        in_specs=[in_vmem] * len(parts) + [anywhere] * (2 + len(after)),
+        out_specs=[in_vmem] * len(out_shape),
+        out_shape=out_shape,
+        scratch_shapes=[
+            pltpu.VMEM((rows, depth), BF16),
+            pltpu.VMEM((SLOTS, 2, depth, tile), BF16),
+            pltpu.SemaphoreType.DMA((SLOTS, 2)),
         ],
         compiler_params=pltpu.CompilerParams(vmem_limit_bytes=VMEM_LIMIT),
-        cost_estimate=pl.CostEstimate(
-            flops=4 * rows * depth * units, bytes_accessed=4 * depth * units, transcendentals=0
-        ),
         name="gate_up",
-    )(x, gate, up, *after)
-
-
-def down_kernel(inner, own, other, w, base, total):
-    h = jnp.where(inner[0] > 0, own[...], other[...])
-    part = jnp.dot(h, w[...], preferred_element_type=F32)
-
-    @pl.when(pl.program_id(0) == 0)
-    def _():
-        total[...] = base[...] + part
-
-    @pl.when(pl.program_id(0) > 0)
-    def _():
-        total[...] += part
+    )(*parts, gate, up, *after)
+
+
+def down_kernel(first, count, tile, inner, own, other, w, base, total, held, sems):
+    def copies(i, slot):
+        rows = pl.ds(pl.multiple_of((first + i) * tile, tile), tile)
+        return [pltpu.make_async_copy(w.at[rows], held.at[slot], sems.at[slot])]
+
+    def work(i, slot):
+        columns = pl.ds(pl.multiple_of(i * tile, tile), tile)
+        h = jnp.where(inner[0] > 0, own[:, columns], other[:, columns])
+        total[...] += jnp.dot(h, held[slot], preferred_element_type=F32)
+
+    total[...] = base[...]
+    stream(count, copies, work)
 
 
 def add_down(inner, own, other, down, base, first, count, tile):
     rows, width = base.shape
-    piece = pl.BlockSpec((rows, tile), lambda i, s: (0, i))
-    whole = pl.BlockSpec((rows, width), lambda i, s: (0, 0))
+    in_vmem = pl.BlockSpec(memory_space=pltpu.VMEM)
     return pl.pallas_call(
-        down_kernel,
-        grid_spec=pltpu.PrefetchScalarGridSpec(
-            num_scalar_prefetch=1,
-            grid=(count,),
-            in_specs=[piece, piece, pl.BlockSpec((tile, width), lambda i, s: (first + i, 0)), whole],
-            out_specs=whole,
-        ),
+        lambda *refs: down_kernel(first, count, tile, *refs),
+        in_specs=[
+            pl.BlockSpec(memory_space=pltpu.SMEM),
+            in_vmem,
+            in_vmem,
+            pl.BlockSpec(memory_space=pl.ANY),
+            in_vmem,
+        ],
+        out_specs=in_vmem,
         out_shape=jax.ShapeDtypeStruct((rows, width), F32),
+        scratch_shapes=[pltpu.VMEM((SLOTS, tile, width), BF16), pltpu.SemaphoreType.DMA((SLOTS,))],
         compiler_params=pltpu.CompilerParams(vmem_limit_bytes=VMEM_LIMIT),
-        cost_estimate=pl.CostEstimate(
-            flops=2 * rows * width * count * tile,
-            bytes_accessed=2 * width * count * tile,
-            transcendentals=0,
-        ),
         name="down",
     )(inner, own, other, down, base)
 
@@ -98,18 +140,22 @@
         tile = unit_tile(units, SHARES)
         inner = ((lax.axis_index("fsdp") + 1) // 2 == 1).astype(jnp.int32).reshape(1)
         scale = keep_scale(keep_bits, width)
-        x = tokens
+        parts = [tokens]
         bits = [1 << b for b in reversed(range((tensor - 1).bit_length()))]
         for bit in bits:
-            x = jnp.concatenate([x, lax.ppermute(x, "tensor", swap(tensor, bit))], axis=0)
-        total = jnp.zeros((x.shape[0], width), F32)
+            parts = parts + [lax.ppermute(part, "tensor", swap(tensor, bit)) for part in parts]
+        total = [jnp.zeros((rows * tensor, width), F32)]
         count = len(SHARES)
         firsts = [sum(SHARES[:c]) for c in range(count)]
         wide, heard, side, crossed, hidden, given = ([None] * count for _ in range(6))
 
         def send_out(c):
             after = [side[c - 2][1]] if c >= 2 else []
-            narrow, wide[c] = partial_sums(x, gate, up, firsts[c], SHARES[c], tile, after)
+            after += [crossed[c - 3]] if c >= 3 else []
+            after += [total[0]] if c >= 4 else []
+            out = partial_sums(parts, gate, up, firsts[c], SHARES[c], tile, after)
+            narrow, wide[c] = out[:2]
+            parts[:] = out[2:] or parts
             heard[c] = lax.ppermute(narrow, "fsdp", [(0, 1), (3, 2)])
 
         def cross(c):
@@ -131,7 +177,8 @@
                 give(c - 2)
             if 0 <= c - 3 < count:
                 p = c - 3
-                total = add_down(inner, hidden[p], given[p], down, total, firsts[p], SHARES[p], tile)
+                total[0] = add_down(inner, hidden[p], given[p], down, total[0], firsts[p], SHARES[p], tile)
+        total = total[0]
         for step, bit in enumerate(reversed(bits)):
             half = total.shape[0] // 2
             away = total[half:]

time: 157 us -> 143 us (0.911)
  waiting for transfers between devices: 39.6 us -> 34.9 us
  Pallas kernels: 54 us -> 49.7 us
  starting transfers between devices: 48.7 us -> 45.7 us
  other arithmetic: 11 us -> 8.79 us
    pallas_call x12 -> x14, Pallas kernels: 54 us -> 49.7 us  [the longest x7 29.9 us: partial_sums(): pl.pallas_call(lambda *refs: up_kernel(first, count, tile, len(parts), *r...]
    ppermute x6 -> x7, waiting for transfers between devices: 9.89 us -> 6.62 us  [send_out(): heard[c] = lax.ppermute(narrow, 'fsdp', [(0, 1), (3, 2)])]
    ppermute x6 -> x7, starting transfers between devices: 29.1 us -> 26.4 us  [send_out(): heard[c] = lax.ppermute(narrow, 'fsdp', [(0, 1), (3, 2)])]
    ppermute x6 -> x7, waiting for transfers between devices: 20.1 us -> 17.9 us  [give(): given[c] = lax.ppermute(hidden[c], 'fsdp', [(1, 0), (2, 3)])]
    add x6 -> x7, other arithmetic: 5.13 us -> 3.44 us  [give(): both = side[c][0] + crossed[c].astype(F32)]
    ppermute x6 -> x7, starting transfers between devices: 6.89 us -> 5.65 us  [cross(): crossed[c] = lax.ppermute(side[c][1], 'fsdp', [(1, 2), (2, 1)])]
    ppermute x6 -> x7, starting transfers between devices: 7.93 us -> 9.03 us  [give(): given[c] = lax.ppermute(hidden[c], 'fsdp', [(1, 0), (2, 3)])]
    ppermute x2 -> x3, waiting for transfers between devices: 4.29 us -> 5.05 us  [shards(): lax.ppermute(part, 'tensor', swap(tensor, bit))]
  transfers between devices with their start and end apart: 22 -> 26, of which waited for: 10 -> 11; matrix products, arithmetic and copies ran while one was open for 7% -> 6% of each run, Pallas kernels for 31% -> 32%
where the time goes in v2:
time: 143 us; the launch traced here: 142 us
  Pallas kernels  49.7 us (35%)
  starting transfers between devices  45.7 us (32%)
  waiting for transfers between devices  34.9 us (24%)
  other arithmetic  8.79 us (6%)
  local copies, waits for them, and re-layouts  2.47 us (2%)
    pallas_call x7, Pallas kernels, partial_sums(): pl.pallas_call(lambda *refs: up_kernel(first, count, tile, len(parts), *r...  29.9 us
    ppermute x7, starting transfers between devices, send_out(): heard[c] = lax.ppermute(narrow, 'fsdp', [(0, 1), (3, 2)])  26.4 us
    pallas_call x7, Pallas kernels, add_down(): pl.pallas_call(lambda *refs: down_kernel(first, count, tile, *refs), in_s...  19.8 us
    ppermute x7, waiting for transfers between devices, give(): given[c] = lax.ppermute(hidden[c], 'fsdp', [(1, 0), (2, 3)])  17.9 us
    ppermute x7, starting transfers between devices, give(): given[c] = lax.ppermute(hidden[c], 'fsdp', [(1, 0), (2, 3)])  9.03 us
    ppermute x7, waiting for transfers between devices, send_out(): heard[c] = lax.ppermute(narrow, 'fsdp', [(0, 1), (3, 2)])  6.62 us
    ppermute x7, starting transfers between devices, cross(): crossed[c] = lax.ppermute(side[c][1], 'fsdp', [(1, 2), (2, 1)])  5.65 us
    ppermute x2, waiting for transfers between devices, shards(): lax.ppermute(away, 'tensor', swap(tensor, bit)).astype(F32)  5.34 us
  transfers between devices with their start and end apart: 26, of which 11 were waited for; matrix products, arithmetic and copies ran while one was open for 6% of the time, Pallas kernels for 32%

profile of v2, /device:TPU:0, one launch (start us, length us, event | category | flops | bytes accessed | tf_op | source)
XLA Modules:
  0.0 142.1 jit_solution(2814489043672563851)
XLA Ops:
  0.0 3.0 %collective-permute-start = (bf16[32,2048]{1,0:T(8,128)(2,1)}, bf16[32,2048]{1,0:T(8,128)(2,1)S(1)}, u32[]{:S(2)}, u32[]{:S(2)}) collective-permute-start(bf16[32,2048]{1,0:T(8,128)(2,1)} %refs_0_.1), channel_id=1, source_target_pairs={{0,16},{8,24},{16,0},{24,8},{1,17},{9,25},{17,1},{25,9},{2,18},{10... | collective-permute-start | bytes 393224 | tf_op jit(solution)/shard_map/ppermute | solution.py:146
  3.0 3.7 %collective-permute-done.refs_1_ = bf16[32,2048]{1,0:T(8,128)(2,1)S(1)} collective-permute-done((bf16[32,2048]{1,0:T(8,128)(2,1)}, bf16[32,2048]{1,0:T(8,128)(2,1)S(1)}, u32[]{:S(2)}, u32[]{:S(2)}) %collective-permute-start) | collective-permute-done | bytes 131104 | tf_op jit(solution)/shard_map/ppermute | solution.py:146
  8.9 2.1 %gate_up.7 = (bf16[2,128,256]{2,1,0:T(8,128)(2,1)S(1)}, f32[2,128,256]{2,1,0:T(8,128)S(1)}, bf16[128,2048]{1,0:T(8,128)(2,1)S(1)}) custom-call(bf16[32,2048]{1,0:T(8,128)(2,1)S(1)} %copy-done, bf16[32,2048]{1,0:T(8,128)(2,1)S(1)} %collective-permute-done.refs_1_, bf16[32,2048]{1,0:T(8,128)(2,1)S(1)} %collective-permute-done.1.refs_2_, ...), custom_call_target="tpu_custom_call" | custom-call | tf_op jit(solution)/shard_map/gate_up/pallas_call | solution.py:81
  11.0 3.7 %collective-permute-start.3 = (bf16[2,128,256]{2,1,0:T(8,128)(2,1)S(1)}, bf16[2,128,256]{2,1,0:T(8,128)(2,1)S(1)}, u32[]{:S(2)}, u32[]{:S(2)}) collective-permute-start(bf16[2,128,256]{2,1,0:T(8,128)(2,1)S(1)} %get-tuple-element.22), channel_id=1, source_target_pairs={{0,2},{6,4},{1,3},{7,5},{8,10},{14,12},{9,11},{15,13},{16,18},{22,... | collective-permute-start | bytes 393224 | tf_op jit(solution)/shard_map/ppermute | solution.py:159
  14.7 4.9 %gate_up.9 = (bf16[2,128,1280]{2,1,0:T(8,128)(2,1)S(1)}, f32[2,128,1280]{2,1,0:T(8,128)S(1)}) custom-call(bf16[128,2048]{1,0:T(8,128)(2,1)S(1)} %get-tuple-element.20.refs_0_, bf16[2048,7168]{1,0:T(8,128)(2,1)} %refs_1_.11, bf16[2048,7168]{1,0:T(8,128)(2,1)} %refs_2_.11), custom_call_target="tpu_custom_call" | custom-call | tf_op jit(solution)/shard_map/gate_up/pallas_call | solution.py:81
  21.7 6.4 %gate_up.8 = (bf16[2,128,1536]{2,1,0:T(8,128)(2,1)}, f32[2,128,1536]{2,1,0:T(8,128)S(1)}) custom-call(bf16[128,2048]{1,0:T(8,128)(2,1)S(1)} %get-tuple-element.20.refs_0_, bf16[2048,7168]{1,0:T(8,128)(2,1)} %refs_1_.11, bf16[2048,7168]{1,0:T(8,128)(2,1)} %refs_2_.11, bf16[2,128,256]{2,1,0:T(8,128)(2,1)S(1)} %fusion.17.refs_3_), custom_call_target="tpu_custom_call" | custom-call | tf_op jit(solution)/shard_map/gate_up/pallas_call | solution.py:81
  28.1 5.0 %collective-permute-start.4 = (bf16[2,128,1536]{2,1,0:T(8,128)(2,1)}, bf16[2,128,1536]{2,1,0:T(8,128)(2,1)}, u32[]{:S(2)}, u32[]{:S(2)}) collective-permute-start(bf16[2,128,1536]{2,1,0:T(8,128)(2,1)} %get-tuple-element.24), channel_id=1, source_target_pairs={{0,2},{6,4},{1,3},{7,5},{8,10},{14,12},{9,11},{15,13},{16,18},{22,... | collective-permute-start | bytes 2359304 | tf_op jit(solution)/shard_map/ppermute | solution.py:159
  33.1 2.9 %collective-permute-done.5 = bf16[2,128,1280]{2,1,0:T(8,128)(2,1)S(1)} collective-permute-done((bf16[2,128,1280]{2,1,0:T(8,128)(2,1)S(1)}, bf16[2,128,1280]{2,1,0:T(8,128)(2,1)S(1)}, u32[]{:S(2)}, u32[]{:S(2)}) %collective-permute-start.5) | collective-permute-done | bytes 655392 | tf_op jit(solution)/shard_map/ppermute | solution.py:159
  37.8 1.5 %collective-permute-start.6 = (bf16[2,128,1280]{2,1,0:T(8,128)(2,1)}, bf16[2,128,1280]{2,1,0:T(8,128)(2,1)}, u32[]{:S(2)}, u32[]{:S(2)}) collective-permute-start(bf16[2,128,1280]{2,1,0:T(8,128)(2,1)} %fusion.2.refs_3_), channel_id=1, source_target_pairs={{2,4},{4,2},{3,5},{5,3},{10,12},{12,10},{11,13},{13,11},{18,20},{2... | collective-permute-start | bytes 1966088 | tf_op jit(solution)/shard_map/ppermute | solution.py:164
  41.3 7.0 %collective-permute-done.8.refs_2_ = bf16[128,256]{1,0:T(8,128)(2,1)} collective-permute-done((bf16[128,256]{1,0:T(8,128)(2,1)}, bf16[128,256]{1,0:T(8,128)(2,1)}, u32[]{:S(2)}, u32[]{:S(2)}) %collective-permute-start.8) | collective-permute-done | bytes 65568 | tf_op jit(solution)/shard_map/ppermute | solution.py:169
  48.4 2.4 %down.7.refs_5_.refs_4_ = f32[128,2048]{1,0:T(8,128)S(1)} custom-call(s32[1]{0:T(128)} %bitcast.1.refs_0_, bf16[128,256]{1,0:T(8,128)(2,1)} %fusion.22.refs_1_, bf16[128,256]{1,0:T(8,128)(2,1)} %collective-permute-done.8.refs_2_, bf16[7168,2048]{1,0:T(8,128)(2,1)} %refs_3_.13, f32[128,2048]{1,0:T(8,128)S(1)} %broadcast_in_dim.2.refs_4_), custom_call_target="tpu_custom_call" | custom-call | tf_op jit(solution)/shard_map/down/pallas_call | solution.py:113
  50.8 5.5 %gate_up.11 = (bf16[2,128,1536]{2,1,0:T(8,128)(2,1)S(1)}, f32[2,128,1536]{2,1,0:T(8,128)S(1)}) custom-call(bf16[128,2048]{1,0:T(8,128)(2,1)S(1)} %get-tuple-element.20.refs_0_, bf16[2048,7168]{1,0:T(8,128)(2,1)} %refs_1_.11, bf16[2048,7168]{1,0:T(8,128)(2,1)} %refs_2_.11, bf16[2,128,1280]{2,1,0:T(8,128)(2,1)} %fusion.2.refs_3_, ...), custom_call_target="tpu_custom_call" | custom-call | tf_op jit(solution)/shard_map/gate_up/pallas_call | solution.py:81
  56.3 1.6 %collective-permute-start.10 = (bf16[2,128,1536]{2,1,0:T(8,128)(2,1)S(1)}, bf16[2,128,1536]{2,1,0:T(8,128)(2,1)S(1)}, u32[]{:S(2)}, u32[]{:S(2)}) collective-permute-start(bf16[2,128,1536]{2,1,0:T(8,128)(2,1)S(1)} %get-tuple-element.30), channel_id=1, source_target_pairs={{0,2},{6,4},{1,3},{7,5},{8,10},{14,12},{9,11},{15,13},{16,18},{22,... | collective-permute-start | bytes 2359304 | tf_op jit(solution)/shard_map/ppermute | solution.py:159
  62.9 4.9 %gate_up.10 = (bf16[2,128,1280]{2,1,0:T(8,128)(2,1)S(1)}, f32[2,128,1280]{2,1,0:T(8,128)S(1)}) custom-call(bf16[128,2048]{1,0:T(8,128)(2,1)S(1)} %get-tuple-element.20.refs_0_, bf16[2048,7168]{1,0:T(8,128)(2,1)} %refs_1_.11, bf16[2048,7168]{1,0:T(8,128)(2,1)} %refs_2_.11, bf16[2,128,1536]{2,1,0:T(8,128)(2,1)S(1)} %fusion.refs_3_, ...), custom_call_target="tpu_custom_call" | custom-call | tf_op jit(solution)/shard_map/gate_up/pallas_call | solution.py:81
  67.8 4.6 %collective-permute-start.9 = (bf16[2,128,1280]{2,1,0:T(8,128)(2,1)S(1)}, bf16[2,128,1280]{2,1,0:T(8,128)(2,1)S(1)}, u32[]{:S(2)}, u32[]{:S(2)}) collective-permute-start(bf16[2,128,1280]{2,1,0:T(8,128)(2,1)S(1)} %get-tuple-element.28), channel_id=1, source_target_pairs={{0,2},{6,4},{1,3},{7,5},{8,10},{14,12},{9,11},{15,13},{16,18},{22,... | collective-permute-start | bytes 1966088 | tf_op jit(solution)/shard_map/ppermute | solution.py:159
  72.4 3.1 %collective-permute-done.10 = bf16[2,128,1536]{2,1,0:T(8,128)(2,1)S(1)} collective-permute-done((bf16[2,128,1536]{2,1,0:T(8,128)(2,1)S(1)}, bf16[2,128,1536]{2,1,0:T(8,128)(2,1)S(1)}, u32[]{:S(2)}, u32[]{:S(2)}) %collective-permute-start.10) | collective-permute-done | bytes 786464 | tf_op jit(solution)/shard_map/ppermute | solution.py:159
  76.4 3.1 %down.8.refs_4_.refs_5_ = f32[128,2048]{1,0:T(8,128)S(1)} custom-call(s32[1]{0:T(128)} %bitcast.1.refs_0_, bf16[128,1280]{1,0:T(8,128)(2,1)S(1)} %fusion.12.refs_1_, bf16[128,1280]{1,0:T(8,128)(2,1)S(1)} %collective-permute-done.14.refs_2_, bf16[7168,2048]{1,0:T(8,128)(2,1)} %refs_3_.13, f32[128,2048]{1,0:T(8,128)S(1)} %down.7.refs_5_.refs_4_), custom_call_target="tpu_custom_call" | custom-call | tf_op jit(solution)/shard_map/down/pallas_call | solution.py:113
  79.5 1.4 convert_add_fusion.1
  82.5 4.1 %gate_up.13 = (bf16[2,128,1024]{2,1,0:T(8,128)(2,1)S(1)}, f32[2,128,1024]{2,1,0:T(8,128)S(1)}) custom-call(bf16[128,2048]{1,0:T(8,128)(2,1)S(1)} %get-tuple-element.20.refs_0_, bf16[2048,7168]{1,0:T(8,128)(2,1)} %refs_1_.11, bf16[2048,7168]{1,0:T(8,128)(2,1)} %refs_2_.11, bf16[2,128,1536]{2,1,0:T(8,128)(2,1)S(1)} %fusion.1.refs_3_, ...), custom_call_target="tpu_custom_call" | custom-call | tf_op jit(solution)/shard_map/gate_up/pallas_call | solution.py:81
  86.5 6.1 %collective-permute-start.18 = (bf16[2,128,1024]{2,1,0:T(8,128)(2,1)S(1)}, bf16[2,128,1024]{2,1,0:T(8,128)(2,1)S(1)}, u32[]{:S(2)}, u32[]{:S(2)}) collective-permute-start(bf16[2,128,1024]{2,1,0:T(8,128)(2,1)S(1)} %get-tuple-element.34), channel_id=1, source_target_pairs={{0,2},{6,4},{1,3},{7,5},{8,10},{14,12},{9,11},{15,13},{16,18},{22,... | collective-permute-start | bytes 1572872 | tf_op jit(solution)/shard_map/ppermute | solution.py:159
  93.5 3.5 %down.9.refs_5_.refs_4_ = f32[128,2048]{1,0:T(8,128)S(1)} custom-call(s32[1]{0:T(128)} %bitcast.1.refs_0_, bf16[128,1536]{1,0:T(8,128)(2,1)S(1)} %fusion.7.refs_1_, bf16[128,1536]{1,0:T(8,128)(2,1)S(1)} %collective-permute-done.13.refs_2_, bf16[7168,2048]{1,0:T(8,128)(2,1)} %refs_3_.13, f32[128,2048]{1,0:T(8,128)S(1)} %down.8.refs_4_.refs_5_), custom_call_target="tpu_custom_call" | custom-call | tf_op jit(solution)/shard_map/down/pallas_call | solution.py:113
  97.0 2.1 %gate_up.12 = (bf16[2,128,256]{2,1,0:T(8,128)(2,1)S(1)}, f32[2,128,256]{2,1,0:T(8,128)S(1)}) custom-call(bf16[128,2048]{1,0:T(8,128)(2,1)S(1)} %get-tuple-element.20.refs_0_, bf16[2048,7168]{1,0:T(8,128)(2,1)} %refs_1_.11, bf16[2048,7168]{1,0:T(8,128)(2,1)} %refs_2_.11, bf16[2,128,1280]{2,1,0:T(8,128)(2,1)S(1)} %fusion.3.refs_3_, ...), custom_call_target="tpu_custom_call" | custom-call | tf_op jit(solution)/shard_map/gate_up/pallas_call | solution.py:81
  99.1 4.0 %collective-permute-start.15 = (bf16[2,128,256]{2,1,0:T(8,128)(2,1)S(1)}, bf16[2,128,256]{2,1,0:T(8,128)(2,1)S(1)}, u32[]{:S(2)}, u32[]{:S(2)}) collective-permute-start(bf16[2,128,256]{2,1,0:T(8,128)(2,1)S(1)} %get-tuple-element.32), channel_id=1, source_target_pairs={{0,2},{6,4},{1,3},{7,5},{8,10},{14,12},{9,11},{15,13},{16,18},{22,... | collective-permute-start | bytes 393224 | tf_op jit(solution)/shard_map/ppermute | solution.py:159
  112.0 2.4 %collective-permute-done.23.refs_2_ = bf16[128,1536]{1,0:T(8,128)(2,1)S(1)} collective-permute-done((bf16[128,1536]{1,0:T(8,128)(2,1)S(1)}, bf16[128,1536]{1,0:T(8,128)(2,1)S(1)}, u32[]{:S(2)}, u32[]{:S(2)}) %collective-permute-start.23) | collective-permute-done | bytes 393248 | tf_op jit(solution)/shard_map/ppermute | solution.py:169
  114.5 3.5 %down.10.refs_4_ = f32[128,2048]{1,0:T(8,128)S(1)} custom-call(s32[1]{0:T(128)} %bitcast.1.refs_0_, bf16[128,1536]{1,0:T(8,128)(2,1)S(1)} %fusion.5.refs_1_, bf16[128,1536]{1,0:T(8,128)(2,1)S(1)} %collective-permute-done.23.refs_2_, bf16[7168,2048]{1,0:T(8,128)(2,1)} %refs_3_.13, f32[128,2048]{1,0:T(8,128)S(1)} %down.9.refs_5_.refs_4_), custom_call_target="tpu_custom_call" | custom-call | tf_op jit(solution)/shard_map/down/pallas_call | solution.py:113
  117.9 8.2 %collective-permute-done.22.refs_2_ = bf16[128,1280]{1,0:T(8,128)(2,1)S(1)} collective-permute-done((bf16[128,1280]{1,0:T(8,128)(2,1)S(1)}, bf16[128,1280]{1,0:T(8,128)(2,1)S(1)}, u32[]{:S(2)}, u32[]{:S(2)}) %collective-permute-start.22) | collective-permute-done | bytes 327712 | tf_op jit(solution)/shard_map/ppermute | solution.py:169
  126.1 3.1 %down.11.refs_4_ = f32[128,2048]{1,0:T(8,128)S(1)} custom-call(s32[1]{0:T(128)} %bitcast.1.refs_0_, bf16[128,1280]{1,0:T(8,128)(2,1)S(1)} %fusion.10.refs_1_, bf16[128,1280]{1,0:T(8,128)(2,1)S(1)} %collective-permute-done.22.refs_2_, bf16[7168,2048]{1,0:T(8,128)(2,1)} %refs_3_.13, f32[128,2048]{1,0:T(8,128)S(1)} %down.10.refs_4_), custom_call_target="tpu_custom_call" | custom-call | tf_op jit(solution)/shard_map/down/pallas_call | solution.py:113
  129.5 2.5 %down.12.refs_4_ = f32[128,2048]{1,0:T(8,128)S(1)} custom-call(s32[1]{0:T(128)} %bitcast.1.refs_0_, bf16[128,1024]{1,0:T(8,128)(2,1)S(1)} %fusion.14.refs_1_, bf16[128,1024]{1,0:T(8,128)(2,1)S(1)} %collective-permute-done.20.refs_2_, bf16[7168,2048]{1,0:T(8,128)(2,1)} %refs_3_.13, f32[128,2048]{1,0:T(8,128)S(1)} %down.11.refs_4_), custom_call_target="tpu_custom_call" | custom-call | tf_op jit(solution)/shard_map/down/pallas_call | solution.py:113
  132.1 1.6 %down.13 = f32[128,2048]{1,0:T(8,128)S(1)} custom-call(s32[1]{0:T(128)} %bitcast.1.refs_0_, bf16[128,256]{1,0:T(8,128)(2,1)S(1)} %fusion.20.refs_1_, bf16[128,256]{1,0:T(8,128)(2,1)S(1)} %collective-permute-done.17.refs_2_, bf16[7168,2048]{1,0:T(8,128)(2,1)} %refs_3_.13, f32[128,2048]{1,0:T(8,128)S(1)} %down.12.refs_4_), custom_call_target="tpu_custom_call" | custom-call | tf_op jit(solution)/shard_map/down/pallas_call | solution.py:113
  133.8 1.9 %collective-permute-done.24 = f32[64,2048]{1,0:T(8,128)S(1)} collective-permute-done((f32[64,2048]{1,0:T(8,128)S(1)}, f32[64,2048]{1,0:T(8,128)S(1)}, u32[]{:S(2)}, u32[]{:S(2)}) %collective-permute-start.24) | collective-permute-done | bytes 524320 | tf_op jit(solution)/shard_map/ppermute | solution.py:186
  135.8 1.6 %collective-permute-start.25 = (bf16[32,2048]{1,0:T(8,128)(2,1)S(1)}, bf16[32,2048]{1,0:T(8,128)(2,1)S(1)}, u32[]{:S(2)}, u32[]{:S(2)}) collective-permute-start(bf16[32,2048]{1,0:T(8,128)(2,1)S(1)} %slice.154), channel_id=1, source_target_pairs={{0,16},{8,24},{16,0},{24,8},{1,17},{9,25},{17,1},{25,9},{2,18},{10... | collective-permute-start | bytes 393224 | tf_op jit(solution)/shard_map/ppermute | solution.py:186
  137.9 3.4 %collective-permute-done.25 = bf16[32,2048]{1,0:T(8,128)(2,1)S(1)} collective-permute-done((bf16[32,2048]{1,0:T(8,128)(2,1)S(1)}, bf16[32,2048]{1,0:T(8,128)(2,1)S(1)}, u32[]{:S(2)}, u32[]{:S(2)}) %collective-permute-start.25) | collective-permute-done | bytes 131104 | tf_op jit(solution)/shard_map/ppermute | solution.py:186
  (73 shorter events, 26.8 us)
Async XLA Ops:
  0.0 6.7 %collective-permute-start = (bf16[32,2048]{1,0:T(8,128)(2,1)}, bf16[32,2048]{1,0:T(8,128)(2,1)S(1)}, u32[]{:S(2)}, u32[]{:S(2)}) collective-permute-start(bf16[32,2048]{1,0:T(8,128)(2,1)} %refs_0_.1), channel_id=1, source_target_pairs={{0,16},{8,24},{16,0},{24,8},{1,17},{9,25},{17,1},{25,9},{2,18},{10... | collective-permute-start | bytes 393224 | tf_op jit(solution)/shard_map/ppermute | solution.py:146
  3.0 3.7 %collective-permute-start.1 = (bf16[32,2048]{1,0:T(8,128)(2,1)}, bf16[32,2048]{1,0:T(8,128)(2,1)S(1)}, u32[]{:S(2)}, u32[]{:S(2)}) collective-permute-start(bf16[32,2048]{1,0:T(8,128)(2,1)} %refs_0_.1), channel_id=1, source_target_pairs={{0,8},{8,0},{16,24},{24,16},{1,9},{9,1},{17,25},{25,17},{2,10},{10... | collective-permute-start | bytes 393224 | tf_op jit(solution)/shard_map/ppermute | solution.py:146
  6.7 1.3 collective-permute-start.2
  8.0 0.9 copy-start
  11.0 9.9 %collective-permute-start.3 = (bf16[2,128,256]{2,1,0:T(8,128)(2,1)S(1)}, bf16[2,128,256]{2,1,0:T(8,128)(2,1)S(1)}, u32[]{:S(2)}, u32[]{:S(2)}) collective-permute-start(bf16[2,128,256]{2,1,0:T(8,128)(2,1)S(1)} %get-tuple-element.22), channel_id=1, source_target_pairs={{0,2},{6,4},{1,3},{7,5},{8,10},{14,12},{9,11},{15,13},{16,18},{22,... | collective-permute-start | bytes 393224 | tf_op jit(solution)/shard_map/ppermute | solution.py:159
  19.6 16.4 %collective-permute-start.5 = (bf16[2,128,1280]{2,1,0:T(8,128)(2,1)S(1)}, bf16[2,128,1280]{2,1,0:T(8,128)(2,1)S(1)}, u32[]{:S(2)}, u32[]{:S(2)}) collective-permute-start(bf16[2,128,1280]{2,1,0:T(8,128)(2,1)S(1)} %get-tuple-element.26), channel_id=1, source_target_pairs={{0,2},{6,4},{1,3},{7,5},{8,10},{14,12},{9,11},{15,13},{16,18},{22,... | collective-permute-start | bytes 1966088 | tf_op jit(solution)/shard_map/ppermute | solution.py:159
  21.0 12.1 %collective-permute-start.7 = (bf16[2,128,256]{2,1,0:T(8,128)(2,1)S(1)}, bf16[2,128,256]{2,1,0:T(8,128)(2,1)S(1)}, u32[]{:S(2)}, u32[]{:S(2)}) collective-permute-start(bf16[2,128,256]{2,1,0:T(8,128)(2,1)S(1)} %fusion.17.refs_3_), channel_id=1, source_target_pairs={{2,4},{4,2},{3,5},{5,3},{10,12},{12,10},{11,13},{13,11},{18,20},{2... | collective-permute-start | bytes 393224 | tf_op jit(solution)/shard_map/ppermute | solution.py:164
  28.1 29.9 %collective-permute-start.4 = (bf16[2,128,1536]{2,1,0:T(8,128)(2,1)}, bf16[2,128,1536]{2,1,0:T(8,128)(2,1)}, u32[]{:S(2)}, u32[]{:S(2)}) collective-permute-start(bf16[2,128,1536]{2,1,0:T(8,128)(2,1)} %get-tuple-element.24), channel_id=1, source_target_pairs={{0,2},{6,4},{1,3},{7,5},{8,10},{14,12},{9,11},{15,13},{16,18},{22,... | collective-permute-start | bytes 2359304 | tf_op jit(solution)/shard_map/ppermute | solution.py:159
  36.0 0.9 copy-start.1
  37.8 22.3 %collective-permute-start.6 = (bf16[2,128,1280]{2,1,0:T(8,128)(2,1)}, bf16[2,128,1280]{2,1,0:T(8,128)(2,1)}, u32[]{:S(2)}, u32[]{:S(2)}) collective-permute-start(bf16[2,128,1280]{2,1,0:T(8,128)(2,1)} %fusion.2.refs_3_), channel_id=1, source_target_pairs={{2,4},{4,2},{3,5},{5,3},{10,12},{12,10},{11,13},{13,11},{18,20},{2... | collective-permute-start | bytes 1966088 | tf_op jit(solution)/shard_map/ppermute | solution.py:164
  40.0 8.3 %collective-permute-start.8 = (bf16[128,256]{1,0:T(8,128)(2,1)}, bf16[128,256]{1,0:T(8,128)(2,1)}, u32[]{:S(2)}, u32[]{:S(2)}) collective-permute-start(bf16[128,256]{1,0:T(8,128)(2,1)} %fusion.22.refs_1_), channel_id=1, source_target_pairs={{2,0},{4,6},{3,1},{5,7},{10,8},{12,14},{11,9},{13,15},{18,16},{20,... | collective-permute-start | bytes 196616 | tf_op jit(solution)/shard_map/ppermute | solution.py:169
  56.3 19.1 %collective-permute-start.10 = (bf16[2,128,1536]{2,1,0:T(8,128)(2,1)S(1)}, bf16[2,128,1536]{2,1,0:T(8,128)(2,1)S(1)}, u32[]{:S(2)}, u32[]{:S(2)}) collective-permute-start(bf16[2,128,1536]{2,1,0:T(8,128)(2,1)S(1)} %get-tuple-element.30), channel_id=1, source_target_pairs={{0,2},{6,4},{1,3},{7,5},{8,10},{14,12},{9,11},{15,13},{16,18},{22,... | collective-permute-start | bytes 2359304 | tf_op jit(solution)/shard_map/ppermute | solution.py:159
  58.0 2.1 %copy-start.2 = (bf16[2,128,1280]{2,1,0:T(8,128)(2,1)S(1)}, bf16[2,128,1280]{2,1,0:T(8,128)(2,1)}, u32[]{:S(2)}) copy-start(bf16[2,128,1280]{2,1,0:T(8,128)(2,1)} %copy-done.1) | copy-start | bytes 1966084
  59.4 20.1 %collective-permute-start.12 = (bf16[2,128,1536]{2,1,0:T(8,128)(2,1)S(1)}, bf16[2,128,1536]{2,1,0:T(8,128)(2,1)S(1)}, u32[]{:S(2)}, u32[]{:S(2)}) collective-permute-start(bf16[2,128,1536]{2,1,0:T(8,128)(2,1)S(1)} %fusion.refs_3_), channel_id=1, source_target_pairs={{2,4},{4,2},{3,5},{5,3},{10,12},{12,10},{11,13},{13,11},{18,20},{2... | collective-permute-start | bytes 2359304 | tf_op jit(solution)/shard_map/ppermute | solution.py:164
  61.6 14.8 %collective-permute-start.14 = (bf16[128,1280]{1,0:T(8,128)(2,1)S(1)}, bf16[128,1280]{1,0:T(8,128)(2,1)S(1)}, u32[]{:S(2)}, u32[]{:S(2)}) collective-permute-start(bf16[128,1280]{1,0:T(8,128)(2,1)S(1)} %fusion.12.refs_1_), channel_id=1, source_target_pairs={{2,0},{4,6},{3,1},{5,7},{10,8},{12,14},{11,9},{13,15},{18,16},{20,... | collective-permute-start | bytes 983048 | tf_op jit(solution)/shard_map/ppermute | solution.py:169
  67.8 24.8 %collective-permute-start.9 = (bf16[2,128,1280]{2,1,0:T(8,128)(2,1)S(1)}, bf16[2,128,1280]{2,1,0:T(8,128)(2,1)S(1)}, u32[]{:S(2)}, u32[]{:S(2)}) collective-permute-start(bf16[2,128,1280]{2,1,0:T(8,128)(2,1)S(1)} %get-tuple-element.28), channel_id=1, source_target_pairs={{0,2},{6,4},{1,3},{7,5},{8,10},{14,12},{9,11},{15,13},{16,18},{22,... | collective-permute-start | bytes 1966088 | tf_op jit(solution)/shard_map/ppermute | solution.py:159
  75.6 21.3 %collective-permute-start.11 = (bf16[2,128,1536]{2,1,0:T(8,128)(2,1)S(1)}, bf16[2,128,1536]{2,1,0:T(8,128)(2,1)S(1)}, u32[]{:S(2)}, u32[]{:S(2)}) collective-permute-start(bf16[2,128,1536]{2,1,0:T(8,128)(2,1)S(1)} %fusion.1.refs_3_), channel_id=1, source_target_pairs={{2,4},{4,2},{3,5},{5,3},{10,12},{12,10},{11,13},{13,11},{18,20},{2... | collective-permute-start | bytes 2359304 | tf_op jit(solution)/shard_map/ppermute | solution.py:164
  81.2 12.3 %collective-permute-start.13 = (bf16[128,1536]{1,0:T(8,128)(2,1)S(1)}, bf16[128,1536]{1,0:T(8,128)(2,1)S(1)}, u32[]{:S(2)}, u32[]{:S(2)}) collective-permute-start(bf16[128,1536]{1,0:T(8,128)(2,1)S(1)} %fusion.7.refs_1_), channel_id=1, source_target_pairs={{2,0},{4,6},{3,1},{5,7},{10,8},{12,14},{11,9},{13,15},{18,16},{20,... | collective-permute-start | bytes 1179656 | tf_op jit(solution)/shard_map/ppermute | solution.py:169
  86.5 19.8 %collective-permute-start.18 = (bf16[2,128,1024]{2,1,0:T(8,128)(2,1)S(1)}, bf16[2,128,1024]{2,1,0:T(8,128)(2,1)S(1)}, u32[]{:S(2)}, u32[]{:S(2)}) collective-permute-start(bf16[2,128,1024]{2,1,0:T(8,128)(2,1)S(1)} %get-tuple-element.34), channel_id=1, source_target_pairs={{0,2},{6,4},{1,3},{7,5},{8,10},{14,12},{9,11},{15,13},{16,18},{22,... | collective-permute-start | bytes 1572872 | tf_op jit(solution)/shard_map/ppermute | solution.py:159
  92.7 14.5 %collective-permute-start.21 = (bf16[2,128,1280]{2,1,0:T(8,128)(2,1)S(1)}, bf16[2,128,1280]{2,1,0:T(8,128)(2,1)S(1)}, u32[]{:S(2)}, u32[]{:S(2)}) collective-permute-start(bf16[2,128,1280]{2,1,0:T(8,128)(2,1)S(1)} %fusion.3.refs_3_), channel_id=1, source_target_pairs={{2,4},{4,2},{3,5},{5,3},{10,12},{12,10},{11,13},{13,11},{18,20},{2... | collective-permute-start | bytes 1966088 | tf_op jit(solution)/shard_map/ppermute | solution.py:164
  99.1 6.6 %collective-permute-start.15 = (bf16[2,128,256]{2,1,0:T(8,128)(2,1)S(1)}, bf16[2,128,256]{2,1,0:T(8,128)(2,1)S(1)}, u32[]{:S(2)}, u32[]{:S(2)}) collective-permute-start(bf16[2,128,256]{2,1,0:T(8,128)(2,1)S(1)} %get-tuple-element.32), channel_id=1, source_target_pairs={{0,2},{6,4},{1,3},{7,5},{8,10},{14,12},{9,11},{15,13},{16,18},{22,... | collective-permute-start | bytes 393224 | tf_op jit(solution)/shard_map/ppermute | solution.py:159
  103.6 10.8 %collective-permute-start.23 = (bf16[128,1536]{1,0:T(8,128)(2,1)S(1)}, bf16[128,1536]{1,0:T(8,128)(2,1)S(1)}, u32[]{:S(2)}, u32[]{:S(2)}) collective-permute-start(bf16[128,1536]{1,0:T(8,128)(2,1)S(1)} %fusion.5.refs_1_), channel_id=1, source_target_pairs={{2,0},{4,6},{3,1},{5,7},{10,8},{12,14},{11,9},{13,15},{18,16},{20,... | collective-permute-start | bytes 1179656 | tf_op jit(solution)/shard_map/ppermute | solution.py:169
  105.7 1.6 %collective-permute-start.16 = (bf16[2,128,256]{2,1,0:T(8,128)(2,1)S(1)}, bf16[2,128,256]{2,1,0:T(8,128)(2,1)S(1)}, u32[]{:S(2)}, u32[]{:S(2)}) collective-permute-start(bf16[2,128,256]{2,1,0:T(8,128)(2,1)S(1)} %fusion.18), channel_id=1, source_target_pairs={{2,4},{4,2},{3,5},{5,3},{10,12},{12,10},{11,13},{13,11},{18,20},{2... | collective-permute-start | bytes 393224 | tf_op jit(solution)/shard_map/ppermute | solution.py:164
  106.5 2.5 %collective-permute-start.19 = (bf16[2,128,1024]{2,1,0:T(8,128)(2,1)S(1)}, bf16[2,128,1024]{2,1,0:T(8,128)(2,1)S(1)}, u32[]{:S(2)}, u32[]{:S(2)}) collective-permute-start(bf16[2,128,1024]{2,1,0:T(8,128)(2,1)S(1)} %fusion.8), channel_id=1, source_target_pairs={{2,4},{4,2},{3,5},{5,3},{10,12},{12,10},{11,13},{13,11},{18,20},{2... | collective-permute-start | bytes 1572872 | tf_op jit(solution)/shard_map/ppermute | solution.py:164
  107.7 18.5 %collective-permute-start.22 = (bf16[128,1280]{1,0:T(8,128)(2,1)S(1)}, bf16[128,1280]{1,0:T(8,128)(2,1)S(1)}, u32[]{:S(2)}, u32[]{:S(2)}) collective-permute-start(bf16[128,1280]{1,0:T(8,128)(2,1)S(1)} %fusion.10.refs_1_), channel_id=1, source_target_pairs={{2,0},{4,6},{3,1},{5,7},{10,8},{12,14},{11,9},{13,15},{18,16},{20,... | collective-permute-start | bytes 983048 | tf_op jit(solution)/shard_map/ppermute | solution.py:169
  109.4 20.1 %collective-permute-start.20 = (bf16[128,1024]{1,0:T(8,128)(2,1)S(1)}, bf16[128,1024]{1,0:T(8,128)(2,1)S(1)}, u32[]{:S(2)}, u32[]{:S(2)}) collective-permute-start(bf16[128,1024]{1,0:T(8,128)(2,1)S(1)} %fusion.14.refs_1_), channel_id=1, source_target_pairs={{2,0},{4,6},{3,1},{5,7},{10,8},{12,14},{11,9},{13,15},{18,16},{20,... | collective-permute-start | bytes 786440 | tf_op jit(solution)/shard_map/ppermute | solution.py:169
  110.7 21.3 %collective-permute-start.17 = (bf16[128,256]{1,0:T(8,128)(2,1)S(1)}, bf16[128,256]{1,0:T(8,128)(2,1)S(1)}, u32[]{:S(2)}, u32[]{:S(2)}) collective-permute-start(bf16[128,256]{1,0:T(8,128)(2,1)S(1)} %fusion.20.refs_1_), channel_id=1, source_target_pairs={{2,0},{4,6},{3,1},{5,7},{10,8},{12,14},{11,9},{13,15},{18,16},{20,... | collective-permute-start | bytes 196616 | tf_op jit(solution)/shard_map/ppermute | solution.py:169
  133.6 3.7 %copy-start.3 = (s32[32,128]{1,0:T(8,128)S(1)}, s32[32,128]{1,0:T(8,128)}, u32[]{:S(2)}) copy-start(s32[32,128]{1,0:T(8,128)} %param.9) | copy-start | bytes 49156
  133.7 2.0 %collective-permute-start.24 = (f32[64,2048]{1,0:T(8,128)S(1)}, f32[64,2048]{1,0:T(8,128)S(1)}, u32[]{:S(2)}, u32[]{:S(2)}) collective-permute-start(f32[64,2048]{1,0:T(8,128)S(1)} %slice.88), channel_id=1, source_target_pairs={{0,8},{8,0},{16,24},{24,16},{1,9},{9,1},{17,25},{25,17},{2,10},{10... | collective-permute-start | bytes 1572872 | tf_op jit(solution)/shard_map/ppermute | solution.py:186
  135.8 5.6 %collective-permute-start.25 = (bf16[32,2048]{1,0:T(8,128)(2,1)S(1)}, bf16[32,2048]{1,0:T(8,128)(2,1)S(1)}, u32[]{:S(2)}, u32[]{:S(2)}) collective-permute-start(bf16[32,2048]{1,0:T(8,128)(2,1)S(1)} %slice.154), channel_id=1, source_target_pairs={{0,16},{8,24},{16,0},{24,8},{1,17},{9,25},{17,1},{25,9},{2,18},{10... | collective-permute-start | bytes 393224 | tf_op jit(solution)/shard_map/ppermute | solution.py:186

commit v3 on v2

--- a/solution.py
+++ b/solution.py
@@ -6,7 +6,8 @@
 from jax.sharding import PartitionSpec as P
 
 F32, BF16 = jnp.float32, jnp.bfloat16
-SHARES = (1, 5, 6, 6, 5, 4, 1)
+SHARES = (1, 5, 6, 6, 4, 4, 2)
+LAG = 3
 SLOTS = 4
 VMEM_LIMIT = 40 << 20
 
@@ -20,11 +21,13 @@
     return tile if tile * sum(shares) == units and tile % 128 == 0 else 0
 
 
-def stream(count, copies, work):
+def start(count, copies):
     for i in range(min(SLOTS, count)):
         for copy in copies(i, i):
             copy.start()
 
+
+def stream(count, copies, work):
     def step(i, _):
         slot = lax.rem(i, SLOTS)
         for copy in copies(i, slot):
@@ -41,10 +44,10 @@
     lax.fori_loop(0, count, step, 0)
 
 
-def up_kernel(first, count, tile, pieces, *refs):
-    parts, (gate, up) = refs[:pieces], refs[pieces : pieces + 2]
-    outs, (x, held, sems) = refs[:-3], refs[-3:]
-    narrow, wide = outs[-2:] if pieces == 1 else outs[-3:-1]
+def up_kernel(first, count, tile, pieces, loads, *refs):
+    parts, (gate, up), refs = refs[:pieces], refs[pieces : pieces + 2], refs[pieces + 2 :]
+    outs, (x, held, sems, sem) = refs[:-4], refs[-4:]
+    message, wide = outs[-2:] if pieces == 1 else outs[-3:-1]
 
     def copies(i, slot):
         columns = pl.ds(pl.multiple_of((first + i) * tile, tile), tile)
@@ -53,24 +56,45 @@
             for j, w in enumerate((gate, up))
         ]
 
-    row = 0
-    for part in parts:
-        x[row : row + part.shape[0]] = part[...]
-        row += part.shape[0]
-    if pieces > 1:
-        outs[-1][...] = x[...]
+    def place():
+        rows = parts[0].shape[0]
+        if pieces > 1:
+            own = pltpu.make_async_copy(parts[0], x.at[:rows], sem)
+            own.start()
+            for j in range(1, pieces):
+                x[j * rows : (j + 1) * rows] = parts[j][...]
+            own.wait()
+            outs[-1][...] = x[...]
+        return x if pieces > 1 else parts[0]
 
     def work(i, slot):
         columns = pl.ds(pl.multiple_of(i * tile, tile), tile)
         for j in range(2):
-            part = jnp.dot(x[...], held[slot, j], preferred_element_type=F32)
-            narrow[j, :, columns] = part.astype(BF16)
+            part = jnp.dot(rows[...], held[slot, j], preferred_element_type=F32)
             wide[j, :, columns] = part
+            if not loads:
+                message[j, :, columns] = part.astype(BF16)
+            else:
+
+                @pl.when(refs[0][0] == 0)
+                def _():
+                    message[j, :, columns] = part.astype(BF16)
+
+    start(count, copies)
+    rows = place()
+    if loads:
+
+        @pl.when(refs[0][0] > 0)
+        def _():
+            units, room = refs[1].shape[1], count * tile
+            message[0, :, : min(units, room)] = refs[1][:, : min(units, room)]
+            if units > room:
+                message[1, :, : units - room] = refs[1][:, room:]
 
     stream(count, copies, work)
 
 
-def partial_sums(parts, gate, up, first, count, tile, after):
+def partial_sums(parts, gate, up, first, count, tile, load, after):
     depth = gate.shape[0]
     rows = sum(part.shape[0] for part in parts)
     units = count * tile
@@ -79,30 +103,39 @@
     if len(parts) > 1:
         out_shape.append(jax.ShapeDtypeStruct((rows, depth), BF16))
     return pl.pallas_call(
-        lambda *refs: up_kernel(first, count, tile, len(parts), *refs),
-        in_specs=[in_vmem] * len(parts) + [anywhere] * (2 + len(after)),
+        lambda *refs: up_kernel(first, count, tile, len(parts), bool(load), *refs),
+        in_specs=[anywhere if len(parts) > 1 else in_vmem]
+        + [in_vmem] * (len(parts) - 1)
+        + [anywhere] * 2
+        + ([pl.BlockSpec(memory_space=pltpu.SMEM), in_vmem] if load else [])
+        + [anywhere] * len(after),
         out_specs=[in_vmem] * len(out_shape),
         out_shape=out_shape,
         scratch_shapes=[
-            pltpu.VMEM((rows, depth), BF16),
+            pltpu.VMEM((rows, depth) if len(parts) > 1 else (16, 128), BF16),
             pltpu.VMEM((SLOTS, 2, depth, tile), BF16),
             pltpu.SemaphoreType.DMA((SLOTS, 2)),
+            pltpu.SemaphoreType.DMA,
         ],
         compiler_params=pltpu.CompilerParams(vmem_limit_bytes=VMEM_LIMIT),
         name="gate_up",
-    )(*parts, gate, up, *after)
+    )(*parts, gate, up, *load, *after)
 
 
 def down_kernel(first, count, tile, inner, own, other, w, base, total, held, sems):
+    room = other.shape[2] // tile
+
     def copies(i, slot):
         rows = pl.ds(pl.multiple_of((first + i) * tile, tile), tile)
         return [pltpu.make_async_copy(w.at[rows], held.at[slot], sems.at[slot])]
 
     def work(i, slot):
         columns = pl.ds(pl.multiple_of(i * tile, tile), tile)
-        h = jnp.where(inner[0] > 0, own[:, columns], other[:, columns])
+        there = pl.ds(pl.multiple_of(lax.rem(i, room) * tile, tile), tile)
+        h = jnp.where(inner[0] > 0, own[:, columns], other[lax.div(i, room), :, there])
         total[...] += jnp.dot(h, held[slot], preferred_element_type=F32)
 
+    start(count, copies)
     total[...] = base[...]
     stream(count, copies, work)
 
@@ -127,6 +160,19 @@
     )(inner, own, other, down, base)
 
 
+def hold(value, *tokens):
+    anywhere = pl.BlockSpec(memory_space=pl.ANY)
+    return pl.pallas_call(
+        lambda *refs: None,
+        in_specs=[anywhere] * (1 + len(tokens)),
+        out_specs=anywhere,
+        out_shape=jax.ShapeDtypeStruct(value.shape, value.dtype),
+        input_output_aliases={0: 0},
+        compiler_params=pltpu.CompilerParams(vmem_limit_bytes=VMEM_LIMIT),
+        name="hold",
+    )(value, *tokens)
+
+
 def keep_scale(keep_bits, width):
     shifts = jnp.arange(16, dtype=jnp.int32)
     keep = jnp.right_shift(keep_bits[:, :, None], shifts[None, None, :]) & 1
@@ -144,41 +190,65 @@
         bits = [1 << b for b in reversed(range((tensor - 1).bit_length()))]
         for bit in bits:
             parts = parts + [lax.ppermute(part, "tensor", swap(tensor, bit)) for part in parts]
-        total = [jnp.zeros((rows * tensor, width), F32)]
         count = len(SHARES)
         firsts = [sum(SHARES[:c]) for c in range(count)]
-        wide, heard, side, crossed, hidden, given = ([None] * count for _ in range(6))
-
-        def send_out(c):
-            after = [side[c - 2][1]] if c >= 2 else []
-            after += [crossed[c - 3]] if c >= 3 else []
-            after += [total[0]] if c >= 4 else []
-            out = partial_sums(parts, gate, up, firsts[c], SHARES[c], tile, after)
-            narrow, wide[c] = out[:2]
+        wide, narrow, heard, side, crossed, kept, given = ([None] * count for _ in range(7))
+        total = [jnp.zeros((rows * tensor, width), F32)]
+        last = count - 1
+
+        outward, across, back = [(0, 1), (3, 2)], [(1, 2), (2, 1)], [(1, 0), (2, 3)]
+
+        def carries(c):
+            return c >= LAG and SHARES[c - LAG] <= 2 * SHARES[c]
+
+        def work_out(c):
+            after = [side[c - 2]] if c >= 2 else []
+            after += [kept[c - 3]] if c >= 3 else []
+            after += [total[c - 4]] if c >= 5 else []
+            load = [inner, kept[c - LAG]] if carries(c) else []
+            out = partial_sums(parts, gate, up, firsts[c], SHARES[c], tile, load, after)
+            wide[c] = out[1]
             parts[:] = out[2:] or parts
-            heard[c] = lax.ppermute(narrow, "fsdp", [(0, 1), (3, 2)])
-
-        def cross(c):
-            added = wide[c] + heard[c].astype(F32)
-            side[c] = (added, added.astype(BF16))
-            crossed[c] = lax.ppermute(side[c][1], "fsdp", [(1, 2), (2, 1)])
-
-        def give(c):
-            both = side[c][0] + crossed[c].astype(F32)
-            hidden[c] = (jax.nn.silu(both[0]) * both[1]).astype(BF16)
-            given[c] = lax.ppermute(hidden[c], "fsdp", [(1, 0), (2, 3)])
-
-        for c in range(count + 3):
+            heard[c] = lax.ppermute(out[0], "fsdp", outward + back if load else outward)
+            if load:
+                given[c - LAG] = heard[c]
+
+        def add(c):
+            wide[c] = wide[c] + heard[c].astype(F32)
+            side[c] = wide[c].astype(BF16)
+            crossed[c] = lax.ppermute(side[c], "fsdp", across)
+
+        def finish(c):
+            if c >= count - 3:
+                wait = [side[count - 1]] if c == count - 3 else [kept[c - 1]]
+                wait += [total[c - 2]]
+                crossed[c] = hold(crossed[c], *wait)
+            both = wide[c] + crossed[c].astype(F32)
+            kept[c] = (jax.nn.silu(both[0]) * both[1]).astype(BF16)
+            if c + LAG >= count or not carries(c + LAG):
+                given[c] = lax.ppermute(kept[c], "fsdp", back)[None]
+
+        def project(c):
+            total.append(add_down(inner, kept[c], given[c], down, total[-1], firsts[c], SHARES[c], tile))
+
+        for c in range(count + 1):
             if c < count:
-                send_out(c)
-            if 0 <= c - 1 < count:
-                cross(c - 1)
-            if 0 <= c - 2 < count:
-                give(c - 2)
-            if 0 <= c - 3 < count:
-                p = c - 3
-                total[0] = add_down(inner, hidden[p], given[p], down, total[0], firsts[p], SHARES[p], tile)
-        total = total[0]
+                work_out(c)
+            if c == count:
+                heard[c - 1] = hold(heard[c - 1], side[c - 2])
+            if c >= 1:
+                add(c - 1)
+            if 2 <= c and c - 2 < count - 3:
+                finish(c - 2)
+            if 4 <= c and c - 4 < count - 5:
+                project(c - 4)
+        for c in range(count - 3, count):
+            while len(total) <= c - 2:
+                project(len(total) - 1)
+            finish(c)
+        while len(total) <= count:
+            project(len(total) - 1)
+        total = total[-1]
         for step, bit in enumerate(reversed(bits)):
             half = total.shape[0] // 2
             away = total[half:]

time: 143 us -> 138 us (0.965)
  waiting for transfers between devices: 34.9 us -> 29.4 us
  other arithmetic: 8.79 us -> 5.06 us
  starting transfers between devices: 45.7 us -> 49.2 us
    ppermute x21 -> x18, waiting for transfers between devices: 24.5 us -> 19 us  [the longest x7 12.1 us: work_out(): heard[c] = lax.ppermute(out[0], 'fsdp', outward + back if load else outward)]
    ppermute x21 -> x18, starting transfers between devices: 41 us -> 44.5 us  [the longest x7 33.9 us: work_out(): heard[c] = lax.ppermute(out[0], 'fsdp', outward + back if load else outward)]
    convert_element_type x14, other arithmetic: 4.56 us -> 1.96 us  [the longest x7 1.07 us: finish(): kept[c] = (jax.nn.silu(both[0]) * both[1]).astype(BF16)]
    pallas_call x7 -> x11, Pallas kernels: 29.9 us -> 32.1 us  [the longest x7 32.1 us: partial_sums(): pl.pallas_call(lambda *refs: up_kernel(first, count, tile, len(parts), bo...]
  transfers between devices with their start and end apart: 26 -> 23, of which waited for: 11 -> 9; matrix products, arithmetic and copies ran while one was open for 6% -> 4% of each run, Pallas kernels for 32% -> 34%
where the time goes in v3:
time: 138 us; the launch traced here: 137 us
  Pallas kernels  50.7 us (37%)
  starting transfers between devices  49.2 us (36%)
  waiting for transfers between devices  29.4 us (21%)
  other arithmetic  5.06 us (4%)
  local copies, waits for them, and re-layouts  2.27 us (2%)
    ppermute x7, starting transfers between devices, work_out(): heard[c] = lax.ppermute(out[0], 'fsdp', outward + back if load else outward)  33.9 us
    pallas_call x7, Pallas kernels, partial_sums(): pl.pallas_call(lambda *refs: up_kernel(first, count, tile, len(parts), bo...  32.1 us
    pallas_call x7, Pallas kernels, add_down(): pl.pallas_call(lambda *refs: down_kernel(first, count, tile, *refs), in_s...  18.6 us
    ppermute x7, waiting for transfers between devices, work_out(): heard[c] = lax.ppermute(out[0], 'fsdp', outward + back if load else outward)  12.1 us
    ppermute x4, waiting for transfers between devices, finish(): given[c] = lax.ppermute(kept[c], 'fsdp', back)[None]  6.86 us
    ppermute x7, starting transfers between devices, add(): crossed[c] = lax.ppermute(side[c], 'fsdp', across)  5.51 us
    ppermute x2, waiting for transfers between devices, shards(): lax.ppermute(away, 'tensor', swap(tensor, bit)).astype(F32)  5.34 us
    ppermute x4, starting transfers between devices, finish(): given[c] = lax.ppermute(kept[c], 'fsdp', back)[None]  5.17 us
  transfers between devices with their start and end apart: 23, of which 9 were waited for; matrix products, arithmetic and copies ran while one was open for 4% of the time, Pallas kernels for 34%

profile of v3, /device:TPU:0, one launch (start us, length us, event | category | flops | bytes accessed | tf_op | source)
XLA Modules:
  0.0 137.2 jit_solution(1365458117830369427)
XLA Ops:
  0.0 3.0 %collective-permute-start = (bf16[32,2048]{1,0:T(8,128)(2,1)}, bf16[32,2048]{1,0:T(8,128)(2,1)S(1)}, u32[]{:S(2)}, u32[]{:S(2)}) collective-permute-start(bf16[32,2048]{1,0:T(8,128)(2,1)} %refs_0_.1), channel_id=1, source_target_pairs={{0,16},{8,24},{16,0},{24,8},{1,17},{9,25},{17,1},{25,9},{2,18},{10... | collective-permute-start | bytes 393224 | tf_op jit(solution)/shard_map/ppermute | solution.py:192
  3.0 3.7 %collective-permute-done.refs_1_ = bf16[32,2048]{1,0:T(8,128)(2,1)S(1)} collective-permute-done((bf16[32,2048]{1,0:T(8,128)(2,1)}, bf16[32,2048]{1,0:T(8,128)(2,1)S(1)}, u32[]{:S(2)}, u32[]{:S(2)}) %collective-permute-start) | collective-permute-done | bytes 131104 | tf_op jit(solution)/shard_map/ppermute | solution.py:192
  6.7 1.3 collective-permute-done.2.refs_3_
  8.9 2.1 %gate_up.7 = (bf16[2,128,256]{2,1,0:T(8,128)(2,1)S(1)}, f32[2,128,256]{2,1,0:T(8,128)S(1)}, bf16[128,2048]{1,0:T(8,128)(2,1)S(1)}) custom-call(bf16[32,2048]{1,0:T(8,128)(2,1)S(1)} %copy-done, bf16[32,2048]{1,0:T(8,128)(2,1)S(1)} %collective-permute-done.refs_1_, bf16[32,2048]{1,0:T(8,128)(2,1)S(1)} %collective-permute-done.1.refs_2_, ...), custom_call_target="tpu_custom_call" | custom-call | tf_op jit(solution)/shard_map/gate_up/pallas_call | solution.py:105
  11.0 3.7 %collective-permute-start.5 = (bf16[2,128,256]{2,1,0:T(8,128)(2,1)S(1)}, bf16[2,128,256]{2,1,0:T(8,128)(2,1)S(1)}, u32[]{:S(2)}, u32[]{:S(2)}) collective-permute-start(bf16[2,128,256]{2,1,0:T(8,128)(2,1)S(1)} %get-tuple-element.24), channel_id=1, source_target_pairs={{0,2},{6,4},{1,3},{7,5},{8,10},{14,12},{9,11},{15,13},{16,18},{22,... | collective-permute-start | bytes 393224 | tf_op jit(solution)/shard_map/ppermute | solution.py:212
  14.7 4.9 %gate_up.8 = (bf16[2,128,1280]{2,1,0:T(8,128)(2,1)S(1)}, f32[2,128,1280]{2,1,0:T(8,128)S(1)}) custom-call(bf16[128,2048]{1,0:T(8,128)(2,1)S(1)} %get-tuple-element.20.refs_0_, bf16[2048,7168]{1,0:T(8,128)(2,1)} %refs_1_.11, bf16[2048,7168]{1,0:T(8,128)(2,1)} %refs_2_.11), custom_call_target="tpu_custom_call" | custom-call | tf_op jit(solution)/shard_map/gate_up/pallas_call | solution.py:105
  19.6 1.3 collective-permute-start.3
  23.0 5.6 %gate_up.9 = (bf16[2,128,1536]{2,1,0:T(8,128)(2,1)S(1)}, f32[2,128,1536]{2,1,0:T(8,128)S(1)}) custom-call(bf16[128,2048]{1,0:T(8,128)(2,1)S(1)} %get-tuple-element.20.refs_0_, bf16[2048,7168]{1,0:T(8,128)(2,1)} %refs_1_.11, bf16[2048,7168]{1,0:T(8,128)(2,1)} %refs_2_.11, bf16[2,128,256]{2,1,0:T(8,128)(2,1)S(1)} %fusion.20.refs_3_), custom_call_target="tpu_custom_call" | custom-call | tf_op jit(solution)/shard_map/gate_up/pallas_call | solution.py:105
  28.6 3.5 %collective-permute-start.6 = (bf16[2,128,1536]{2,1,0:T(8,128)(2,1)S(1)}, bf16[2,128,1536]{2,1,0:T(8,128)(2,1)S(1)}, u32[]{:S(2)}, u32[]{:S(2)}) collective-permute-start(bf16[2,128,1536]{2,1,0:T(8,128)(2,1)S(1)} %get-tuple-element.26), channel_id=1, source_target_pairs={{0,2},{6,4},{1,3},{7,5},{8,10},{14,12},{9,11},{15,13},{16,18},{22,... | collective-permute-start | bytes 2359304 | tf_op jit(solution)/shard_map/ppermute | solution.py:212
  33.0 3.0 %collective-permute-done.3 = bf16[2,128,1280]{2,1,0:T(8,128)(2,1)S(1)} collective-permute-done((bf16[2,128,1280]{2,1,0:T(8,128)(2,1)S(1)}, bf16[2,128,1280]{2,1,0:T(8,128)(2,1)S(1)}, u32[]{:S(2)}, u32[]{:S(2)}) %collective-permute-start.3) | collective-permute-done | bytes 655392 | tf_op jit(solution)/shard_map/ppermute | solution.py:212
  36.9 6.7 %gate_up.11 = (bf16[2,128,1536]{2,1,0:T(8,128)(2,1)S(1)}, f32[2,128,1536]{2,1,0:T(8,128)S(1)}) custom-call(bf16[128,2048]{1,0:T(8,128)(2,1)S(1)} %get-tuple-element.20.refs_0_, bf16[2048,7168]{1,0:T(8,128)(2,1)} %refs_1_.11, bf16[2048,7168]{1,0:T(8,128)(2,1)} %refs_2_.11, s32[1]{0:T(128)} %bitcast.1.refs_3_.refs_0_, ...), custom_call_target="tpu_custom_call" | custom-call | tf_op jit(solution)/shard_map/gate_up/pallas_call | solution.py:105
  43.6 5.3 %collective-permute-start.9 = (bf16[2,128,1536]{2,1,0:T(8,128)(2,1)S(1)}, bf16[2,128,1536]{2,1,0:T(8,128)(2,1)S(1)}, u32[]{:S(2)}, u32[]{:S(2)}) collective-permute-start(bf16[2,128,1536]{2,1,0:T(8,128)(2,1)S(1)} %get-tuple-element.30), channel_id=1, source_target_pairs={{0,2},{6,4},{2,0},{4,6},{1,3},{7,5},{3,1},{5,7},{8,10},{14,12},{10... | collective-permute-start | bytes 2359304 | tf_op jit(solution)/shard_map/ppermute | solution.py:212
  48.9 3.9 %collective-permute-done.6 = bf16[2,128,1536]{2,1,0:T(8,128)(2,1)S(1)} collective-permute-done((bf16[2,128,1536]{2,1,0:T(8,128)(2,1)S(1)}, bf16[2,128,1536]{2,1,0:T(8,128)(2,1)S(1)}, u32[]{:S(2)}, u32[]{:S(2)}) %collective-permute-start.6) | collective-permute-done | bytes 786464 | tf_op jit(solution)/shard_map/ppermute | solution.py:212
  54.2 5.0 %gate_up.10 = (bf16[2,128,1024]{2,1,0:T(8,128)(2,1)S(1)}, f32[2,128,1024]{2,1,0:T(8,128)S(1)}) custom-call(bf16[128,2048]{1,0:T(8,128)(2,1)S(1)} %get-tuple-element.20.refs_0_, bf16[2048,7168]{1,0:T(8,128)(2,1)} %refs_1_.11, bf16[2048,7168]{1,0:T(8,128)(2,1)} %refs_2_.11, s32[1]{0:T(128)} %bitcast.1.refs_3_.refs_0_, ...), custom_call_target="tpu_custom_call" | custom-call | tf_op jit(solution)/shard_map/gate_up/pallas_call | solution.py:105
  59.2 5.3 %collective-permute-start.7 = (bf16[2,128,1024]{2,1,0:T(8,128)(2,1)S(1)}, bf16[2,128,1024]{2,1,0:T(8,128)(2,1)S(1)}, u32[]{:S(2)}, u32[]{:S(2)}) collective-permute-start(bf16[2,128,1024]{2,1,0:T(8,128)(2,1)S(1)} %get-tuple-element.28), channel_id=1, source_target_pairs={{0,2},{6,4},{2,0},{4,6},{1,3},{7,5},{3,1},{5,7},{8,10},{14,12},{10... | collective-permute-start | bytes 1572872 | tf_op jit(solution)/shard_map/ppermute | solution.py:212
  64.5 5.2 %collective-permute-done.9.refs_2_ = bf16[2,128,1536]{2,1,0:T(8,128)(2,1)S(1)} collective-permute-done((bf16[2,128,1536]{2,1,0:T(8,128)(2,1)S(1)}, bf16[2,128,1536]{2,1,0:T(8,128)(2,1)S(1)}, u32[]{:S(2)}, u32[]{:S(2)}) %collective-permute-start.9) | collective-permute-done | bytes 786464 | tf_op jit(solution)/shard_map/ppermute | solution.py:212
  70.7 1.6 %down.7.refs_4_.refs_7_ = f32[128,2048]{1,0:T(8,128)S(1)} custom-call(s32[1]{0:T(128)} %bitcast.1.refs_3_.refs_0_, bf16[128,256]{1,0:T(8,128)(2,1)S(1)} %fusion.22.refs_4_.refs_6_.refs_1_, bf16[2,128,1536]{2,1,0:T(8,128)(2,1)S(1)} %collective-permute-done.9.refs_2_, bf16[7168,2048]{1,0:T(8,128)(2,1)} %refs_3_.13, f32[128,2048]{1,0:T(8,128)S(1)} %broadcast_in_dim.17.refs_4_), custom_call_target="tpu_custom_call" | custom-call | tf_op jit(solution)/shard_map/down/pallas_call | solution.py:146
  72.9 5.0 %gate_up.13 = (bf16[2,128,1024]{2,1,0:T(8,128)(2,1)S(1)}, f32[2,128,1024]{2,1,0:T(8,128)S(1)}) custom-call(bf16[128,2048]{1,0:T(8,128)(2,1)S(1)} %get-tuple-element.20.refs_0_, bf16[2048,7168]{1,0:T(8,128)(2,1)} %refs_1_.11, bf16[2048,7168]{1,0:T(8,128)(2,1)} %refs_2_.11, s32[1]{0:T(128)} %bitcast.1.refs_3_.refs_0_, ...), custom_call_target="tpu_custom_call" | custom-call | tf_op jit(solution)/shard_map/gate_up/pallas_call | solution.py:105
  77.9 5.3 %collective-permute-start.13 = (bf16[2,128,1024]{2,1,0:T(8,128)(2,1)S(1)}, bf16[2,128,1024]{2,1,0:T(8,128)(2,1)S(1)}, u32[]{:S(2)}, u32[]{:S(2)}) collective-permute-start(bf16[2,128,1024]{2,1,0:T(8,128)(2,1)S(1)} %get-tuple-element.34), channel_id=1, source_target_pairs={{0,2},{6,4},{2,0},{4,6},{1,3},{7,5},{3,1},{5,7},{8,10},{14,12},{10... | collective-permute-start | bytes 1572872 | tf_op jit(solution)/shard_map/ppermute | solution.py:212
  84.0 3.1 %down.8.refs_5_.refs_2_.refs_4_ = f32[128,2048]{1,0:T(8,128)S(1)} custom-call(s32[1]{0:T(128)} %bitcast.1.refs_3_.refs_0_, bf16[128,1280]{1,0:T(8,128)(2,1)S(1)} %fusion.10.refs_4_.refs_6_.refs_1_, bf16[2,128,1024]{2,1,0:T(8,128)(2,1)S(1)} %collective-permute-done.7.refs_2_, bf16[7168,2048]{1,0:T(8,128)(2,1)} %refs_3_.13, f32[128,2048]{1,0:T(8,128)S(1)} %down.7.refs_4_.refs_7_), custom_call_target="tpu_custom_call" | custom-call | tf_op jit(solution)/shard_map/down/pallas_call | solution.py:146
  89.0 2.8 %gate_up.12 = (bf16[2,128,512]{2,1,0:T(8,128)(2,1)S(1)}, f32[2,128,512]{2,1,0:T(8,128)S(1)}) custom-call(bf16[128,2048]{1,0:T(8,128)(2,1)S(1)} %get-tuple-element.20.refs_0_, bf16[2048,7168]{1,0:T(8,128)(2,1)} %refs_1_.11, bf16[2048,7168]{1,0:T(8,128)(2,1)} %refs_2_.11, bf16[2,128,1024]{2,1,0:T(8,128)(2,1)S(1)} %fusion.7.refs_3_, ...), custom_call_target="tpu_custom_call" | custom-call | tf_op jit(solution)/shard_map/gate_up/pallas_call | solution.py:105
  91.8 9.5 %collective-permute-start.11 = (bf16[2,128,512]{2,1,0:T(8,128)(2,1)S(1)}, bf16[2,128,512]{2,1,0:T(8,128)(2,1)S(1)}, u32[]{:S(2)}, u32[]{:S(2)}) collective-permute-start(bf16[2,128,512]{2,1,0:T(8,128)(2,1)S(1)} %get-tuple-element.32), channel_id=1, source_target_pairs={{0,2},{6,4},{1,3},{7,5},{8,10},{14,12},{9,11},{15,13},{16,18},{22,... | collective-permute-start | bytes 786440 | tf_op jit(solution)/shard_map/ppermute | solution.py:212
  102.2 3.5 %down.9.refs_2_.refs_4_ = f32[128,2048]{1,0:T(8,128)S(1)} custom-call(s32[1]{0:T(128)} %bitcast.1.refs_3_.refs_0_, bf16[128,1536]{1,0:T(8,128)(2,1)S(1)} %fusion.4.refs_4_.refs_6_.refs_1_, bf16[2,128,1024]{2,1,0:T(8,128)(2,1)S(1)} %collective-permute-done.13.refs_2_, bf16[7168,2048]{1,0:T(8,128)(2,1)} %refs_3_.13, f32[128,2048]{1,0:T(8,128)S(1)} %down.8.refs_5_.refs_2_.refs_4_), custom_call_target="tpu_custom_call" | custom-call | tf_op jit(solution)/shard_map/down/pallas_call | solution.py:146
  108.2 3.5 %down.10.refs_2_.refs_4_ = f32[128,2048]{1,0:T(8,128)S(1)} custom-call(s32[1]{0:T(128)} %bitcast.1.refs_3_.refs_0_, bf16[128,1536]{1,0:T(8,128)(2,1)S(1)} %fusion.6.refs_4_.refs_1_, bf16[1,128,1536]{2,1,0:T(8,128)(2,1)S(1)} %bitcast.76, bf16[7168,2048]{1,0:T(8,128)(2,1)} %refs_3_.13, f32[128,2048]{1,0:T(8,128)S(1)} %down.9.refs_2_.refs_4_), custom_call_target="tpu_custom_call" | custom-call | tf_op jit(solution)/shard_map/down/pallas_call | solution.py:146
  114.9 5.1 %collective-permute-done.20 = bf16[128,1024]{1,0:T(8,128)(2,1)S(1)} collective-permute-done((bf16[128,1024]{1,0:T(8,128)(2,1)S(1)}, bf16[128,1024]{1,0:T(8,128)(2,1)S(1)}, u32[]{:S(2)}, u32[]{:S(2)}) %collective-permute-start.20) | collective-permute-done | bytes 262176 | tf_op jit(solution)/shard_map/ppermute | solution.py:229
  120.0 2.5 %down.11.refs_4_ = f32[128,2048]{1,0:T(8,128)S(1)} custom-call(s32[1]{0:T(128)} %bitcast.1.refs_3_.refs_0_, bf16[128,1024]{1,0:T(8,128)(2,1)S(1)} %fusion.14.refs_1_, bf16[1,128,1024]{2,1,0:T(8,128)(2,1)S(1)} %bitcast.77, bf16[7168,2048]{1,0:T(8,128)(2,1)} %refs_3_.13, f32[128,2048]{1,0:T(8,128)S(1)} %down.10.refs_2_.refs_4_), custom_call_target="tpu_custom_call" | custom-call | tf_op jit(solution)/shard_map/down/pallas_call | solution.py:146
  122.5 1.7 %collective-permute-done.19 = bf16[128,1024]{1,0:T(8,128)(2,1)S(1)} collective-permute-done((bf16[128,1024]{1,0:T(8,128)(2,1)S(1)}, bf16[128,1024]{1,0:T(8,128)(2,1)S(1)}, u32[]{:S(2)}, u32[]{:S(2)}) %collective-permute-start.19) | collective-permute-done | bytes 262176 | tf_op jit(solution)/shard_map/ppermute | solution.py:229
  124.3 2.5 %down.12.refs_4_ = f32[128,2048]{1,0:T(8,128)S(1)} custom-call(s32[1]{0:T(128)} %bitcast.1.refs_3_.refs_0_, bf16[128,1024]{1,0:T(8,128)(2,1)S(1)} %fusion.12.refs_1_, bf16[1,128,1024]{2,1,0:T(8,128)(2,1)S(1)} %bitcast.78, bf16[7168,2048]{1,0:T(8,128)(2,1)} %refs_3_.13, f32[128,2048]{1,0:T(8,128)S(1)} %down.11.refs_4_), custom_call_target="tpu_custom_call" | custom-call | tf_op jit(solution)/shard_map/down/pallas_call | solution.py:146
  126.8 1.9 %down.13 = f32[128,2048]{1,0:T(8,128)S(1)} custom-call(s32[1]{0:T(128)} %bitcast.1.refs_3_.refs_0_, bf16[128,512]{1,0:T(8,128)(2,1)S(1)} %fusion.19.refs_1_, bf16[1,128,512]{2,1,0:T(8,128)(2,1)S(1)} %bitcast.79, bf16[7168,2048]{1,0:T(8,128)(2,1)} %refs_3_.13, f32[128,2048]{1,0:T(8,128)S(1)} %down.12.refs_4_), custom_call_target="tpu_custom_call" | custom-call | tf_op jit(solution)/shard_map/down/pallas_call | solution.py:146
  128.9 1.9 %collective-permute-done.21 = f32[64,2048]{1,0:T(8,128)S(1)} collective-permute-done((f32[64,2048]{1,0:T(8,128)S(1)}, f32[64,2048]{1,0:T(8,128)S(1)}, u32[]{:S(2)}, u32[]{:S(2)}) %collective-permute-start.21) | collective-permute-done | bytes 524320 | tf_op jit(solution)/shard_map/ppermute | solution.py:256
  130.8 1.6 %collective-permute-start.22 = (bf16[32,2048]{1,0:T(8,128)(2,1)S(1)}, bf16[32,2048]{1,0:T(8,128)(2,1)S(1)}, u32[]{:S(2)}, u32[]{:S(2)}) collective-permute-start(bf16[32,2048]{1,0:T(8,128)(2,1)S(1)} %slice.154), channel_id=1, source_target_pairs={{0,16},{8,24},{16,0},{24,8},{1,17},{9,25},{17,1},{25,9},{2,18},{10... | collective-permute-start | bytes 393224 | tf_op jit(solution)/shard_map/ppermute | solution.py:256
  133.0 3.4 %collective-permute-done.22 = bf16[32,2048]{1,0:T(8,128)(2,1)S(1)} collective-permute-done((bf16[32,2048]{1,0:T(8,128)(2,1)S(1)}, bf16[32,2048]{1,0:T(8,128)(2,1)S(1)}, u32[]{:S(2)}, u32[]{:S(2)}) %collective-permute-start.22) | collective-permute-done | bytes 131104 | tf_op jit(solution)/shard_map/ppermute | solution.py:256
  (71 shorter events, 18.1 us)
Async XLA Ops:
  0.0 6.7 %collective-permute-start = (bf16[32,2048]{1,0:T(8,128)(2,1)}, bf16[32,2048]{1,0:T(8,128)(2,1)S(1)}, u32[]{:S(2)}, u32[]{:S(2)}) collective-permute-start(bf16[32,2048]{1,0:T(8,128)(2,1)} %refs_0_.1), channel_id=1, source_target_pairs={{0,16},{8,24},{16,0},{24,8},{1,17},{9,25},{17,1},{25,9},{2,18},{10... | collective-permute-start | bytes 393224 | tf_op jit(solution)/shard_map/ppermute | solution.py:192
  3.0 3.7 %collective-permute-start.1 = (bf16[32,2048]{1,0:T(8,128)(2,1)}, bf16[32,2048]{1,0:T(8,128)(2,1)S(1)}, u32[]{:S(2)}, u32[]{:S(2)}) collective-permute-start(bf16[32,2048]{1,0:T(8,128)(2,1)} %refs_0_.1), channel_id=1, source_target_pairs={{0,8},{8,0},{16,24},{24,16},{1,9},{9,1},{17,25},{25,17},{2,10},{10... | collective-permute-start | bytes 393224 | tf_op jit(solution)/shard_map/ppermute | solution.py:192
  6.7 1.3 collective-permute-start.2
  8.0 0.9 copy-start
  11.0 10.0 %collective-permute-start.5 = (bf16[2,128,256]{2,1,0:T(8,128)(2,1)S(1)}, bf16[2,128,256]{2,1,0:T(8,128)(2,1)S(1)}, u32[]{:S(2)}, u32[]{:S(2)}) collective-permute-start(bf16[2,128,256]{2,1,0:T(8,128)(2,1)S(1)} %get-tuple-element.24), channel_id=1, source_target_pairs={{0,2},{6,4},{1,3},{7,5},{8,10},{14,12},{9,11},{15,13},{16,18},{22,... | collective-permute-start | bytes 393224 | tf_op jit(solution)/shard_map/ppermute | solution.py:212
  19.6 16.4 %collective-permute-start.3 = (bf16[2,128,1280]{2,1,0:T(8,128)(2,1)S(1)}, bf16[2,128,1280]{2,1,0:T(8,128)(2,1)S(1)}, u32[]{:S(2)}, u32[]{:S(2)}) collective-permute-start(bf16[2,128,1280]{2,1,0:T(8,128)(2,1)S(1)} %get-tuple-element.22), channel_id=1, source_target_pairs={{0,2},{6,4},{1,3},{7,5},{8,10},{14,12},{9,11},{15,13},{16,18},{22,... | collective-permute-start | bytes 1966088 | tf_op jit(solution)/shard_map/ppermute | solution.py:212
  21.0 0.7 copy-start.1
  21.7 10.4 %collective-permute-start.8 = (bf16[2,128,256]{2,1,0:T(8,128)(2,1)S(1)}, bf16[2,128,256]{2,1,0:T(8,128)(2,1)}, u32[]{:S(2)}, u32[]{:S(2)}) collective-permute-start(bf16[2,128,256]{2,1,0:T(8,128)(2,1)S(1)} %fusion.20.refs_3_), channel_id=1, source_target_pairs={{2,4},{4,2},{3,5},{5,3},{10,12},{12,10},{11,13},{13,11},{18,20},{2... | collective-permute-start | bytes 393224 | tf_op jit(solution)/shard_map/ppermute | solution.py:219
  23.0 9.1 %copy-start.2 = (bf16[2,128,256]{2,1,0:T(8,128)(2,1)S(1)}, bf16[2,128,256]{2,1,0:T(8,128)(2,1)}, u32[]{:S(2)}) copy-start(bf16[2,128,256]{2,1,0:T(8,128)(2,1)} %copy-done.1) | copy-start | bytes 393220
  28.6 24.3 %collective-permute-start.6 = (bf16[2,128,1536]{2,1,0:T(8,128)(2,1)S(1)}, bf16[2,128,1536]{2,1,0:T(8,128)(2,1)S(1)}, u32[]{:S(2)}, u32[]{:S(2)}) collective-permute-start(bf16[2,128,1536]{2,1,0:T(8,128)(2,1)S(1)} %get-tuple-element.26), channel_id=1, source_target_pairs={{0,2},{6,4},{1,3},{7,5},{8,10},{14,12},{9,11},{15,13},{16,18},{22,... | collective-permute-start | bytes 2359304 | tf_op jit(solution)/shard_map/ppermute | solution.py:212
  36.1 17.7 %collective-permute-start.4 = (bf16[2,128,1280]{2,1,0:T(8,128)(2,1)S(1)}, bf16[2,128,1280]{2,1,0:T(8,128)(2,1)S(1)}, u32[]{:S(2)}, u32[]{:S(2)}) collective-permute-start(bf16[2,128,1280]{2,1,0:T(8,128)(2,1)S(1)} %fusion.2.refs_5_), channel_id=1, source_target_pairs={{2,4},{4,2},{3,5},{5,3},{10,12},{12,10},{11,13},{13,11},{18,20},{2... | collective-permute-start | bytes 1966088 | tf_op jit(solution)/shard_map/ppermute | solution.py:219
  43.6 26.1 %collective-permute-start.9 = (bf16[2,128,1536]{2,1,0:T(8,128)(2,1)S(1)}, bf16[2,128,1536]{2,1,0:T(8,128)(2,1)S(1)}, u32[]{:S(2)}, u32[]{:S(2)}) collective-permute-start(bf16[2,128,1536]{2,1,0:T(8,128)(2,1)S(1)} %get-tuple-element.30), channel_id=1, source_target_pairs={{0,2},{6,4},{2,0},{4,6},{1,3},{7,5},{3,1},{5,7},{8,10},{14,12},{10... | collective-permute-start | bytes 2359304 | tf_op jit(solution)/shard_map/ppermute | solution.py:212
  53.1 19.3 %collective-permute-start.12 = (bf16[2,128,1536]{2,1,0:T(8,128)(2,1)S(1)}, bf16[2,128,1536]{2,1,0:T(8,128)(2,1)S(1)}, u32[]{:S(2)}, u32[]{:S(2)}) collective-permute-start(bf16[2,128,1536]{2,1,0:T(8,128)(2,1)S(1)} %fusion.refs_5_), channel_id=1, source_target_pairs={{2,4},{4,2},{3,5},{5,3},{10,12},{12,10},{11,13},{13,11},{18,20},{2... | collective-permute-start | bytes 2359304 | tf_op jit(solution)/shard_map/ppermute | solution.py:219
  59.2 23.9 %collective-permute-start.7 = (bf16[2,128,1024]{2,1,0:T(8,128)(2,1)S(1)}, bf16[2,128,1024]{2,1,0:T(8,128)(2,1)S(1)}, u32[]{:S(2)}, u32[]{:S(2)}) collective-permute-start(bf16[2,128,1024]{2,1,0:T(8,128)(2,1)S(1)} %get-tuple-element.28), channel_id=1, source_target_pairs={{0,2},{6,4},{2,0},{4,6},{1,3},{7,5},{3,1},{5,7},{8,10},{14,12},{10... | collective-permute-start | bytes 1572872 | tf_op jit(solution)/shard_map/ppermute | solution.py:212
  69.9 17.3 %collective-permute-start.10 = (bf16[2,128,1536]{2,1,0:T(8,128)(2,1)S(1)}, bf16[2,128,1536]{2,1,0:T(8,128)(2,1)S(1)}, u32[]{:S(2)}, u32[]{:S(2)}) collective-permute-start(bf16[2,128,1536]{2,1,0:T(8,128)(2,1)S(1)} %fusion.1.refs_5_), channel_id=1, source_target_pairs={{2,4},{4,2},{3,5},{5,3},{10,12},{12,10},{11,13},{13,11},{18,20},{2... | collective-permute-start | bytes 2359304 | tf_op jit(solution)/shard_map/ppermute | solution.py:219
  77.9 23.4 %collective-permute-start.13 = (bf16[2,128,1024]{2,1,0:T(8,128)(2,1)S(1)}, bf16[2,128,1024]{2,1,0:T(8,128)(2,1)S(1)}, u32[]{:S(2)}, u32[]{:S(2)}) collective-permute-start(bf16[2,128,1024]{2,1,0:T(8,128)(2,1)S(1)} %get-tuple-element.34), channel_id=1, source_target_pairs={{0,2},{6,4},{2,0},{4,6},{1,3},{7,5},{3,1},{5,7},{8,10},{14,12},{10... | collective-permute-start | bytes 1572872 | tf_op jit(solution)/shard_map/ppermute | solution.py:212
  83.3 23.1 %collective-permute-start.16 = (bf16[2,128,1024]{2,1,0:T(8,128)(2,1)S(1)}, bf16[2,128,1024]{2,1,0:T(8,128)(2,1)S(1)}, u32[]{:S(2)}, u32[]{:S(2)}) collective-permute-start(bf16[2,128,1024]{2,1,0:T(8,128)(2,1)S(1)} %fusion.7.refs_3_), channel_id=1, source_target_pairs={{2,4},{4,2},{3,5},{5,3},{10,12},{12,10},{11,13},{13,11},{18,20},{2... | collective-permute-start | bytes 1572872 | tf_op jit(solution)/shard_map/ppermute | solution.py:219
  87.7 20.4 %collective-permute-start.17 = (bf16[128,1536]{1,0:T(8,128)(2,1)S(1)}, bf16[128,1536]{1,0:T(8,128)(2,1)S(1)}, u32[]{:S(2)}, u32[]{:S(2)}) collective-permute-start(bf16[128,1536]{1,0:T(8,128)(2,1)S(1)} %fusion.6.refs_4_.refs_1_), channel_id=1, source_target_pairs={{2,0},{4,6},{3,1},{5,7},{10,8},{12,14},{11,9},{13,15},{18,16},{20,... | collective-permute-start | bytes 1179656 | tf_op jit(solution)/shard_map/ppermute | solution.py:229
  91.8 13.8 %collective-permute-start.11 = (bf16[2,128,512]{2,1,0:T(8,128)(2,1)S(1)}, bf16[2,128,512]{2,1,0:T(8,128)(2,1)S(1)}, u32[]{:S(2)}, u32[]{:S(2)}) collective-permute-start(bf16[2,128,512]{2,1,0:T(8,128)(2,1)S(1)} %get-tuple-element.32), channel_id=1, source_target_pairs={{0,2},{6,4},{1,3},{7,5},{8,10},{14,12},{9,11},{15,13},{16,18},{22,... | collective-permute-start | bytes 786440 | tf_op jit(solution)/shard_map/ppermute | solution.py:212
  101.5 10.2 %collective-permute-start.15 = (bf16[2,128,1024]{2,1,0:T(8,128)(2,1)S(1)}, bf16[2,128,1024]{2,1,0:T(8,128)(2,1)S(1)}, u32[]{:S(2)}, u32[]{:S(2)}) collective-permute-start(bf16[2,128,1024]{2,1,0:T(8,128)(2,1)S(1)} %fusion.8.refs_1_), channel_id=1, source_target_pairs={{2,4},{4,2},{3,5},{5,3},{10,12},{12,10},{11,13},{13,11},{18,20},{2... | collective-permute-start | bytes 1572872 | tf_op jit(solution)/shard_map/ppermute | solution.py:219
  105.7 7.6 %collective-permute-start.14 = (bf16[2,128,512]{2,1,0:T(8,128)(2,1)S(1)}, bf16[2,128,512]{2,1,0:T(8,128)(2,1)S(1)}, u32[]{:S(2)}, u32[]{:S(2)}) collective-permute-start(bf16[2,128,512]{2,1,0:T(8,128)(2,1)S(1)} %fusion.15.refs_1_), channel_id=1, source_target_pairs={{2,4},{4,2},{3,5},{5,3},{10,12},{12,10},{11,13},{13,11},{18,20},{2... | collective-permute-start | bytes 786440 | tf_op jit(solution)/shard_map/ppermute | solution.py:219
  106.8 13.1 %collective-permute-start.20 = (bf16[128,1024]{1,0:T(8,128)(2,1)S(1)}, bf16[128,1024]{1,0:T(8,128)(2,1)S(1)}, u32[]{:S(2)}, u32[]{:S(2)}) collective-permute-start(bf16[128,1024]{1,0:T(8,128)(2,1)S(1)} %fusion.14.refs_1_), channel_id=1, source_target_pairs={{2,0},{4,6},{3,1},{5,7},{10,8},{12,14},{11,9},{13,15},{18,16},{20,... | collective-permute-start | bytes 786440 | tf_op jit(solution)/shard_map/ppermute | solution.py:229
  112.1 12.2 %collective-permute-start.19 = (bf16[128,1024]{1,0:T(8,128)(2,1)S(1)}, bf16[128,1024]{1,0:T(8,128)(2,1)S(1)}, u32[]{:S(2)}, u32[]{:S(2)}) collective-permute-start(bf16[128,1024]{1,0:T(8,128)(2,1)S(1)} %fusion.12.refs_1_), channel_id=1, source_target_pairs={{2,0},{4,6},{3,1},{5,7},{10,8},{12,14},{11,9},{13,15},{18,16},{20,... | collective-permute-start | bytes 786440 | tf_op jit(solution)/shard_map/ppermute | solution.py:229
  113.6 13.2 %collective-permute-start.18 = (bf16[128,512]{1,0:T(8,128)(2,1)S(1)}, bf16[128,512]{1,0:T(8,128)(2,1)S(1)}, u32[]{:S(2)}, u32[]{:S(2)}) collective-permute-start(bf16[128,512]{1,0:T(8,128)(2,1)S(1)} %fusion.19.refs_1_), channel_id=1, source_target_pairs={{2,0},{4,6},{3,1},{5,7},{10,8},{12,14},{11,9},{13,15},{18,16},{20,... | collective-permute-start | bytes 393224 | tf_op jit(solution)/shard_map/ppermute | solution.py:229
  128.7 3.7 %copy-start.3 = (s32[32,128]{1,0:T(8,128)S(1)}, s32[32,128]{1,0:T(8,128)}, u32[]{:S(2)}) copy-start(s32[32,128]{1,0:T(8,128)} %param.9) | copy-start | bytes 49156
  128.8 2.0 %collective-permute-start.21 = (f32[64,2048]{1,0:T(8,128)S(1)}, f32[64,2048]{1,0:T(8,128)S(1)}, u32[]{:S(2)}, u32[]{:S(2)}) collective-permute-start(f32[64,2048]{1,0:T(8,128)S(1)} %slice.88), channel_id=1, source_target_pairs={{0,8},{8,0},{16,24},{24,16},{1,9},{9,1},{17,25},{25,17},{2,10},{10... | collective-permute-start | bytes 1572872 | tf_op jit(solution)/shard_map/ppermute | solution.py:256
  130.8 5.6 %collective-permute-start.22 = (bf16[32,2048]{1,0:T(8,128)(2,1)S(1)}, bf16[32,2048]{1,0:T(8,128)(2,1)S(1)}, u32[]{:S(2)}, u32[]{:S(2)}) collective-permute-start(bf16[32,2048]{1,0:T(8,128)(2,1)S(1)} %slice.154), channel_id=1, source_target_pairs={{0,16},{8,24},{16,0},{24,8},{1,17},{9,25},{17,1},{25,9},{2,18},{10... | collective-permute-start | bytes 393224 | tf_op jit(solution)/shard_map/ppermute | solution.py:256

commit v4 on v3

--- a/solution.py
+++ b/solution.py
@@ -6,9 +6,9 @@
 from jax.sharding import PartitionSpec as P
 
 F32, BF16 = jnp.float32, jnp.bfloat16
-SHARES = (1, 5, 6, 6, 4, 4, 2)
+SHARES = (2, 5, 5, 5, 5, 4, 2)
 LAG = 3
-SLOTS = 4
+SLOTS = 6
 VMEM_LIMIT = 40 << 20
 
 
@@ -219,10 +219,10 @@
             crossed[c] = lax.ppermute(side[c], "fsdp", across)
 
         def finish(c):
-            if c >= count - 3:
-                wait = [side[count - 1]] if c == count - 3 else [kept[c - 1]]
-                wait += [total[c - 2]]
-                crossed[c] = hold(crossed[c], *wait)
+            if c == count - 3:
+                crossed[c] = hold(crossed[c], side[count - 2])
+            elif c > count - 3:
+                crossed[c] = hold(crossed[c], side[count - 1], kept[c - 1], total[-1])
             both = wide[c] + crossed[c].astype(F32)
             kept[c] = (jax.nn.silu(both[0]) * both[1]).astype(BF16)
             if c + LAG >= count or not carries(c + LAG):
@@ -231,21 +231,25 @@
         def project(c):
             total.append(add_down(inner, kept[c], given[c], down, total[-1], firsts[c], SHARES[c], tile))
 
-        for c in range(count + 1):
-            if c < count:
-                work_out(c)
-            if c == count:
-                heard[c - 1] = hold(heard[c - 1], side[c - 2])
+        for c in range(count):
+            work_out(c)
             if c >= 1:
                 add(c - 1)
-            if 2 <= c and c - 2 < count - 3:
+            if 2 <= c < count - 1:
                 finish(c - 2)
-            if 4 <= c and c - 4 < count - 5:
+            if 4 <= c < count - 1:
                 project(c - 4)
-        for c in range(count - 3, count):
-            while len(total) <= c - 2:
-                project(len(total) - 1)
-            finish(c)
+        finish(count - 3)
+        while len(total) <= count - 5:
+            project(len(total) - 1)
+        total[-1] = hold(total[-1], kept[count - 3])
+        heard[count - 1] = hold(heard[count - 1], side[count - 2], kept[count - 3])
+        add(count - 1)
+        while len(total) <= count - 3:
+            project(len(total) - 1)
+        total[-1] = hold(total[-1], side[count - 1])
+        finish(count - 2)
+        finish(count - 1)
         while len(total) <= count:
             project(len(total) - 1)
         total = total[-1]

time: 138 us -> 134 us (0.971)
  waiting for transfers between devices: 29.4 us -> 21.8 us
  starting transfers between devices: 49.2 us -> 52.5 us
  other arithmetic: 5.06 us -> 6.88 us
    ppermute x7, waiting for transfers between devices: 12.1 us -> 4.2 us  [work_out(): heard[c] = lax.ppermute(out[0], 'fsdp', outward + back if load else outward)]
    ppermute x7, starting transfers between devices: 33.9 us -> 37.2 us  [work_out(): heard[c] = lax.ppermute(out[0], 'fsdp', outward + back if load else outward)]
  transfers between devices with their start and end apart: 23 -> 23, of which waited for: 9 -> 9; matrix products, arithmetic and copies ran while one was open for 4% -> 5% of each run, Pallas kernels for 34% -> 34%
where the time goes in v4:
time: 134 us; the launch traced here: 133 us
  starting transfers between devices  52.5 us (39%)
  Pallas kernels  49.8 us (37%)
  waiting for transfers between devices  21.8 us (16%)
  other arithmetic  6.88 us (5%)
  local copies, waits for them, and re-layouts  1.61 us (1%)
    ppermute x7, starting transfers between devices, work_out(): heard[c] = lax.ppermute(out[0], 'fsdp', outward + back if load else outward)  37.2 us
    pallas_call x7, Pallas kernels, partial_sums(): pl.pallas_call(lambda *refs: up_kernel(first, count, tile, len(parts), bo...  32 us
    pallas_call x7, Pallas kernels, add_down(): pl.pallas_call(lambda *refs: down_kernel(first, count, tile, *refs), in_s...  17.8 us
    ppermute x4, waiting for transfers between devices, finish(): given[c] = lax.ppermute(kept[c], 'fsdp', back)[None]  7.19 us
    ppermute x7, starting transfers between devices, add(): crossed[c] = lax.ppermute(side[c], 'fsdp', across)  5.55 us
    ppermute x2, waiting for transfers between devices, shards(): lax.ppermute(away, 'tensor', swap(tensor, bit)).astype(F32)  5.34 us
    ppermute x4, starting transfers between devices, finish(): given[c] = lax.ppermute(kept[c], 'fsdp', back)[None]  5.17 us
    ppermute x3, waiting for transfers between devices, shards(): lax.ppermute(part, 'tensor', swap(tensor, bit))  5.05 us
  transfers between devices with their start and end apart: 23, of which 9 were waited for; matrix products, arithmetic and copies ran while one was open for 5% of the time, Pallas kernels for 34%

profile of v4, /device:TPU:0, one launch (start us, length us, event | category | flops | bytes accessed | tf_op | source)
XLA Modules:
  0.0 133.2 jit_solution(14117941404145062049)
XLA Ops:
  0.0 3.0 %collective-permute-start = (bf16[32,2048]{1,0:T(8,128)(2,1)}, bf16[32,2048]{1,0:T(8,128)(2,1)S(1)}, u32[]{:S(2)}, u32[]{:S(2)}) collective-permute-start(bf16[32,2048]{1,0:T(8,128)(2,1)} %refs_0_.1), channel_id=1, source_target_pairs={{0,16},{8,24},{16,0},{24,8},{1,17},{9,25},{17,1},{25,9},{2,18},{10... | collective-permute-start | bytes 393224 | tf_op jit(solution)/shard_map/ppermute | solution.py:192
  3.0 3.7 %collective-permute-done.refs_1_ = bf16[32,2048]{1,0:T(8,128)(2,1)S(1)} collective-permute-done((bf16[32,2048]{1,0:T(8,128)(2,1)}, bf16[32,2048]{1,0:T(8,128)(2,1)S(1)}, u32[]{:S(2)}, u32[]{:S(2)}) %collective-permute-start) | collective-permute-done | bytes 131104 | tf_op jit(solution)/shard_map/ppermute | solution.py:192
  6.7 1.3 %collective-permute-done.2.refs_3_ = bf16[32,2048]{1,0:T(8,128)(2,1)S(1)} collective-permute-done((bf16[32,2048]{1,0:T(8,128)(2,1)S(1)}, bf16[32,2048]{1,0:T(8,128)(2,1)S(1)}, u32[]{:S(2)}, u32[]{:S(2)}) %collective-permute-start.2) | collective-permute-done | bytes 131104 | tf_op jit(solution)/shard_map/ppermute | solution.py:192
  8.9 2.8 %gate_up.7 = (bf16[2,128,512]{2,1,0:T(8,128)(2,1)S(1)}, f32[2,128,512]{2,1,0:T(8,128)S(1)}, bf16[128,2048]{1,0:T(8,128)(2,1)S(1)}) custom-call(bf16[32,2048]{1,0:T(8,128)(2,1)S(1)} %copy-done, bf16[32,2048]{1,0:T(8,128)(2,1)S(1)} %collective-permute-done.refs_1_, bf16[32,2048]{1,0:T(8,128)(2,1)S(1)} %collective-permute-done.1.refs_2_, ...), custom_call_target="tpu_custom_call" | custom-call | tf_op jit(solution)/shard_map/gate_up/pallas_call | solution.py:105
  11.7 3.7 %collective-permute-start.5 = (bf16[2,128,512]{2,1,0:T(8,128)(2,1)S(1)}, bf16[2,128,512]{2,1,0:T(8,128)(2,1)S(1)}, u32[]{:S(2)}, u32[]{:S(2)}) collective-permute-start(bf16[2,128,512]{2,1,0:T(8,128)(2,1)S(1)} %get-tuple-element.24), channel_id=1, source_target_pairs={{0,2},{6,4},{1,3},{7,5},{8,10},{14,12},{9,11},{15,13},{16,18},{22,... | collective-permute-start | bytes 786440 | tf_op jit(solution)/shard_map/ppermute | solution.py:212
  15.4 4.7 %gate_up.8 = (bf16[2,128,1280]{2,1,0:T(8,128)(2,1)S(1)}, f32[2,128,1280]{2,1,0:T(8,128)S(1)}) custom-call(bf16[128,2048]{1,0:T(8,128)(2,1)S(1)} %get-tuple-element.20.refs_0_, bf16[2048,7168]{1,0:T(8,128)(2,1)} %refs_1_.11, bf16[2048,7168]{1,0:T(8,128)(2,1)} %refs_2_.11), custom_call_target="tpu_custom_call" | custom-call | tf_op jit(solution)/shard_map/gate_up/pallas_call | solution.py:105
  20.2 2.1 %collective-permute-start.3 = (bf16[2,128,1280]{2,1,0:T(8,128)(2,1)S(1)}, bf16[2,128,1280]{2,1,0:T(8,128)(2,1)}, u32[]{:S(2)}, u32[]{:S(2)}) collective-permute-start(bf16[2,128,1280]{2,1,0:T(8,128)(2,1)S(1)} %get-tuple-element.22), channel_id=1, source_target_pairs={{0,2},{6,4},{1,3},{7,5},{8,10},{14,12},{9,11},{15,13},{16,18},{22,... | collective-permute-start | bytes 1966088 | tf_op jit(solution)/shard_map/ppermute | solution.py:212
  22.4 1.4 %collective-permute-start.8 = (bf16[2,128,512]{2,1,0:T(8,128)(2,1)S(1)}, bf16[2,128,512]{2,1,0:T(8,128)(2,1)}, u32[]{:S(2)}, u32[]{:S(2)}) collective-permute-start(bf16[2,128,512]{2,1,0:T(8,128)(2,1)S(1)} %fusion.15.refs_3_), channel_id=1, source_target_pairs={{2,4},{4,2},{3,5},{5,3},{10,12},{12,10},{11,13},{13,11},{18,20},{2... | collective-permute-start | bytes 786440 | tf_op jit(solution)/shard_map/ppermute | solution.py:219
  23.7 4.7 %gate_up.9 = (bf16[2,128,1280]{2,1,0:T(8,128)(2,1)S(1)}, f32[2,128,1280]{2,1,0:T(8,128)S(1)}) custom-call(bf16[128,2048]{1,0:T(8,128)(2,1)S(1)} %get-tuple-element.20.refs_0_, bf16[2048,7168]{1,0:T(8,128)(2,1)} %refs_1_.11, bf16[2048,7168]{1,0:T(8,128)(2,1)} %refs_2_.11, bf16[2,128,512]{2,1,0:T(8,128)(2,1)S(1)} %fusion.15.refs_3_), custom_call_target="tpu_custom_call" | custom-call | tf_op jit(solution)/shard_map/gate_up/pallas_call | solution.py:105
  28.4 5.6 %collective-permute-start.6 = (bf16[2,128,1280]{2,1,0:T(8,128)(2,1)S(1)}, bf16[2,128,1280]{2,1,0:T(8,128)(2,1)S(1)}, u32[]{:S(2)}, u32[]{:S(2)}) collective-permute-start(bf16[2,128,1280]{2,1,0:T(8,128)(2,1)S(1)} %get-tuple-element.26), channel_id=1, source_target_pairs={{0,2},{6,4},{1,3},{7,5},{8,10},{14,12},{9,11},{15,13},{16,18},{22,... | collective-permute-start | bytes 1966088 | tf_op jit(solution)/shard_map/ppermute | solution.py:212
  35.1 1.5 %collective-permute-done.3 = bf16[2,128,1280]{2,1,0:T(8,128)(2,1)} collective-permute-done((bf16[2,128,1280]{2,1,0:T(8,128)(2,1)S(1)}, bf16[2,128,1280]{2,1,0:T(8,128)(2,1)}, u32[]{:S(2)}, u32[]{:S(2)}) %collective-permute-start.3) | collective-permute-done | bytes 655392 | tf_op jit(solution)/shard_map/ppermute | solution.py:212
  38.5 6.0 %gate_up.11 = (bf16[2,128,1280]{2,1,0:T(8,128)(2,1)S(1)}, f32[2,128,1280]{2,1,0:T(8,128)S(1)}) custom-call(bf16[128,2048]{1,0:T(8,128)(2,1)S(1)} %get-tuple-element.20.refs_0_, bf16[2048,7168]{1,0:T(8,128)(2,1)} %refs_1_.11, bf16[2048,7168]{1,0:T(8,128)(2,1)} %refs_2_.11, s32[1]{0:T(128)} %bitcast.1.refs_3_.refs_0_, ...), custom_call_target="tpu_custom_call" | custom-call | tf_op jit(solution)/shard_map/gate_up/pallas_call | solution.py:105
  44.5 5.4 %collective-permute-start.9 = (bf16[2,128,1280]{2,1,0:T(8,128)(2,1)S(1)}, bf16[2,128,1280]{2,1,0:T(8,128)(2,1)S(1)}, u32[]{:S(2)}, u32[]{:S(2)}) collective-permute-start(bf16[2,128,1280]{2,1,0:T(8,128)(2,1)S(1)} %get-tuple-element.30), channel_id=1, source_target_pairs={{0,2},{6,4},{2,0},{4,6},{1,3},{7,5},{3,1},{5,7},{8,10},{14,12},{10... | collective-permute-start | bytes 1966088 | tf_op jit(solution)/shard_map/ppermute | solution.py:212
  52.9 5.9 %gate_up.10 = (bf16[2,128,1280]{2,1,0:T(8,128)(2,1)S(1)}, f32[2,128,1280]{2,1,0:T(8,128)S(1)}) custom-call(bf16[128,2048]{1,0:T(8,128)(2,1)S(1)} %get-tuple-element.20.refs_0_, bf16[2048,7168]{1,0:T(8,128)(2,1)} %refs_1_.11, bf16[2048,7168]{1,0:T(8,128)(2,1)} %refs_2_.11, s32[1]{0:T(128)} %bitcast.1.refs_3_.refs_0_, ...), custom_call_target="tpu_custom_call" | custom-call | tf_op jit(solution)/shard_map/gate_up/pallas_call | solution.py:105
  58.8 7.1 %collective-permute-start.7 = (bf16[2,128,1280]{2,1,0:T(8,128)(2,1)S(1)}, bf16[2,128,1280]{2,1,0:T(8,128)(2,1)S(1)}, u32[]{:S(2)}, u32[]{:S(2)}) collective-permute-start(bf16[2,128,1280]{2,1,0:T(8,128)(2,1)S(1)} %get-tuple-element.28), channel_id=1, source_target_pairs={{0,2},{6,4},{2,0},{4,6},{1,3},{7,5},{3,1},{5,7},{8,10},{14,12},{10... | collective-permute-start | bytes 1966088 | tf_op jit(solution)/shard_map/ppermute | solution.py:212
  66.9 1.9 %down.7.refs_4_.refs_7_ = f32[128,2048]{1,0:T(8,128)S(1)} custom-call(s32[1]{0:T(128)} %bitcast.1.refs_3_.refs_0_, bf16[128,512]{1,0:T(8,128)(2,1)S(1)} %fusion.22.refs_4_.refs_6_.refs_1_, bf16[2,128,1280]{2,1,0:T(8,128)(2,1)S(1)} %collective-permute-done.9.refs_2_, bf16[7168,2048]{1,0:T(8,128)(2,1)} %refs_3_.13, f32[128,2048]{1,0:T(8,128)S(1)} %broadcast_in_dim.17.refs_4_), custom_call_target="tpu_custom_call" | custom-call | tf_op jit(solution)/shard_map/down/pallas_call | solution.py:146
  69.2 5.1 %gate_up.13 = (bf16[2,128,1024]{2,1,0:T(8,128)(2,1)S(1)}, f32[2,128,1024]{2,1,0:T(8,128)S(1)}) custom-call(bf16[128,2048]{1,0:T(8,128)(2,1)S(1)} %get-tuple-element.20.refs_0_, bf16[2048,7168]{1,0:T(8,128)(2,1)} %refs_1_.11, bf16[2048,7168]{1,0:T(8,128)(2,1)} %refs_2_.11, s32[1]{0:T(128)} %bitcast.1.refs_3_.refs_0_, ...), custom_call_target="tpu_custom_call" | custom-call | tf_op jit(solution)/shard_map/gate_up/pallas_call | solution.py:105
  74.3 4.0 %collective-permute-start.13 = (bf16[2,128,1024]{2,1,0:T(8,128)(2,1)S(1)}, bf16[2,128,1024]{2,1,0:T(8,128)(2,1)S(1)}, u32[]{:S(2)}, u32[]{:S(2)}) collective-permute-start(bf16[2,128,1024]{2,1,0:T(8,128)(2,1)S(1)} %get-tuple-element.34), channel_id=1, source_target_pairs={{0,2},{6,4},{2,0},{4,6},{1,3},{7,5},{3,1},{5,7},{8,10},{14,12},{10... | collective-permute-start | bytes 1572872 | tf_op jit(solution)/shard_map/ppermute | solution.py:212
  80.3 1.3 collective-permute-start.17
  81.6 2.9 %down.8.refs_5_.refs_0_ = f32[128,2048]{1,0:T(8,128)S(1)} custom-call(s32[1]{0:T(128)} %bitcast.1.refs_3_.refs_0_, bf16[128,1280]{1,0:T(8,128)(2,1)S(1)} %fusion.12.refs_4_.refs_6_.refs_1_, bf16[2,128,1280]{2,1,0:T(8,128)(2,1)S(1)} %collective-permute-done.7.refs_2_, bf16[7168,2048]{1,0:T(8,128)(2,1)} %refs_3_.13, f32[128,2048]{1,0:T(8,128)S(1)} %down.7.refs_4_.refs_7_), custom_call_target="tpu_custom_call" | custom-call | tf_op jit(solution)/shard_map/down/pallas_call | solution.py:146
  84.5 2.8 %gate_up.12 = (bf16[2,128,512]{2,1,0:T(8,128)(2,1)S(1)}, f32[2,128,512]{2,1,0:T(8,128)S(1)}) custom-call(bf16[128,2048]{1,0:T(8,128)(2,1)S(1)} %get-tuple-element.20.refs_0_, bf16[2048,7168]{1,0:T(8,128)(2,1)} %refs_1_.11, bf16[2048,7168]{1,0:T(8,128)(2,1)} %refs_2_.11, bf16[2,128,1280]{2,1,0:T(8,128)(2,1)S(1)} %fusion.2.refs_3_, ...), custom_call_target="tpu_custom_call" | custom-call | tf_op jit(solution)/shard_map/gate_up/pallas_call | solution.py:105
  87.3 9.3 %collective-permute-start.11 = (bf16[2,128,512]{2,1,0:T(8,128)(2,1)S(1)}, bf16[2,128,512]{2,1,0:T(8,128)(2,1)S(1)}, u32[]{:S(2)}, u32[]{:S(2)}) collective-permute-start(bf16[2,128,512]{2,1,0:T(8,128)(2,1)S(1)} %get-tuple-element.32), channel_id=1, source_target_pairs={{0,2},{6,4},{1,3},{7,5},{8,10},{14,12},{9,11},{15,13},{16,18},{22,... | collective-permute-start | bytes 786440 | tf_op jit(solution)/shard_map/ppermute | solution.py:212
  101.2 2.9 %down.9.refs_4_ = f32[128,2048]{1,0:T(8,128)S(1)} custom-call(s32[1]{0:T(128)} %bitcast.1.refs_3_.refs_0_, bf16[128,1280]{1,0:T(8,128)(2,1)S(1)} %fusion.8.refs_4_.refs_6_.refs_1_, bf16[2,128,1024]{2,1,0:T(8,128)(2,1)S(1)} %collective-permute-done.13.refs_2_, bf16[7168,2048]{1,0:T(8,128)(2,1)} %refs_3_.13, f32[128,2048]{1,0:T(8,128)S(1)} %hold.8.refs_4_), custom_call_target="tpu_custom_call" | custom-call | tf_op jit(solution)/shard_map/down/pallas_call | solution.py:146
  104.0 2.9 %down.10.refs_0_ = f32[128,2048]{1,0:T(8,128)S(1)} custom-call(s32[1]{0:T(128)} %bitcast.1.refs_3_.refs_0_, bf16[128,1280]{1,0:T(8,128)(2,1)S(1)} %fusion.10.refs_4_.refs_1_, bf16[1,128,1280]{2,1,0:T(8,128)(2,1)S(1)} %bitcast.77, bf16[7168,2048]{1,0:T(8,128)(2,1)} %refs_3_.13, f32[128,2048]{1,0:T(8,128)S(1)} %down.9.refs_4_), custom_call_target="tpu_custom_call" | custom-call | tf_op jit(solution)/shard_map/down/pallas_call | solution.py:146
  107.4 1.3 collective-permute-start.19
  110.2 2.9 %down.11.refs_4_ = f32[128,2048]{1,0:T(8,128)S(1)} custom-call(s32[1]{0:T(128)} %bitcast.1.refs_3_.refs_0_, bf16[128,1280]{1,0:T(8,128)(2,1)S(1)} %fusion.6.refs_2_.refs_1_, bf16[1,128,1280]{2,1,0:T(8,128)(2,1)S(1)} %bitcast.76, bf16[7168,2048]{1,0:T(8,128)(2,1)} %refs_3_.13, f32[128,2048]{1,0:T(8,128)S(1)} %hold.9.refs_3_.refs_4_), custom_call_target="tpu_custom_call" | custom-call | tf_op jit(solution)/shard_map/down/pallas_call | solution.py:146
  113.1 7.2 %collective-permute-done.19 = bf16[128,1024]{1,0:T(8,128)(2,1)S(1)} collective-permute-done((bf16[128,1024]{1,0:T(8,128)(2,1)S(1)}, bf16[128,1024]{1,0:T(8,128)(2,1)S(1)}, u32[]{:S(2)}, u32[]{:S(2)}) %collective-permute-start.19) | collective-permute-done | bytes 262176 | tf_op jit(solution)/shard_map/ppermute | solution.py:229
  120.3 2.5 %down.12.refs_4_ = f32[128,2048]{1,0:T(8,128)S(1)} custom-call(s32[1]{0:T(128)} %bitcast.1.refs_3_.refs_0_, bf16[128,1024]{1,0:T(8,128)(2,1)S(1)} %fusion.14.refs_2_.refs_1_, bf16[1,128,1024]{2,1,0:T(8,128)(2,1)S(1)} %bitcast.78, bf16[7168,2048]{1,0:T(8,128)(2,1)} %refs_3_.13, f32[128,2048]{1,0:T(8,128)S(1)} %down.11.refs_4_), custom_call_target="tpu_custom_call" | custom-call | tf_op jit(solution)/shard_map/down/pallas_call | solution.py:146
  122.8 1.9 %down.13 = f32[128,2048]{1,0:T(8,128)S(1)} custom-call(s32[1]{0:T(128)} %bitcast.1.refs_3_.refs_0_, bf16[128,512]{1,0:T(8,128)(2,1)S(1)} %fusion.20.refs_1_, bf16[1,128,512]{2,1,0:T(8,128)(2,1)S(1)} %bitcast.79, bf16[7168,2048]{1,0:T(8,128)(2,1)} %refs_3_.13, f32[128,2048]{1,0:T(8,128)S(1)} %down.12.refs_4_), custom_call_target="tpu_custom_call" | custom-call | tf_op jit(solution)/shard_map/down/pallas_call | solution.py:146
  124.9 1.9 %collective-permute-done.21 = f32[64,2048]{1,0:T(8,128)S(1)} collective-permute-done((f32[64,2048]{1,0:T(8,128)S(1)}, f32[64,2048]{1,0:T(8,128)S(1)}, u32[]{:S(2)}, u32[]{:S(2)}) %collective-permute-start.21) | collective-permute-done | bytes 524320 | tf_op jit(solution)/shard_map/ppermute | solution.py:260
  126.9 1.6 %collective-permute-start.22 = (bf16[32,2048]{1,0:T(8,128)(2,1)S(1)}, bf16[32,2048]{1,0:T(8,128)(2,1)S(1)}, u32[]{:S(2)}, u32[]{:S(2)}) collective-permute-start(bf16[32,2048]{1,0:T(8,128)(2,1)S(1)} %slice.154), channel_id=1, source_target_pairs={{0,16},{8,24},{16,0},{24,8},{1,17},{9,25},{17,1},{25,9},{2,18},{10... | collective-permute-start | bytes 393224 | tf_op jit(solution)/shard_map/ppermute | solution.py:260
  129.0 3.4 %collective-permute-done.22 = bf16[32,2048]{1,0:T(8,128)(2,1)S(1)} collective-permute-done((bf16[32,2048]{1,0:T(8,128)(2,1)S(1)}, bf16[32,2048]{1,0:T(8,128)(2,1)S(1)}, u32[]{:S(2)}, u32[]{:S(2)}) %collective-permute-start.22) | collective-permute-done | bytes 131104 | tf_op jit(solution)/shard_map/ppermute | solution.py:260
  (69 shorter events, 18.1 us)
Async XLA Ops:
  0.0 6.7 %collective-permute-start = (bf16[32,2048]{1,0:T(8,128)(2,1)}, bf16[32,2048]{1,0:T(8,128)(2,1)S(1)}, u32[]{:S(2)}, u32[]{:S(2)}) collective-permute-start(bf16[32,2048]{1,0:T(8,128)(2,1)} %refs_0_.1), channel_id=1, source_target_pairs={{0,16},{8,24},{16,0},{24,8},{1,17},{9,25},{17,1},{25,9},{2,18},{10... | collective-permute-start | bytes 393224 | tf_op jit(solution)/shard_map/ppermute | solution.py:192
  3.0 3.7 %collective-permute-start.1 = (bf16[32,2048]{1,0:T(8,128)(2,1)}, bf16[32,2048]{1,0:T(8,128)(2,1)S(1)}, u32[]{:S(2)}, u32[]{:S(2)}) collective-permute-start(bf16[32,2048]{1,0:T(8,128)(2,1)} %refs_0_.1), channel_id=1, source_target_pairs={{0,8},{8,0},{16,24},{24,16},{1,9},{9,1},{17,25},{25,17},{2,10},{10... | collective-permute-start | bytes 393224 | tf_op jit(solution)/shard_map/ppermute | solution.py:192
  6.7 1.3 %collective-permute-start.2 = (bf16[32,2048]{1,0:T(8,128)(2,1)S(1)}, bf16[32,2048]{1,0:T(8,128)(2,1)S(1)}, u32[]{:S(2)}, u32[]{:S(2)}) collective-permute-start(bf16[32,2048]{1,0:T(8,128)(2,1)S(1)} %collective-permute-done.refs_1_), channel_id=1, source_target_pairs={{0,8},{8,0},{16,24},{24,16},{1,9},{9,1},{17,25},{25,17},{2,10},{10... | collective-permute-start | bytes 393224 | tf_op jit(solution)/shard_map/ppermute | solution.py:192
  8.0 0.9 copy-start
  11.7 10.6 %collective-permute-start.5 = (bf16[2,128,512]{2,1,0:T(8,128)(2,1)S(1)}, bf16[2,128,512]{2,1,0:T(8,128)(2,1)S(1)}, u32[]{:S(2)}, u32[]{:S(2)}) collective-permute-start(bf16[2,128,512]{2,1,0:T(8,128)(2,1)S(1)} %get-tuple-element.24), channel_id=1, source_target_pairs={{0,2},{6,4},{1,3},{7,5},{8,10},{14,12},{9,11},{15,13},{16,18},{22,... | collective-permute-start | bytes 786440 | tf_op jit(solution)/shard_map/ppermute | solution.py:212
  20.2 16.4 %collective-permute-start.3 = (bf16[2,128,1280]{2,1,0:T(8,128)(2,1)S(1)}, bf16[2,128,1280]{2,1,0:T(8,128)(2,1)}, u32[]{:S(2)}, u32[]{:S(2)}) collective-permute-start(bf16[2,128,1280]{2,1,0:T(8,128)(2,1)S(1)} %get-tuple-element.22), channel_id=1, source_target_pairs={{0,2},{6,4},{1,3},{7,5},{8,10},{14,12},{9,11},{15,13},{16,18},{22,... | collective-permute-start | bytes 1966088 | tf_op jit(solution)/shard_map/ppermute | solution.py:212
  22.4 11.7 %collective-permute-start.8 = (bf16[2,128,512]{2,1,0:T(8,128)(2,1)S(1)}, bf16[2,128,512]{2,1,0:T(8,128)(2,1)}, u32[]{:S(2)}, u32[]{:S(2)}) collective-permute-start(bf16[2,128,512]{2,1,0:T(8,128)(2,1)S(1)} %fusion.15.refs_3_), channel_id=1, source_target_pairs={{2,4},{4,2},{3,5},{5,3},{10,12},{12,10},{11,13},{13,11},{18,20},{2... | collective-permute-start | bytes 786440 | tf_op jit(solution)/shard_map/ppermute | solution.py:219
  28.4 22.1 %collective-permute-start.6 = (bf16[2,128,1280]{2,1,0:T(8,128)(2,1)S(1)}, bf16[2,128,1280]{2,1,0:T(8,128)(2,1)S(1)}, u32[]{:S(2)}, u32[]{:S(2)}) collective-permute-start(bf16[2,128,1280]{2,1,0:T(8,128)(2,1)S(1)} %get-tuple-element.26), channel_id=1, source_target_pairs={{0,2},{6,4},{1,3},{7,5},{8,10},{14,12},{9,11},{15,13},{16,18},{22,... | collective-permute-start | bytes 1966088 | tf_op jit(solution)/shard_map/ppermute | solution.py:212
  37.7 13.7 %collective-permute-start.4 = (bf16[2,128,1280]{2,1,0:T(8,128)(2,1)S(1)}, bf16[2,128,1280]{2,1,0:T(8,128)(2,1)S(1)}, u32[]{:S(2)}, u32[]{:S(2)}) collective-permute-start(bf16[2,128,1280]{2,1,0:T(8,128)(2,1)S(1)} %fusion.refs_5_), channel_id=1, source_target_pairs={{2,4},{4,2},{3,5},{5,3},{10,12},{12,10},{11,13},{13,11},{18,20},{2... | collective-permute-start | bytes 1966088 | tf_op jit(solution)/shard_map/ppermute | solution.py:219
  44.5 21.5 %collective-permute-start.9 = (bf16[2,128,1280]{2,1,0:T(8,128)(2,1)S(1)}, bf16[2,128,1280]{2,1,0:T(8,128)(2,1)S(1)}, u32[]{:S(2)}, u32[]{:S(2)}) collective-permute-start(bf16[2,128,1280]{2,1,0:T(8,128)(2,1)S(1)} %get-tuple-element.30), channel_id=1, source_target_pairs={{0,2},{6,4},{2,0},{4,6},{1,3},{7,5},{3,1},{5,7},{8,10},{14,12},{10... | collective-permute-start | bytes 1966088 | tf_op jit(solution)/shard_map/ppermute | solution.py:212
  50.7 18.1 %collective-permute-start.12 = (bf16[2,128,1280]{2,1,0:T(8,128)(2,1)S(1)}, bf16[2,128,1280]{2,1,0:T(8,128)(2,1)S(1)}, u32[]{:S(2)}, u32[]{:S(2)}) collective-permute-start(bf16[2,128,1280]{2,1,0:T(8,128)(2,1)S(1)} %fusion.1.refs_5_), channel_id=1, source_target_pairs={{2,4},{4,2},{3,5},{5,3},{10,12},{12,10},{11,13},{13,11},{18,20},{2... | collective-permute-start | bytes 1966088 | tf_op jit(solution)/shard_map/ppermute | solution.py:219
  58.8 20.2 %collective-permute-start.7 = (bf16[2,128,1280]{2,1,0:T(8,128)(2,1)S(1)}, bf16[2,128,1280]{2,1,0:T(8,128)(2,1)S(1)}, u32[]{:S(2)}, u32[]{:S(2)}) collective-permute-start(bf16[2,128,1280]{2,1,0:T(8,128)(2,1)S(1)} %get-tuple-element.28), channel_id=1, source_target_pairs={{0,2},{6,4},{2,0},{4,6},{1,3},{7,5},{3,1},{5,7},{8,10},{14,12},{10... | collective-permute-start | bytes 1966088 | tf_op jit(solution)/shard_map/ppermute | solution.py:212
  66.1 13.8 %collective-permute-start.10 = (bf16[2,128,1280]{2,1,0:T(8,128)(2,1)S(1)}, bf16[2,128,1280]{2,1,0:T(8,128)(2,1)S(1)}, u32[]{:S(2)}, u32[]{:S(2)}) collective-permute-start(bf16[2,128,1280]{2,1,0:T(8,128)(2,1)S(1)} %fusion.3.refs_5_), channel_id=1, source_target_pairs={{2,4},{4,2},{3,5},{5,3},{10,12},{12,10},{11,13},{13,11},{18,20},{2... | collective-permute-start | bytes 1966088 | tf_op jit(solution)/shard_map/ppermute | solution.py:219
  74.3 22.2 %collective-permute-start.13 = (bf16[2,128,1024]{2,1,0:T(8,128)(2,1)S(1)}, bf16[2,128,1024]{2,1,0:T(8,128)(2,1)S(1)}, u32[]{:S(2)}, u32[]{:S(2)}) collective-permute-start(bf16[2,128,1024]{2,1,0:T(8,128)(2,1)S(1)} %get-tuple-element.34), channel_id=1, source_target_pairs={{0,2},{6,4},{2,0},{4,6},{1,3},{7,5},{3,1},{5,7},{8,10},{14,12},{10... | collective-permute-start | bytes 1572872 | tf_op jit(solution)/shard_map/ppermute | solution.py:212
  79.2 18.2 %collective-permute-start.14 = (bf16[2,128,1280]{2,1,0:T(8,128)(2,1)S(1)}, bf16[2,128,1280]{2,1,0:T(8,128)(2,1)S(1)}, u32[]{:S(2)}, u32[]{:S(2)}) collective-permute-start(bf16[2,128,1280]{2,1,0:T(8,128)(2,1)S(1)} %fusion.2.refs_3_), channel_id=1, source_target_pairs={{2,4},{4,2},{3,5},{5,3},{10,12},{12,10},{11,13},{13,11},{18,20},{2... | collective-permute-start | bytes 1966088 | tf_op jit(solution)/shard_map/ppermute | solution.py:219
  80.3 23.8 %collective-permute-start.17 = (bf16[128,1280]{1,0:T(8,128)(2,1)S(1)}, bf16[128,1280]{1,0:T(8,128)(2,1)S(1)}, u32[]{:S(2)}, u32[]{:S(2)}) collective-permute-start(bf16[128,1280]{1,0:T(8,128)(2,1)S(1)} %fusion.10.refs_4_.refs_1_), channel_id=1, source_target_pairs={{2,0},{4,6},{3,1},{5,7},{10,8},{12,14},{11,9},{13,15},{18,16},{20,... | collective-permute-start | bytes 983048 | tf_op jit(solution)/shard_map/ppermute | solution.py:229
  87.3 13.1 %collective-permute-start.11 = (bf16[2,128,512]{2,1,0:T(8,128)(2,1)S(1)}, bf16[2,128,512]{2,1,0:T(8,128)(2,1)S(1)}, u32[]{:S(2)}, u32[]{:S(2)}) collective-permute-start(bf16[2,128,512]{2,1,0:T(8,128)(2,1)S(1)} %get-tuple-element.32), channel_id=1, source_target_pairs={{0,2},{6,4},{1,3},{7,5},{8,10},{14,12},{9,11},{15,13},{16,18},{22,... | collective-permute-start | bytes 786440 | tf_op jit(solution)/shard_map/ppermute | solution.py:212
  96.7 10.2 %collective-permute-start.16 = (bf16[2,128,1024]{2,1,0:T(8,128)(2,1)S(1)}, bf16[2,128,1024]{2,1,0:T(8,128)(2,1)S(1)}, u32[]{:S(2)}, u32[]{:S(2)}) collective-permute-start(bf16[2,128,1024]{2,1,0:T(8,128)(2,1)S(1)} %fusion.4.refs_1_), channel_id=1, source_target_pairs={{2,4},{4,2},{3,5},{5,3},{10,12},{12,10},{11,13},{13,11},{18,20},{2... | collective-permute-start | bytes 1572872 | tf_op jit(solution)/shard_map/ppermute | solution.py:219
  97.8 12.3 %collective-permute-start.20 = (bf16[128,1280]{1,0:T(8,128)(2,1)S(1)}, bf16[128,1280]{1,0:T(8,128)(2,1)S(1)}, u32[]{:S(2)}, u32[]{:S(2)}) collective-permute-start(bf16[128,1280]{1,0:T(8,128)(2,1)S(1)} %fusion.6.refs_2_.refs_1_), channel_id=1, source_target_pairs={{2,0},{4,6},{3,1},{5,7},{10,8},{12,14},{11,9},{13,15},{18,16},{20,... | collective-permute-start | bytes 983048 | tf_op jit(solution)/shard_map/ppermute | solution.py:229
  100.5 8.2 %collective-permute-start.15 = (bf16[2,128,512]{2,1,0:T(8,128)(2,1)S(1)}, bf16[2,128,512]{2,1,0:T(8,128)(2,1)S(1)}, u32[]{:S(2)}, u32[]{:S(2)}) collective-permute-start(bf16[2,128,512]{2,1,0:T(8,128)(2,1)S(1)} %fusion.16.refs_1_), channel_id=1, source_target_pairs={{2,4},{4,2},{3,5},{5,3},{10,12},{12,10},{11,13},{13,11},{18,20},{2... | collective-permute-start | bytes 786440 | tf_op jit(solution)/shard_map/ppermute | solution.py:219
  107.4 12.9 %collective-permute-start.19 = (bf16[128,1024]{1,0:T(8,128)(2,1)S(1)}, bf16[128,1024]{1,0:T(8,128)(2,1)S(1)}, u32[]{:S(2)}, u32[]{:S(2)}) collective-permute-start(bf16[128,1024]{1,0:T(8,128)(2,1)S(1)} %fusion.14.refs_2_.refs_1_), channel_id=1, source_target_pairs={{2,0},{4,6},{3,1},{5,7},{10,8},{12,14},{11,9},{13,15},{18,16},{20,... | collective-permute-start | bytes 786440 | tf_op jit(solution)/shard_map/ppermute | solution.py:229
  108.9 13.9 %collective-permute-start.18 = (bf16[128,512]{1,0:T(8,128)(2,1)S(1)}, bf16[128,512]{1,0:T(8,128)(2,1)S(1)}, u32[]{:S(2)}, u32[]{:S(2)}) collective-permute-start(bf16[128,512]{1,0:T(8,128)(2,1)S(1)} %fusion.20.refs_1_), channel_id=1, source_target_pairs={{2,0},{4,6},{3,1},{5,7},{10,8},{12,14},{11,9},{13,15},{18,16},{20,... | collective-permute-start | bytes 393224 | tf_op jit(solution)/shard_map/ppermute | solution.py:229
  124.7 3.7 %copy-start.1 = (s32[32,128]{1,0:T(8,128)S(1)}, s32[32,128]{1,0:T(8,128)}, u32[]{:S(2)}) copy-start(s32[32,128]{1,0:T(8,128)} %param.9) | copy-start | bytes 49156
  124.8 2.0 %collective-permute-start.21 = (f32[64,2048]{1,0:T(8,128)S(1)}, f32[64,2048]{1,0:T(8,128)S(1)}, u32[]{:S(2)}, u32[]{:S(2)}) collective-permute-start(f32[64,2048]{1,0:T(8,128)S(1)} %slice.88), channel_id=1, source_target_pairs={{0,8},{8,0},{16,24},{24,16},{1,9},{9,1},{17,25},{25,17},{2,10},{10... | collective-permute-start | bytes 1572872 | tf_op jit(solution)/shard_map/ppermute | solution.py:260
  126.9 5.6 %collective-permute-start.22 = (bf16[32,2048]{1,0:T(8,128)(2,1)S(1)}, bf16[32,2048]{1,0:T(8,128)(2,1)S(1)}, u32[]{:S(2)}, u32[]{:S(2)}) collective-permute-start(bf16[32,2048]{1,0:T(8,128)(2,1)S(1)} %slice.154), channel_id=1, source_target_pairs={{0,16},{8,24},{16,0},{24,8},{1,17},{9,25},{17,1},{25,9},{2,18},{10... | collective-permute-start | bytes 393224 | tf_op jit(solution)/shard_map/ppermute | solution.py:260

commit v5 on v4

--- a/solution.py
+++ b/solution.py
@@ -6,7 +6,7 @@
 from jax.sharding import PartitionSpec as P
 
 F32, BF16 = jnp.float32, jnp.bfloat16
-SHARES = (2, 5, 5, 5, 5, 4, 2)
+SHARES = (2, 5, 5, 5, 5, 3, 3)
 LAG = 3
 SLOTS = 6
 VMEM_LIMIT = 40 << 20

time: 134 us -> 136 us (1.015)
  waiting for transfers between devices: 21.8 us -> 28.3 us
  starting transfers between devices: 52.5 us -> 48 us
    ppermute x4 -> x3, waiting for transfers between devices: 7.19 us -> 12.1 us  [finish(): given[c] = lax.ppermute(kept[c], 'fsdp', back)[None]]
    ppermute x7, starting transfers between devices: 37.2 us -> 34 us  [work_out(): heard[c] = lax.ppermute(out[0], 'fsdp', outward + back if load else outward)]
    ppermute x7, waiting for transfers between devices: 4.2 us -> 5.74 us  [work_out(): heard[c] = lax.ppermute(out[0], 'fsdp', outward + back if load else outward)]
    ppermute x4 -> x3, starting transfers between devices: 5.17 us -> 3.88 us  [finish(): given[c] = lax.ppermute(kept[c], 'fsdp', back)[None]]
  transfers between devices with their start and end apart: 23 -> 22, of which waited for: 9 -> 11; matrix products, arithmetic and copies ran while one was open for 5% -> 5% of each run, Pallas kernels for 34% -> 34%
where the time goes in v5:
time: 136 us
  Pallas kernels  50.5 us (37%)
  starting transfers between devices  48 us (35%)
  waiting for transfers between devices  28.3 us (21%)
  other arithmetic  6.77 us (5%)
  local copies, waits for them, and re-layouts  1.61 us (1%)
    ppermute x7, starting transfers between devices, work_out(): heard[c] = lax.ppermute(out[0], 'fsdp', outward + back if load else outward)  34 us
    pallas_call x7, Pallas kernels, partial_sums(): pl.pallas_call(lambda *refs: up_kernel(first, count, tile, len(parts), bo...  32.6 us
    pallas_call x7, Pallas kernels, add_down(): pl.pallas_call(lambda *refs: down_kernel(first, count, tile, *refs), in_s...  17.9 us
    ppermute x3, waiting for transfers between devices, finish(): given[c] = lax.ppermute(kept[c], 'fsdp', back)[None]  12.1 us
    ppermute x7, waiting for transfers between devices, work_out(): heard[c] = lax.ppermute(out[0], 'fsdp', outward + back if load else outward)  5.74 us
    ppermute x7, starting transfers between devices, add(): crossed[c] = lax.ppermute(side[c], 'fsdp', across)  5.56 us
    ppermute x2, waiting for transfers between devices, shards(): lax.ppermute(away, 'tensor', swap(tensor, bit)).astype(F32)  5.36 us
    ppermute x3, waiting for transfers between devices, shards(): lax.ppermute(part, 'tensor', swap(tensor, bit))  5.05 us
  transfers between devices with their start and end apart: 22, of which 11 were waited for; matrix products, arithmetic and copies ran while one was open for 5% of the time, Pallas kernels for 34%

profile of v5, /device:TPU:0, one launch (start us, length us, event | category | flops | bytes accessed | tf_op | source)
XLA Modules:
  0.0 135.6 jit_solution(10588815286273936765)
XLA Ops:
  0.0 3.0 %collective-permute-start = (bf16[32,2048]{1,0:T(8,128)(2,1)}, bf16[32,2048]{1,0:T(8,128)(2,1)S(1)}, u32[]{:S(2)}, u32[]{:S(2)}) collective-permute-start(bf16[32,2048]{1,0:T(8,128)(2,1)} %refs_0_.1), channel_id=1, source_target_pairs={{0,16},{8,24},{16,0},{24,8},{1,17},{9,25},{17,1},{25,9},{2,18},{10... | collective-permute-start | bytes 393224 | tf_op jit(solution)/shard_map/ppermute | solution.py:192
  3.0 3.7 %collective-permute-done.refs_1_ = bf16[32,2048]{1,0:T(8,128)(2,1)S(1)} collective-permute-done((bf16[32,2048]{1,0:T(8,128)(2,1)}, bf16[32,2048]{1,0:T(8,128)(2,1)S(1)}, u32[]{:S(2)}, u32[]{:S(2)}) %collective-permute-start) | collective-permute-done | bytes 131104 | tf_op jit(solution)/shard_map/ppermute | solution.py:192
  8.9 2.8 %gate_up.7 = (bf16[2,128,512]{2,1,0:T(8,128)(2,1)S(1)}, f32[2,128,512]{2,1,0:T(8,128)S(1)}, bf16[128,2048]{1,0:T(8,128)(2,1)S(1)}) custom-call(bf16[32,2048]{1,0:T(8,128)(2,1)S(1)} %copy-done, bf16[32,2048]{1,0:T(8,128)(2,1)S(1)} %collective-permute-done.refs_1_, bf16[32,2048]{1,0:T(8,128)(2,1)S(1)} %collective-permute-done.1.refs_2_, ...), custom_call_target="tpu_custom_call" | custom-call | tf_op jit(solution)/shard_map/gate_up/pallas_call | solution.py:105
  11.7 3.7 %collective-permute-start.3 = (bf16[2,128,512]{2,1,0:T(8,128)(2,1)S(1)}, bf16[2,128,512]{2,1,0:T(8,128)(2,1)S(1)}, u32[]{:S(2)}, u32[]{:S(2)}) collective-permute-start(bf16[2,128,512]{2,1,0:T(8,128)(2,1)S(1)} %get-tuple-element.22), channel_id=1, source_target_pairs={{0,2},{6,4},{1,3},{7,5},{8,10},{14,12},{9,11},{15,13},{16,18},{22,... | collective-permute-start | bytes 786440 | tf_op jit(solution)/shard_map/ppermute | solution.py:212
  15.4 4.7 %gate_up.8 = (bf16[2,128,1280]{2,1,0:T(8,128)(2,1)S(1)}, f32[2,128,1280]{2,1,0:T(8,128)S(1)}) custom-call(bf16[128,2048]{1,0:T(8,128)(2,1)S(1)} %get-tuple-element.20.refs_0_, bf16[2048,7168]{1,0:T(8,128)(2,1)} %refs_1_.11, bf16[2048,7168]{1,0:T(8,128)(2,1)} %refs_2_.11), custom_call_target="tpu_custom_call" | custom-call | tf_op jit(solution)/shard_map/gate_up/pallas_call | solution.py:105
  20.2 2.1 %collective-permute-start.5 = (bf16[2,128,1280]{2,1,0:T(8,128)(2,1)S(1)}, bf16[2,128,1280]{2,1,0:T(8,128)(2,1)}, u32[]{:S(2)}, u32[]{:S(2)}) collective-permute-start(bf16[2,128,1280]{2,1,0:T(8,128)(2,1)S(1)} %get-tuple-element.24), channel_id=1, source_target_pairs={{0,2},{6,4},{1,3},{7,5},{8,10},{14,12},{9,11},{15,13},{16,18},{22,... | collective-permute-start | bytes 1966088 | tf_op jit(solution)/shard_map/ppermute | solution.py:212
  22.4 1.4 %collective-permute-start.4 = (bf16[2,128,512]{2,1,0:T(8,128)(2,1)S(1)}, bf16[2,128,512]{2,1,0:T(8,128)(2,1)}, u32[]{:S(2)}, u32[]{:S(2)}) collective-permute-start(bf16[2,128,512]{2,1,0:T(8,128)(2,1)S(1)} %fusion.18.refs_3_), channel_id=1, source_target_pairs={{2,4},{4,2},{3,5},{5,3},{10,12},{12,10},{11,13},{13,11},{18,20},{2... | collective-permute-start | bytes 786440 | tf_op jit(solution)/shard_map/ppermute | solution.py:219
  23.8 4.7 %gate_up.10 = (bf16[2,128,1280]{2,1,0:T(8,128)(2,1)S(1)}, f32[2,128,1280]{2,1,0:T(8,128)S(1)}) custom-call(bf16[128,2048]{1,0:T(8,128)(2,1)S(1)} %get-tuple-element.20.refs_0_, bf16[2048,7168]{1,0:T(8,128)(2,1)} %refs_1_.11, bf16[2048,7168]{1,0:T(8,128)(2,1)} %refs_2_.11, bf16[2,128,512]{2,1,0:T(8,128)(2,1)S(1)} %fusion.18.refs_3_), custom_call_target="tpu_custom_call" | custom-call | tf_op jit(solution)/shard_map/gate_up/pallas_call | solution.py:105
  28.5 5.5 %collective-permute-start.9 = (bf16[2,128,1280]{2,1,0:T(8,128)(2,1)S(1)}, bf16[2,128,1280]{2,1,0:T(8,128)(2,1)S(1)}, u32[]{:S(2)}, u32[]{:S(2)}) collective-permute-start(bf16[2,128,1280]{2,1,0:T(8,128)(2,1)S(1)} %get-tuple-element.28), channel_id=1, source_target_pairs={{0,2},{6,4},{1,3},{7,5},{8,10},{14,12},{9,11},{15,13},{16,18},{22,... | collective-permute-start | bytes 1966088 | tf_op jit(solution)/shard_map/ppermute | solution.py:212
  35.1 1.5 %collective-permute-done.5 = bf16[2,128,1280]{2,1,0:T(8,128)(2,1)} collective-permute-done((bf16[2,128,1280]{2,1,0:T(8,128)(2,1)S(1)}, bf16[2,128,1280]{2,1,0:T(8,128)(2,1)}, u32[]{:S(2)}, u32[]{:S(2)}) %collective-permute-start.5) | collective-permute-done | bytes 655392 | tf_op jit(solution)/shard_map/ppermute | solution.py:212
  38.5 6.0 %gate_up.9 = (bf16[2,128,1280]{2,1,0:T(8,128)(2,1)S(1)}, f32[2,128,1280]{2,1,0:T(8,128)S(1)}) custom-call(bf16[128,2048]{1,0:T(8,128)(2,1)S(1)} %get-tuple-element.20.refs_0_, bf16[2048,7168]{1,0:T(8,128)(2,1)} %refs_1_.11, bf16[2048,7168]{1,0:T(8,128)(2,1)} %refs_2_.11, s32[1]{0:T(128)} %bitcast.1.refs_3_.refs_0_, ...), custom_call_target="tpu_custom_call" | custom-call | tf_op jit(solution)/shard_map/gate_up/pallas_call | solution.py:105
  44.5 5.4 %collective-permute-start.6 = (bf16[2,128,1280]{2,1,0:T(8,128)(2,1)S(1)}, bf16[2,128,1280]{2,1,0:T(8,128)(2,1)S(1)}, u32[]{:S(2)}, u32[]{:S(2)}) collective-permute-start(bf16[2,128,1280]{2,1,0:T(8,128)(2,1)S(1)} %get-tuple-element.26), channel_id=1, source_target_pairs={{0,2},{6,4},{2,0},{4,6},{1,3},{7,5},{3,1},{5,7},{8,10},{14,12},{10... | collective-permute-start | bytes 1966088 | tf_op jit(solution)/shard_map/ppermute | solution.py:212
  52.9 5.9 %gate_up.11 = (bf16[2,128,1280]{2,1,0:T(8,128)(2,1)S(1)}, f32[2,128,1280]{2,1,0:T(8,128)S(1)}) custom-call(bf16[128,2048]{1,0:T(8,128)(2,1)S(1)} %get-tuple-element.20.refs_0_, bf16[2048,7168]{1,0:T(8,128)(2,1)} %refs_1_.11, bf16[2048,7168]{1,0:T(8,128)(2,1)} %refs_2_.11, s32[1]{0:T(128)} %bitcast.1.refs_3_.refs_0_, ...), custom_call_target="tpu_custom_call" | custom-call | tf_op jit(solution)/shard_map/gate_up/pallas_call | solution.py:105
  58.9 7.1 %collective-permute-start.10 = (bf16[2,128,1280]{2,1,0:T(8,128)(2,1)S(1)}, bf16[2,128,1280]{2,1,0:T(8,128)(2,1)S(1)}, u32[]{:S(2)}, u32[]{:S(2)}) collective-permute-start(bf16[2,128,1280]{2,1,0:T(8,128)(2,1)S(1)} %get-tuple-element.30), channel_id=1, source_target_pairs={{0,2},{6,4},{2,0},{4,6},{1,3},{7,5},{3,1},{5,7},{8,10},{14,12},{10... | collective-permute-start | bytes 1966088 | tf_op jit(solution)/shard_map/ppermute | solution.py:212
  66.9 1.9 %down.7.refs_4_.refs_7_ = f32[128,2048]{1,0:T(8,128)S(1)} custom-call(s32[1]{0:T(128)} %bitcast.1.refs_3_.refs_0_, bf16[128,512]{1,0:T(8,128)(2,1)S(1)} %fusion.22.refs_4_.refs_6_.refs_1_, bf16[2,128,1280]{2,1,0:T(8,128)(2,1)S(1)} %collective-permute-done.6.refs_2_, bf16[7168,2048]{1,0:T(8,128)(2,1)} %refs_3_.13, f32[128,2048]{1,0:T(8,128)S(1)} %broadcast_in_dim.14.refs_4_), custom_call_target="tpu_custom_call" | custom-call | tf_op jit(solution)/shard_map/down/pallas_call | solution.py:146
  69.2 4.2 %gate_up.13 = (bf16[2,128,768]{2,1,0:T(8,128)(2,1)S(1)}, f32[2,128,768]{2,1,0:T(8,128)S(1)}) custom-call(bf16[128,2048]{1,0:T(8,128)(2,1)S(1)} %get-tuple-element.20.refs_0_, bf16[2048,7168]{1,0:T(8,128)(2,1)} %refs_1_.11, bf16[2048,7168]{1,0:T(8,128)(2,1)} %refs_2_.11, s32[1]{0:T(128)} %bitcast.1.refs_3_.refs_0_, ...), custom_call_target="tpu_custom_call" | custom-call | tf_op jit(solution)/shard_map/gate_up/pallas_call | solution.py:105
  73.5 3.9 %collective-permute-start.13 = (bf16[2,128,768]{2,1,0:T(8,128)(2,1)S(1)}, bf16[2,128,768]{2,1,0:T(8,128)(2,1)S(1)}, u32[]{:S(2)}, u32[]{:S(2)}) collective-permute-start(bf16[2,128,768]{2,1,0:T(8,128)(2,1)S(1)} %get-tuple-element.34), channel_id=1, source_target_pairs={{0,2},{6,4},{2,0},{4,6},{1,3},{7,5},{3,1},{5,7},{8,10},{14,12},{10... | collective-permute-start | bytes 1179656 | tf_op jit(solution)/shard_map/ppermute | solution.py:212
  77.4 2.5 %collective-permute-done.10.refs_2_ = bf16[2,128,1280]{2,1,0:T(8,128)(2,1)S(1)} collective-permute-done((bf16[2,128,1280]{2,1,0:T(8,128)(2,1)S(1)}, bf16[2,128,1280]{2,1,0:T(8,128)(2,1)S(1)}, u32[]{:S(2)}, u32[]{:S(2)}) %collective-permute-start.10) | collective-permute-done | bytes 655392 | tf_op jit(solution)/shard_map/ppermute | solution.py:212
  80.7 2.9 %down.8.refs_7_.refs_0_ = f32[128,2048]{1,0:T(8,128)S(1)} custom-call(s32[1]{0:T(128)} %bitcast.1.refs_3_.refs_0_, bf16[128,1280]{1,0:T(8,128)(2,1)S(1)} %fusion.9.refs_4_.refs_6_.refs_1_, bf16[2,128,1280]{2,1,0:T(8,128)(2,1)S(1)} %collective-permute-done.10.refs_2_, bf16[7168,2048]{1,0:T(8,128)(2,1)} %refs_3_.13, f32[128,2048]{1,0:T(8,128)S(1)} %down.7.refs_4_.refs_7_), custom_call_target="tpu_custom_call" | custom-call | tf_op jit(solution)/shard_map/down/pallas_call | solution.py:146
  84.0 4.2 %gate_up.12 = (bf16[2,128,768]{2,1,0:T(8,128)(2,1)S(1)}, f32[2,128,768]{2,1,0:T(8,128)S(1)}) custom-call(bf16[128,2048]{1,0:T(8,128)(2,1)S(1)} %get-tuple-element.20.refs_0_, bf16[2048,7168]{1,0:T(8,128)(2,1)} %refs_1_.11, bf16[2048,7168]{1,0:T(8,128)(2,1)} %refs_2_.11, s32[1]{0:T(128)} %bitcast.1.refs_3_.refs_0_, ...), custom_call_target="tpu_custom_call" | custom-call | tf_op jit(solution)/shard_map/gate_up/pallas_call | solution.py:105
  88.2 6.1 %collective-permute-start.11 = (bf16[2,128,768]{2,1,0:T(8,128)(2,1)S(1)}, bf16[2,128,768]{2,1,0:T(8,128)(2,1)S(1)}, u32[]{:S(2)}, u32[]{:S(2)}) collective-permute-start(bf16[2,128,768]{2,1,0:T(8,128)(2,1)S(1)} %get-tuple-element.32), channel_id=1, source_target_pairs={{0,2},{6,4},{2,0},{4,6},{1,3},{7,5},{3,1},{5,7},{8,10},{14,12},{10... | collective-permute-start | bytes 1179656 | tf_op jit(solution)/shard_map/ppermute | solution.py:212
  96.9 2.9 %down.9.refs_4_ = f32[128,2048]{1,0:T(8,128)S(1)} custom-call(s32[1]{0:T(128)} %bitcast.1.refs_3_.refs_0_, bf16[128,1280]{1,0:T(8,128)(2,1)S(1)} %fusion.7.refs_4_.refs_6_.refs_1_, bf16[2,128,768]{2,1,0:T(8,128)(2,1)S(1)} %collective-permute-done.13.refs_2_, bf16[7168,2048]{1,0:T(8,128)(2,1)} %refs_3_.13, f32[128,2048]{1,0:T(8,128)S(1)} %hold.8.refs_4_), custom_call_target="tpu_custom_call" | custom-call | tf_op jit(solution)/shard_map/down/pallas_call | solution.py:146
  100.9 2.9 %down.10.refs_0_ = f32[128,2048]{1,0:T(8,128)S(1)} custom-call(s32[1]{0:T(128)} %bitcast.1.refs_3_.refs_0_, bf16[128,1280]{1,0:T(8,128)(2,1)S(1)} %fusion.11.refs_4_.refs_6_.refs_1_, bf16[2,128,768]{2,1,0:T(8,128)(2,1)S(1)} %collective-permute-done.11.refs_0_.refs_2_, bf16[7168,2048]{1,0:T(8,128)(2,1)} %refs_3_.13, f32[128,2048]{1,0:T(8,128)S(1)} %down.9.refs_4_), custom_call_target="tpu_custom_call" | custom-call | tf_op jit(solution)/shard_map/down/pallas_call | solution.py:146
  107.7 1.5 %collective-permute-done.19 = bf16[128,1280]{1,0:T(8,128)(2,1)S(1)} collective-permute-done((bf16[128,1280]{1,0:T(8,128)(2,1)S(1)}, bf16[128,1280]{1,0:T(8,128)(2,1)S(1)}, u32[]{:S(2)}, u32[]{:S(2)}) %collective-permute-start.19) | collective-permute-done | bytes 327712 | tf_op jit(solution)/shard_map/ppermute | solution.py:229
  109.2 2.9 %down.11.refs_4_ = f32[128,2048]{1,0:T(8,128)S(1)} custom-call(s32[1]{0:T(128)} %bitcast.1.refs_3_.refs_0_, bf16[128,1280]{1,0:T(8,128)(2,1)S(1)} %fusion.5.refs_2_.refs_1_, bf16[1,128,1280]{2,1,0:T(8,128)(2,1)S(1)} %bitcast.75, bf16[7168,2048]{1,0:T(8,128)(2,1)} %refs_3_.13, f32[128,2048]{1,0:T(8,128)S(1)} %hold.9.refs_3_.refs_4_), custom_call_target="tpu_custom_call" | custom-call | tf_op jit(solution)/shard_map/down/pallas_call | solution.py:146
  112.1 7.4 %collective-permute-done.18 = bf16[128,768]{1,0:T(8,128)(2,1)S(1)} collective-permute-done((bf16[128,768]{1,0:T(8,128)(2,1)S(1)}, bf16[128,768]{1,0:T(8,128)(2,1)S(1)}, u32[]{:S(2)}, u32[]{:S(2)}) %collective-permute-start.18) | collective-permute-done | bytes 196640 | tf_op jit(solution)/shard_map/ppermute | solution.py:229
  119.4 2.2 %down.12.refs_4_ = f32[128,2048]{1,0:T(8,128)S(1)} custom-call(s32[1]{0:T(128)} %bitcast.1.refs_3_.refs_0_, bf16[128,768]{1,0:T(8,128)(2,1)S(1)} %fusion.17.refs_2_.refs_1_, bf16[1,128,768]{2,1,0:T(8,128)(2,1)S(1)} %bitcast.76, bf16[7168,2048]{1,0:T(8,128)(2,1)} %refs_3_.13, f32[128,2048]{1,0:T(8,128)S(1)} %down.11.refs_4_), custom_call_target="tpu_custom_call" | custom-call | tf_op jit(solution)/shard_map/down/pallas_call | solution.py:146
  121.7 3.2 %collective-permute-done.17 = bf16[128,768]{1,0:T(8,128)(2,1)S(1)} collective-permute-done((bf16[128,768]{1,0:T(8,128)(2,1)S(1)}, bf16[128,768]{1,0:T(8,128)(2,1)S(1)}, u32[]{:S(2)}, u32[]{:S(2)}) %collective-permute-start.17) | collective-permute-done | bytes 196640 | tf_op jit(solution)/shard_map/ppermute | solution.py:229
  124.9 2.2 %down.13 = f32[128,2048]{1,0:T(8,128)S(1)} custom-call(s32[1]{0:T(128)} %bitcast.1.refs_3_.refs_0_, bf16[128,768]{1,0:T(8,128)(2,1)S(1)} %fusion.15.refs_1_, bf16[1,128,768]{2,1,0:T(8,128)(2,1)S(1)} %bitcast.77, bf16[7168,2048]{1,0:T(8,128)(2,1)} %refs_3_.13, f32[128,2048]{1,0:T(8,128)S(1)} %down.12.refs_4_), custom_call_target="tpu_custom_call" | custom-call | tf_op jit(solution)/shard_map/down/pallas_call | solution.py:146
  127.3 1.9 %collective-permute-done.20 = f32[64,2048]{1,0:T(8,128)S(1)} collective-permute-done((f32[64,2048]{1,0:T(8,128)S(1)}, f32[64,2048]{1,0:T(8,128)S(1)}, u32[]{:S(2)}, u32[]{:S(2)}) %collective-permute-start.20) | collective-permute-done | bytes 524320 | tf_op jit(solution)/shard_map/ppermute | solution.py:260
  129.3 1.6 %collective-permute-start.21 = (bf16[32,2048]{1,0:T(8,128)(2,1)S(1)}, bf16[32,2048]{1,0:T(8,128)(2,1)S(1)}, u32[]{:S(2)}, u32[]{:S(2)}) collective-permute-start(bf16[32,2048]{1,0:T(8,128)(2,1)S(1)} %slice.154), channel_id=1, source_target_pairs={{0,16},{8,24},{16,0},{24,8},{1,17},{9,25},{17,1},{25,9},{2,18},{10... | collective-permute-start | bytes 393224 | tf_op jit(solution)/shard_map/ppermute | solution.py:260
  131.4 3.5 %collective-permute-done.21 = bf16[32,2048]{1,0:T(8,128)(2,1)S(1)} collective-permute-done((bf16[32,2048]{1,0:T(8,128)(2,1)S(1)}, bf16[32,2048]{1,0:T(8,128)(2,1)S(1)}, u32[]{:S(2)}, u32[]{:S(2)}) %collective-permute-start.21) | collective-permute-done | bytes 131104 | tf_op jit(solution)/shard_map/ppermute | solution.py:260
  (67 shorter events, 19.7 us)
Async XLA Ops:
  0.0 6.7 %collective-permute-start = (bf16[32,2048]{1,0:T(8,128)(2,1)}, bf16[32,2048]{1,0:T(8,128)(2,1)S(1)}, u32[]{:S(2)}, u32[]{:S(2)}) collective-permute-start(bf16[32,2048]{1,0:T(8,128)(2,1)} %refs_0_.1), channel_id=1, source_target_pairs={{0,16},{8,24},{16,0},{24,8},{1,17},{9,25},{17,1},{25,9},{2,18},{10... | collective-permute-start | bytes 393224 | tf_op jit(solution)/shard_map/ppermute | solution.py:192
  3.0 3.7 %collective-permute-start.1 = (bf16[32,2048]{1,0:T(8,128)(2,1)}, bf16[32,2048]{1,0:T(8,128)(2,1)S(1)}, u32[]{:S(2)}, u32[]{:S(2)}) collective-permute-start(bf16[32,2048]{1,0:T(8,128)(2,1)} %refs_0_.1), channel_id=1, source_target_pairs={{0,8},{8,0},{16,24},{24,16},{1,9},{9,1},{17,25},{25,17},{2,10},{10... | collective-permute-start | bytes 393224 | tf_op jit(solution)/shard_map/ppermute | solution.py:192
  6.7 1.3 collective-permute-start.2
  8.0 0.9 copy-start
  11.7 10.6 %collective-permute-start.3 = (bf16[2,128,512]{2,1,0:T(8,128)(2,1)S(1)}, bf16[2,128,512]{2,1,0:T(8,128)(2,1)S(1)}, u32[]{:S(2)}, u32[]{:S(2)}) collective-permute-start(bf16[2,128,512]{2,1,0:T(8,128)(2,1)S(1)} %get-tuple-element.22), channel_id=1, source_target_pairs={{0,2},{6,4},{1,3},{7,5},{8,10},{14,12},{9,11},{15,13},{16,18},{22,... | collective-permute-start | bytes 786440 | tf_op jit(solution)/shard_map/ppermute | solution.py:212
  20.2 16.4 %collective-permute-start.5 = (bf16[2,128,1280]{2,1,0:T(8,128)(2,1)S(1)}, bf16[2,128,1280]{2,1,0:T(8,128)(2,1)}, u32[]{:S(2)}, u32[]{:S(2)}) collective-permute-start(bf16[2,128,1280]{2,1,0:T(8,128)(2,1)S(1)} %get-tuple-element.24), channel_id=1, source_target_pairs={{0,2},{6,4},{1,3},{7,5},{8,10},{14,12},{9,11},{15,13},{16,18},{22,... | collective-permute-start | bytes 1966088 | tf_op jit(solution)/shard_map/ppermute | solution.py:212
  22.4 11.6 %collective-permute-start.4 = (bf16[2,128,512]{2,1,0:T(8,128)(2,1)S(1)}, bf16[2,128,512]{2,1,0:T(8,128)(2,1)}, u32[]{:S(2)}, u32[]{:S(2)}) collective-permute-start(bf16[2,128,512]{2,1,0:T(8,128)(2,1)S(1)} %fusion.18.refs_3_), channel_id=1, source_target_pairs={{2,4},{4,2},{3,5},{5,3},{10,12},{12,10},{11,13},{13,11},{18,20},{2... | collective-permute-start | bytes 786440 | tf_op jit(solution)/shard_map/ppermute | solution.py:219
  28.5 22.1 %collective-permute-start.9 = (bf16[2,128,1280]{2,1,0:T(8,128)(2,1)S(1)}, bf16[2,128,1280]{2,1,0:T(8,128)(2,1)S(1)}, u32[]{:S(2)}, u32[]{:S(2)}) collective-permute-start(bf16[2,128,1280]{2,1,0:T(8,128)(2,1)S(1)} %get-tuple-element.28), channel_id=1, source_target_pairs={{0,2},{6,4},{1,3},{7,5},{8,10},{14,12},{9,11},{15,13},{16,18},{22,... | collective-permute-start | bytes 1966088 | tf_op jit(solution)/shard_map/ppermute | solution.py:212
  37.7 13.7 %collective-permute-start.8 = (bf16[2,128,1280]{2,1,0:T(8,128)(2,1)S(1)}, bf16[2,128,1280]{2,1,0:T(8,128)(2,1)S(1)}, u32[]{:S(2)}, u32[]{:S(2)}) collective-permute-start(bf16[2,128,1280]{2,1,0:T(8,128)(2,1)S(1)} %fusion.refs_5_), channel_id=1, source_target_pairs={{2,4},{4,2},{3,5},{5,3},{10,12},{12,10},{11,13},{13,11},{18,20},{2... | collective-permute-start | bytes 1966088 | tf_op jit(solution)/shard_map/ppermute | solution.py:219
  44.5 21.5 %collective-permute-start.6 = (bf16[2,128,1280]{2,1,0:T(8,128)(2,1)S(1)}, bf16[2,128,1280]{2,1,0:T(8,128)(2,1)S(1)}, u32[]{:S(2)}, u32[]{:S(2)}) collective-permute-start(bf16[2,128,1280]{2,1,0:T(8,128)(2,1)S(1)} %get-tuple-element.26), channel_id=1, source_target_pairs={{0,2},{6,4},{2,0},{4,6},{1,3},{7,5},{3,1},{5,7},{8,10},{14,12},{10... | collective-permute-start | bytes 1966088 | tf_op jit(solution)/shard_map/ppermute | solution.py:212
  50.7 18.2 %collective-permute-start.12 = (bf16[2,128,1280]{2,1,0:T(8,128)(2,1)S(1)}, bf16[2,128,1280]{2,1,0:T(8,128)(2,1)S(1)}, u32[]{:S(2)}, u32[]{:S(2)}) collective-permute-start(bf16[2,128,1280]{2,1,0:T(8,128)(2,1)S(1)} %fusion.2.refs_5_), channel_id=1, source_target_pairs={{2,4},{4,2},{3,5},{5,3},{10,12},{12,10},{11,13},{13,11},{18,20},{2... | collective-permute-start | bytes 1966088 | tf_op jit(solution)/shard_map/ppermute | solution.py:219
  58.9 21.0 %collective-permute-start.10 = (bf16[2,128,1280]{2,1,0:T(8,128)(2,1)S(1)}, bf16[2,128,1280]{2,1,0:T(8,128)(2,1)S(1)}, u32[]{:S(2)}, u32[]{:S(2)}) collective-permute-start(bf16[2,128,1280]{2,1,0:T(8,128)(2,1)S(1)} %get-tuple-element.30), channel_id=1, source_target_pairs={{0,2},{6,4},{2,0},{4,6},{1,3},{7,5},{3,1},{5,7},{8,10},{14,12},{10... | collective-permute-start | bytes 1966088 | tf_op jit(solution)/shard_map/ppermute | solution.py:212
  66.1 17.5 %collective-permute-start.7 = (bf16[2,128,1280]{2,1,0:T(8,128)(2,1)S(1)}, bf16[2,128,1280]{2,1,0:T(8,128)(2,1)S(1)}, u32[]{:S(2)}, u32[]{:S(2)}) collective-permute-start(bf16[2,128,1280]{2,1,0:T(8,128)(2,1)S(1)} %fusion.1.refs_5_), channel_id=1, source_target_pairs={{2,4},{4,2},{3,5},{5,3},{10,12},{12,10},{11,13},{13,11},{18,20},{2... | collective-permute-start | bytes 1966088 | tf_op jit(solution)/shard_map/ppermute | solution.py:219
  73.5 20.9 %collective-permute-start.13 = (bf16[2,128,768]{2,1,0:T(8,128)(2,1)S(1)}, bf16[2,128,768]{2,1,0:T(8,128)(2,1)S(1)}, u32[]{:S(2)}, u32[]{:S(2)}) collective-permute-start(bf16[2,128,768]{2,1,0:T(8,128)(2,1)S(1)} %get-tuple-element.34), channel_id=1, source_target_pairs={{0,2},{6,4},{2,0},{4,6},{1,3},{7,5},{3,1},{5,7},{8,10},{14,12},{10... | collective-permute-start | bytes 1179656 | tf_op jit(solution)/shard_map/ppermute | solution.py:212
  80.0 15.1 %collective-permute-start.14 = (bf16[2,128,1280]{2,1,0:T(8,128)(2,1)S(1)}, bf16[2,128,1280]{2,1,0:T(8,128)(2,1)S(1)}, u32[]{:S(2)}, u32[]{:S(2)}) collective-permute-start(bf16[2,128,1280]{2,1,0:T(8,128)(2,1)S(1)} %fusion.3.refs_5_), channel_id=1, source_target_pairs={{2,4},{4,2},{3,5},{5,3},{10,12},{12,10},{11,13},{13,11},{18,20},{2... | collective-permute-start | bytes 1966088 | tf_op jit(solution)/shard_map/ppermute | solution.py:219
  88.2 12.6 %collective-permute-start.11 = (bf16[2,128,768]{2,1,0:T(8,128)(2,1)S(1)}, bf16[2,128,768]{2,1,0:T(8,128)(2,1)S(1)}, u32[]{:S(2)}, u32[]{:S(2)}) collective-permute-start(bf16[2,128,768]{2,1,0:T(8,128)(2,1)S(1)} %get-tuple-element.32), channel_id=1, source_target_pairs={{0,2},{6,4},{2,0},{4,6},{1,3},{7,5},{3,1},{5,7},{8,10},{14,12},{10... | collective-permute-start | bytes 1179656 | tf_op jit(solution)/shard_map/ppermute | solution.py:212
  94.4 10.1 %collective-permute-start.16 = (bf16[2,128,768]{2,1,0:T(8,128)(2,1)S(1)}, bf16[2,128,768]{2,1,0:T(8,128)(2,1)S(1)}, u32[]{:S(2)}, u32[]{:S(2)}) collective-permute-start(bf16[2,128,768]{2,1,0:T(8,128)(2,1)S(1)} %fusion.12.refs_1_), channel_id=1, source_target_pairs={{2,4},{4,2},{3,5},{5,3},{10,12},{12,10},{11,13},{13,11},{18,20},{2... | collective-permute-start | bytes 1179656 | tf_op jit(solution)/shard_map/ppermute | solution.py:219
  95.6 13.6 %collective-permute-start.19 = (bf16[128,1280]{1,0:T(8,128)(2,1)S(1)}, bf16[128,1280]{1,0:T(8,128)(2,1)S(1)}, u32[]{:S(2)}, u32[]{:S(2)}) collective-permute-start(bf16[128,1280]{1,0:T(8,128)(2,1)S(1)} %fusion.5.refs_2_.refs_1_), channel_id=1, source_target_pairs={{2,0},{4,6},{3,1},{5,7},{10,8},{12,14},{11,9},{13,15},{18,16},{20,... | collective-permute-start | bytes 983048 | tf_op jit(solution)/shard_map/ppermute | solution.py:229
  103.9 2.3 %collective-permute-start.15 = (bf16[2,128,768]{2,1,0:T(8,128)(2,1)S(1)}, bf16[2,128,768]{2,1,0:T(8,128)(2,1)S(1)}, u32[]{:S(2)}, u32[]{:S(2)}) collective-permute-start(bf16[2,128,768]{2,1,0:T(8,128)(2,1)S(1)} %fusion.13.refs_1_), channel_id=1, source_target_pairs={{2,4},{4,2},{3,5},{5,3},{10,12},{12,10},{11,13},{13,11},{18,20},{2... | collective-permute-start | bytes 1179656 | tf_op jit(solution)/shard_map/ppermute | solution.py:219
  104.8 14.6 %collective-permute-start.18 = (bf16[128,768]{1,0:T(8,128)(2,1)S(1)}, bf16[128,768]{1,0:T(8,128)(2,1)S(1)}, u32[]{:S(2)}, u32[]{:S(2)}) collective-permute-start(bf16[128,768]{1,0:T(8,128)(2,1)S(1)} %fusion.17.refs_2_.refs_1_), channel_id=1, source_target_pairs={{2,0},{4,6},{3,1},{5,7},{10,8},{12,14},{11,9},{13,15},{18,16},{20,... | collective-permute-start | bytes 589832 | tf_op jit(solution)/shard_map/ppermute | solution.py:229
  106.4 18.5 %collective-permute-start.17 = (bf16[128,768]{1,0:T(8,128)(2,1)S(1)}, bf16[128,768]{1,0:T(8,128)(2,1)S(1)}, u32[]{:S(2)}, u32[]{:S(2)}) collective-permute-start(bf16[128,768]{1,0:T(8,128)(2,1)S(1)} %fusion.15.refs_1_), channel_id=1, source_target_pairs={{2,0},{4,6},{3,1},{5,7},{10,8},{12,14},{11,9},{13,15},{18,16},{20,... | collective-permute-start | bytes 589832 | tf_op jit(solution)/shard_map/ppermute | solution.py:229
  127.1 3.7 %copy-start.1 = (s32[32,128]{1,0:T(8,128)S(1)}, s32[32,128]{1,0:T(8,128)}, u32[]{:S(2)}) copy-start(s32[32,128]{1,0:T(8,128)} %param.9) | copy-start | bytes 49156
  127.2 2.0 %collective-permute-start.20 = (f32[64,2048]{1,0:T(8,128)S(1)}, f32[64,2048]{1,0:T(8,128)S(1)}, u32[]{:S(2)}, u32[]{:S(2)}) collective-permute-start(f32[64,2048]{1,0:T(8,128)S(1)} %slice.88), channel_id=1, source_target_pairs={{0,8},{8,0},{16,24},{24,16},{1,9},{9,1},{17,25},{25,17},{2,10},{10... | collective-permute-start | bytes 1572872 | tf_op jit(solution)/shard_map/ppermute | solution.py:260
  129.3 5.6 %collective-permute-start.21 = (bf16[32,2048]{1,0:T(8,128)(2,1)S(1)}, bf16[32,2048]{1,0:T(8,128)(2,1)S(1)}, u32[]{:S(2)}, u32[]{:S(2)}) collective-permute-start(bf16[32,2048]{1,0:T(8,128)(2,1)S(1)} %slice.154), channel_id=1, source_target_pairs={{0,16},{8,24},{16,0},{24,8},{1,17},{9,25},{17,1},{25,9},{2,18},{10... | collective-permute-start | bytes 393224 | tf_op jit(solution)/shard_map/ppermute | solution.py:260
